TPU v7x, 256 devices: a whole 4x4x8 slice. The times are simulated.
256 devices in a mesh: cache: 32 (over y_lo, z, core), heads: 8 (over x, y_hi).
Axes of the slice: x: 4, y: 4 (y_hi: 2, y_lo: 2; y = y_hi * 2 + y_lo), z: 8, core: 2. Of those that a mesh axis runs over, the one named last changes fastest.
Arguments:
- queries: bfloat16 [4096, 4096], P('cache', 'heads'), may hold values from -10 to 10
- cache_keys: bfloat16 [49152, 1024], P('cache', 'heads'), may hold values from -6 to 6
- cache_values: bfloat16 [49152, 1024], P('cache', 'heads'), may hold values from -6 to 6
- suffix_keys: bfloat16 [4096, 1024], P('cache', 'heads'), may hold values from -8 to 8
- suffix_values: bfloat16 [4096, 1024], P('cache', 'heads'), may hold values from -6 to 6
- out_weight: bfloat16 [4096, 8192], P('heads'), may hold values from -0.09375 to 0.09375
- ancestor_mask: int32 [64, 384], P(None, 'cache'), may hold values from 0 to 1, as said below
- leaf_node: int32 [32], P('cache'), may hold values from 0 to 63
- suffix_len: int32 [32], P('cache'), may hold values from 2 to 128, as said below
Outputs:
- mixed: bfloat16 [4096, 8192], P('cache', 'heads')
Inputs may be any that keep to these rules, and one draw needn't show every extreme that they name: ancestor_mask[n, c] is 1 exactly when the tree node that owns cache block c is n or an ancestor of n; node 0 is the root. `suffix_len`: some block has all 128 suffix tokens live.
All inputs are finite; a program needn't handle non-finite values.
Results may differ from a plain program's by a relative error of at most 0.011.
Values may be sent and summed in bfloat16 or wider, within the bound.
No kernel may reach another device: no remote copies, remote signals or barrier semaphores. Data moves between devices by JAX's collectives and lax.ppermute only.
A program may use at most 128 MiB of HBM per device.

v0:
```python
import math

import jax
import jax.numpy as jnp
from jax import lax
from jax.sharding import PartitionSpec as P


def shifted(x, axis, by):
    count = lax.axis_size(axis)
    return lax.ppermute(x, axis, [(i, (i + by) % count) for i in range(count)])


def absorb(running, query_rows, allowed, key_rows, value_rows, score_scale):
    maxima, totals, summed = running
    scores = (
        lax.dot_general(
            query_rows, key_rows, (((1,), (1,)), ((), ())), preferred_element_type=jnp.float32
        )
        * score_scale
    )
    scores = jnp.where(allowed, scores, -jnp.inf)
    updated = jnp.maximum(maxima, jnp.max(scores, axis=1))
    steady = jnp.where(jnp.isfinite(updated), updated, 0.0)
    weights = jnp.exp(scores - steady[:, None])
    rescale = jnp.exp(maxima - steady)
    totals = totals * rescale + jnp.sum(weights, axis=1)
    summed = summed * rescale[:, None] + jnp.dot(
        weights.astype(jnp.bfloat16), value_rows, preferred_element_type=jnp.float32
    )
    return (updated, totals, summed)


def own_suffix(query_rows, key_rows, value_rows, lengths, heads_here, block_len, score_scale):
    row_count = query_rows.shape[0]
    row_tok = jnp.arange(row_count, dtype=jnp.int32) // heads_here
    col_tok = jnp.arange(key_rows.shape[0], dtype=jnp.int32)
    same_block = row_tok[:, None] // block_len == col_tok[None, :] // block_len
    causal = col_tok[None, :] % block_len <= row_tok[:, None] % block_len
    live_keys = col_tok % block_len < jnp.repeat(lengths, block_len)
    allowed = same_block & causal & live_keys[None, :]
    initial = (
        jnp.full((row_count,), -jnp.inf, jnp.float32),
        jnp.zeros((row_count,), jnp.float32),
        jnp.zeros((row_count, key_rows.shape[1]), jnp.float32),
    )
    return absorb(initial, query_rows, allowed, key_rows, value_rows, score_scale)


def cache_allowed(leaf_ids, ancestor_mask, heads_here, block_len):
    node_ids = jnp.arange(ancestor_mask.shape[0], dtype=jnp.int32)
    picked = jnp.sum(
        jnp.where(leaf_ids[:, None, None] == node_ids[None, :, None], ancestor_mask[None, :, :], 0),
        axis=1,
    )
    block_rows, block_cols = picked.shape
    expanded = jnp.broadcast_to(
        (picked > 0)[:, None, :, None], (block_rows, block_len * heads_here, block_cols, block_len)
    )
    return expanded.reshape(block_rows * block_len * heads_here, block_cols * block_len)


def shards(
    queries,
    cache_keys,
    cache_values,
    suffix_keys,
    suffix_values,
    out_weight,
    ancestor_mask,
    leaf_node,
    suffix_len,
):
    members = lax.axis_size("cache")
    position = lax.axis_index("cache")
    head_dim = cache_keys.shape[1]
    tok_here = queries.shape[0]
    heads_here = queries.shape[1] // head_dim
    blocks_here = leaf_node.shape[0]
    block_len = tok_here // blocks_here
    score_scale = 1.0 / math.sqrt(head_dim)
    all_leaves = lax.all_gather(leaf_node, "cache", axis=0, tiled=True)

    def leaves_from(anchor):
        return lax.dynamic_slice_in_dim(all_leaves, anchor * blocks_here, blocks_here)

    def visit(states, lanes, anchors, lane_heads):
        allowed = jnp.concatenate(
            [
                cache_allowed(leaves_from(anchor), ancestor_mask, lane_heads, block_len)
                for anchor in anchors
            ],
            axis=0,
        )
        joined = tuple(
            (
                jnp.concatenate([lane_state[field_number] for lane_state in states], axis=0)
                for field_number in range(3)
            )
        )
        merged = absorb(joined, lanes[0], allowed, cache_keys, cache_values, score_scale)
        return [tuple((piece_of for piece_of in merged))]

    query_rows = queries.reshape(tok_here * heads_here, head_dim)
    running = own_suffix(
        query_rows, suffix_keys, suffix_values, suffix_len, heads_here, block_len, score_scale
    )

    def advance(turn_number, carry):
        query_rows, running = carry
        running = visit([running], [query_rows], [(position - turn_number) % members], heads_here)[
            0
        ]
        query_rows = shifted(query_rows, "cache", 1)
        running = shifted(running, "cache", 1)
        return (query_rows, running)

    def double_turn(pair_number, carry):
        return advance(2 * pair_number + 1, advance(2 * pair_number, carry))

    query_rows, running = lax.fori_loop(0, members // 2, double_turn, (query_rows, running))
    maxima, totals, summed = running
    attended = (
        (summed / totals[:, None]).astype(jnp.bfloat16).reshape(tok_here, heads_here * head_dim)
    )
    projected = jnp.dot(attended, out_weight, preferred_element_type=jnp.float32)
    return lax.psum_scatter(projected, "heads", scatter_dimension=1, tiled=True).astype(
        jnp.bfloat16
    )


def solution(mesh):
    return jax.shard_map(
        shards,
        mesh=mesh,
        in_specs=(
            P("cache", "heads"),
            P("cache", "heads"),
            P("cache", "heads"),
            P("cache", "heads"),
            P("cache", "heads"),
            P("heads", None),
            P(None, "cache"),
            P("cache"),
            P("cache"),
        ),
        out_specs=P("cache", "heads"),
        check_vma=False,
    )
```

profile of v0, /device:TPU:6, one launch (start us, length us, event | category | flops | bytes accessed | tf_op | source)
XLA Modules:
  0.0 518.9 jit_solution(5660759191597480708)
XLA Ops:
  11.4 19.5 %all-reduce = s32[32]{0:T(128)S(1)} all-reduce(s32[32]{0:T(128)S(1)} %dynamic-update-slice), channel_id=1, replica_groups=mesh['cache'=32,'heads'=8] {'cache'}, use_global_device_ids=true, to_apply=%add | all-reduce | flops 32 | bytes 256
  31.8 385.8 %while.21 = (s32[]{:T(128)}, bf16[512,128]{1,0:T(8,128)(2,1)S(1)}, f32[512]{0:T(512)S(1)}, f32[512]{0:T(512)S(1)}, f32[512,128]{1,0:T(8,128)S(1)}, /*index=5*/s3...) while((s32[]{:T(128)}, bf16[512,128]{1,0:T(8,128)(2,1)S(1)}, ...), condition=%wide.region_9.10_spmd, body=%wide.region_2.9_spmd.sunk | while | flops 816587904 | bytes 28154212 | solution.py:121
  42.2 4.6 collective-permute-done.4
  47.8 9.0 %collective-permute-done.3 = f32[512]{0:T(512)S(1)} collective-permute-done((f32[512]{0:T(512)S(1)}, f32[512]{0:T(512)S(1)}, u32[]{:S(2)}, u32[]{:S(2)}) %collective-permute-start.3) | collective-permute-done | bytes 2080 | tf_op jit(solution)/shard_map/while/body/eval_jaxpr/ppermute | solution.py:11
  67.3 3.6 collective-permute-done.4
  71.9 9.0 %collective-permute-done.3 = f32[512]{0:T(512)S(1)} collective-permute-done((f32[512]{0:T(512)S(1)}, f32[512]{0:T(512)S(1)}, u32[]{:S(2)}, u32[]{:S(2)}) %collective-permute-start.3) | collective-permute-done | bytes 2080 | tf_op jit(solution)/shard_map/while/body/eval_jaxpr/ppermute | solution.py:11
  91.3 3.6 collective-permute-done.4
  95.9 9.0 %collective-permute-done.3 = f32[512]{0:T(512)S(1)} collective-permute-done((f32[512]{0:T(512)S(1)}, f32[512]{0:T(512)S(1)}, u32[]{:S(2)}, u32[]{:S(2)}) %collective-permute-start.3) | collective-permute-done | bytes 2080 | tf_op jit(solution)/shard_map/while/body/eval_jaxpr/ppermute | solution.py:11
  115.4 3.6 collective-permute-done.4
  120.0 9.0 %collective-permute-done.3 = f32[512]{0:T(512)S(1)} collective-permute-done((f32[512]{0:T(512)S(1)}, f32[512]{0:T(512)S(1)}, u32[]{:S(2)}, u32[]{:S(2)}) %collective-permute-start.3) | collective-permute-done | bytes 2080 | tf_op jit(solution)/shard_map/while/body/eval_jaxpr/ppermute | solution.py:11
  139.4 3.6 collective-permute-done.4
  144.0 9.0 %collective-permute-done.3 = f32[512]{0:T(512)S(1)} collective-permute-done((f32[512]{0:T(512)S(1)}, f32[512]{0:T(512)S(1)}, u32[]{:S(2)}, u32[]{:S(2)}) %collective-permute-start.3) | collective-permute-done | bytes 2080 | tf_op jit(solution)/shard_map/while/body/eval_jaxpr/ppermute | solution.py:11
  163.5 3.6 collective-permute-done.4
  168.1 9.0 %collective-permute-done.3 = f32[512]{0:T(512)S(1)} collective-permute-done((f32[512]{0:T(512)S(1)}, f32[512]{0:T(512)S(1)}, u32[]{:S(2)}, u32[]{:S(2)}) %collective-permute-start.3) | collective-permute-done | bytes 2080 | tf_op jit(solution)/shard_map/while/body/eval_jaxpr/ppermute | solution.py:11
  187.5 3.6 collective-permute-done.4
  192.1 9.0 %collective-permute-done.3 = f32[512]{0:T(512)S(1)} collective-permute-done((f32[512]{0:T(512)S(1)}, f32[512]{0:T(512)S(1)}, u32[]{:S(2)}, u32[]{:S(2)}) %collective-permute-start.3) | collective-permute-done | bytes 2080 | tf_op jit(solution)/shard_map/while/body/eval_jaxpr/ppermute | solution.py:11
  211.6 3.6 collective-permute-done.4
  216.2 9.0 %collective-permute-done.3 = f32[512]{0:T(512)S(1)} collective-permute-done((f32[512]{0:T(512)S(1)}, f32[512]{0:T(512)S(1)}, u32[]{:S(2)}, u32[]{:S(2)}) %collective-permute-start.3) | collective-permute-done | bytes 2080 | tf_op jit(solution)/shard_map/while/body/eval_jaxpr/ppermute | solution.py:11
  235.6 3.6 collective-permute-done.4
  240.2 9.0 %collective-permute-done.3 = f32[512]{0:T(512)S(1)} collective-permute-done((f32[512]{0:T(512)S(1)}, f32[512]{0:T(512)S(1)}, u32[]{:S(2)}, u32[]{:S(2)}) %collective-permute-start.3) | collective-permute-done | bytes 2080 | tf_op jit(solution)/shard_map/while/body/eval_jaxpr/ppermute | solution.py:11
  264.3 9.0 %collective-permute-done.3 = f32[512]{0:T(512)S(1)} collective-permute-done((f32[512]{0:T(512)S(1)}, f32[512]{0:T(512)S(1)}, u32[]{:S(2)}, u32[]{:S(2)}) %collective-permute-start.3) | collective-permute-done | bytes 2080 | tf_op jit(solution)/shard_map/while/body/eval_jaxpr/ppermute | solution.py:11
  283.7 3.6 collective-permute-done.4
  288.3 9.0 %collective-permute-done.3 = f32[512]{0:T(512)S(1)} collective-permute-done((f32[512]{0:T(512)S(1)}, f32[512]{0:T(512)S(1)}, u32[]{:S(2)}, u32[]{:S(2)}) %collective-permute-start.3) | collective-permute-done | bytes 2080 | tf_op jit(solution)/shard_map/while/body/eval_jaxpr/ppermute | solution.py:11
  312.4 9.0 %collective-permute-done.3 = f32[512]{0:T(512)S(1)} collective-permute-done((f32[512]{0:T(512)S(1)}, f32[512]{0:T(512)S(1)}, u32[]{:S(2)}, u32[]{:S(2)}) %collective-permute-start.3) | collective-permute-done | bytes 2080 | tf_op jit(solution)/shard_map/while/body/eval_jaxpr/ppermute | solution.py:11
  331.8 3.6 collective-permute-done.4
  336.4 9.0 %collective-permute-done.3 = f32[512]{0:T(512)S(1)} collective-permute-done((f32[512]{0:T(512)S(1)}, f32[512]{0:T(512)S(1)}, u32[]{:S(2)}, u32[]{:S(2)}) %collective-permute-start.3) | collective-permute-done | bytes 2080 | tf_op jit(solution)/shard_map/while/body/eval_jaxpr/ppermute | solution.py:11
  360.5 9.0 %collective-permute-done.3 = f32[512]{0:T(512)S(1)} collective-permute-done((f32[512]{0:T(512)S(1)}, f32[512]{0:T(512)S(1)}, u32[]{:S(2)}, u32[]{:S(2)}) %collective-permute-start.3) | collective-permute-done | bytes 2080 | tf_op jit(solution)/shard_map/while/body/eval_jaxpr/ppermute | solution.py:11
  379.9 3.6 collective-permute-done.4
  384.5 9.0 %collective-permute-done.3 = f32[512]{0:T(512)S(1)} collective-permute-done((f32[512]{0:T(512)S(1)}, f32[512]{0:T(512)S(1)}, u32[]{:S(2)}, u32[]{:S(2)}) %collective-permute-start.3) | collective-permute-done | bytes 2080 | tf_op jit(solution)/shard_map/while/body/eval_jaxpr/ppermute | solution.py:11
  408.5 9.0 %collective-permute-done.3 = f32[512]{0:T(512)S(1)} collective-permute-done((f32[512]{0:T(512)S(1)}, f32[512]{0:T(512)S(1)}, u32[]{:S(2)}, u32[]{:S(2)}) %collective-permute-start.3) | collective-permute-done | bytes 2080 | tf_op jit(solution)/shard_map/while/body/eval_jaxpr/ppermute | solution.py:11
  417.9 6.6 %fusion.34 = f32[128,8192]{1,0:T(8,128)} fusion(bf16[128,512]{1,0:T(8,128)(2,1)S(1)} %reshape.295, bf16[512,8192]{1,0:T(8,128)(2,1)} %param.16), kind=kOutput, calls=%fused_computation.70 | convolution fusion | flops 1073741824 | bytes 12713984 | tf_op jit(solution)/shard_map/dot_general | solution.py:126
  424.5 85.8 %reduce-scatter.2.cloned.1.call-done = f32[128,1024]{1,0:T(8,128)} async-done(((f32[128,8192]{1,0:T(8,128)}), f32[128,1024]{1,0:T(8,128)}) %reduce-scatter.2.cloned.1.call-update) | async-done | bytes 524304 | tf_op jit(solution)/shard_map/reduce_scatter | solution.py:127
  (583 shorter events, 201.0 us)
Async XLA Ops:
  6.5 503.7 %reduce-scatter.2.cloned.1.call-start = ((), (), s32[]{:S(2)}) async-start(), calls=%async_computation.1 | async-start | bytes 4718592 | tf_op jit(solution)/shard_map/reduce_scatter | solution.py:127
  47.5 9.4 %collective-permute-start.7 = (f32[512,128]{1,0:T(8,128)S(1)}, f32[512,128]{1,0:T(8,128)S(1)}, u32[]{:S(2)}, u32[]{:S(2)}) collective-permute-start(f32[512,128]{1,0:T(8,128)S(1)} %multiply_add_fusion.8), channel_id=1, source_target_pairs={{0,8},{8,16},{16,24},{24,32},{32,40},{40,48},{48,56},{56,64},{64,7... | collective-permute-start | bytes 786440 | tf_op jit(solution)/shard_map/while/body/eval_jaxpr/ppermute | solution.py:11
  47.6 9.3 %collective-permute-start.1 = (bf16[512,128]{1,0:T(8,128)(2,1)S(1)}, bf16[512,128]{1,0:T(8,128)(2,1)S(1)}, u32[]{:S(2)}, u32[]{:S(2)}) collective-permute-start(bf16[512,128]{1,0:T(8,128)(2,1)S(1)} %collective-permute-done), channel_id=1, source_target_pairs={{0,8},{8,16},{16,24},{24,32},{32,40},{40,48},{48,56},{56,64},{64,7... | collective-permute-start | bytes 393224 | tf_op jit(solution)/shard_map/while/body/eval_jaxpr/ppermute | solution.py:11
  71.5 9.4 %collective-permute-start.7 = (f32[512,128]{1,0:T(8,128)S(1)}, f32[512,128]{1,0:T(8,128)S(1)}, u32[]{:S(2)}, u32[]{:S(2)}) collective-permute-start(f32[512,128]{1,0:T(8,128)S(1)} %multiply_add_fusion.8), channel_id=1, source_target_pairs={{0,8},{8,16},{16,24},{24,32},{32,40},{40,48},{48,56},{56,64},{64,7... | collective-permute-start | bytes 786440 | tf_op jit(solution)/shard_map/while/body/eval_jaxpr/ppermute | solution.py:11
  71.6 9.3 %collective-permute-start.1 = (bf16[512,128]{1,0:T(8,128)(2,1)S(1)}, bf16[512,128]{1,0:T(8,128)(2,1)S(1)}, u32[]{:S(2)}, u32[]{:S(2)}) collective-permute-start(bf16[512,128]{1,0:T(8,128)(2,1)S(1)} %collective-permute-done), channel_id=1, source_target_pairs={{0,8},{8,16},{16,24},{24,32},{32,40},{40,48},{48,56},{56,64},{64,7... | collective-permute-start | bytes 393224 | tf_op jit(solution)/shard_map/while/body/eval_jaxpr/ppermute | solution.py:11
  95.6 9.4 %collective-permute-start.7 = (f32[512,128]{1,0:T(8,128)S(1)}, f32[512,128]{1,0:T(8,128)S(1)}, u32[]{:S(2)}, u32[]{:S(2)}) collective-permute-start(f32[512,128]{1,0:T(8,128)S(1)} %multiply_add_fusion.8), channel_id=1, source_target_pairs={{0,8},{8,16},{16,24},{24,32},{32,40},{40,48},{48,56},{56,64},{64,7... | collective-permute-start | bytes 786440 | tf_op jit(solution)/shard_map/while/body/eval_jaxpr/ppermute | solution.py:11
  95.7 9.3 %collective-permute-start.1 = (bf16[512,128]{1,0:T(8,128)(2,1)S(1)}, bf16[512,128]{1,0:T(8,128)(2,1)S(1)}, u32[]{:S(2)}, u32[]{:S(2)}) collective-permute-start(bf16[512,128]{1,0:T(8,128)(2,1)S(1)} %collective-permute-done), channel_id=1, source_target_pairs={{0,8},{8,16},{16,24},{24,32},{32,40},{40,48},{48,56},{56,64},{64,7... | collective-permute-start | bytes 393224 | tf_op jit(solution)/shard_map/while/body/eval_jaxpr/ppermute | solution.py:11
  119.6 9.4 %collective-permute-start.7 = (f32[512,128]{1,0:T(8,128)S(1)}, f32[512,128]{1,0:T(8,128)S(1)}, u32[]{:S(2)}, u32[]{:S(2)}) collective-permute-start(f32[512,128]{1,0:T(8,128)S(1)} %multiply_add_fusion.8), channel_id=1, source_target_pairs={{0,8},{8,16},{16,24},{24,32},{32,40},{40,48},{48,56},{56,64},{64,7... | collective-permute-start | bytes 786440 | tf_op jit(solution)/shard_map/while/body/eval_jaxpr/ppermute | solution.py:11
  119.7 9.3 %collective-permute-start.1 = (bf16[512,128]{1,0:T(8,128)(2,1)S(1)}, bf16[512,128]{1,0:T(8,128)(2,1)S(1)}, u32[]{:S(2)}, u32[]{:S(2)}) collective-permute-start(bf16[512,128]{1,0:T(8,128)(2,1)S(1)} %collective-permute-done), channel_id=1, source_target_pairs={{0,8},{8,16},{16,24},{24,32},{32,40},{40,48},{48,56},{56,64},{64,7... | collective-permute-start | bytes 393224 | tf_op jit(solution)/shard_map/while/body/eval_jaxpr/ppermute | solution.py:11
  143.7 9.4 %collective-permute-start.7 = (f32[512,128]{1,0:T(8,128)S(1)}, f32[512,128]{1,0:T(8,128)S(1)}, u32[]{:S(2)}, u32[]{:S(2)}) collective-permute-start(f32[512,128]{1,0:T(8,128)S(1)} %multiply_add_fusion.8), channel_id=1, source_target_pairs={{0,8},{8,16},{16,24},{24,32},{32,40},{40,48},{48,56},{56,64},{64,7... | collective-permute-start | bytes 786440 | tf_op jit(solution)/shard_map/while/body/eval_jaxpr/ppermute | solution.py:11
  143.8 9.3 %collective-permute-start.1 = (bf16[512,128]{1,0:T(8,128)(2,1)S(1)}, bf16[512,128]{1,0:T(8,128)(2,1)S(1)}, u32[]{:S(2)}, u32[]{:S(2)}) collective-permute-start(bf16[512,128]{1,0:T(8,128)(2,1)S(1)} %collective-permute-done), channel_id=1, source_target_pairs={{0,8},{8,16},{16,24},{24,32},{32,40},{40,48},{48,56},{56,64},{64,7... | collective-permute-start | bytes 393224 | tf_op jit(solution)/shard_map/while/body/eval_jaxpr/ppermute | solution.py:11
  167.7 9.4 %collective-permute-start.7 = (f32[512,128]{1,0:T(8,128)S(1)}, f32[512,128]{1,0:T(8,128)S(1)}, u32[]{:S(2)}, u32[]{:S(2)}) collective-permute-start(f32[512,128]{1,0:T(8,128)S(1)} %multiply_add_fusion.8), channel_id=1, source_target_pairs={{0,8},{8,16},{16,24},{24,32},{32,40},{40,48},{48,56},{56,64},{64,7... | collective-permute-start | bytes 786440 | tf_op jit(solution)/shard_map/while/body/eval_jaxpr/ppermute | solution.py:11
  167.8 9.3 %collective-permute-start.1 = (bf16[512,128]{1,0:T(8,128)(2,1)S(1)}, bf16[512,128]{1,0:T(8,128)(2,1)S(1)}, u32[]{:S(2)}, u32[]{:S(2)}) collective-permute-start(bf16[512,128]{1,0:T(8,128)(2,1)S(1)} %collective-permute-done), channel_id=1, source_target_pairs={{0,8},{8,16},{16,24},{24,32},{32,40},{40,48},{48,56},{56,64},{64,7... | collective-permute-start | bytes 393224 | tf_op jit(solution)/shard_map/while/body/eval_jaxpr/ppermute | solution.py:11
  191.8 9.4 %collective-permute-start.7 = (f32[512,128]{1,0:T(8,128)S(1)}, f32[512,128]{1,0:T(8,128)S(1)}, u32[]{:S(2)}, u32[]{:S(2)}) collective-permute-start(f32[512,128]{1,0:T(8,128)S(1)} %multiply_add_fusion.8), channel_id=1, source_target_pairs={{0,8},{8,16},{16,24},{24,32},{32,40},{40,48},{48,56},{56,64},{64,7... | collective-permute-start | bytes 786440 | tf_op jit(solution)/shard_map/while/body/eval_jaxpr/ppermute | solution.py:11
  191.9 9.3 %collective-permute-start.1 = (bf16[512,128]{1,0:T(8,128)(2,1)S(1)}, bf16[512,128]{1,0:T(8,128)(2,1)S(1)}, u32[]{:S(2)}, u32[]{:S(2)}) collective-permute-start(bf16[512,128]{1,0:T(8,128)(2,1)S(1)} %collective-permute-done), channel_id=1, source_target_pairs={{0,8},{8,16},{16,24},{24,32},{32,40},{40,48},{48,56},{56,64},{64,7... | collective-permute-start | bytes 393224 | tf_op jit(solution)/shard_map/while/body/eval_jaxpr/ppermute | solution.py:11
  215.8 9.4 %collective-permute-start.7 = (f32[512,128]{1,0:T(8,128)S(1)}, f32[512,128]{1,0:T(8,128)S(1)}, u32[]{:S(2)}, u32[]{:S(2)}) collective-permute-start(f32[512,128]{1,0:T(8,128)S(1)} %multiply_add_fusion.8), channel_id=1, source_target_pairs={{0,8},{8,16},{16,24},{24,32},{32,40},{40,48},{48,56},{56,64},{64,7... | collective-permute-start | bytes 786440 | tf_op jit(solution)/shard_map/while/body/eval_jaxpr/ppermute | solution.py:11
  215.9 9.3 %collective-permute-start.1 = (bf16[512,128]{1,0:T(8,128)(2,1)S(1)}, bf16[512,128]{1,0:T(8,128)(2,1)S(1)}, u32[]{:S(2)}, u32[]{:S(2)}) collective-permute-start(bf16[512,128]{1,0:T(8,128)(2,1)S(1)} %collective-permute-done), channel_id=1, source_target_pairs={{0,8},{8,16},{16,24},{24,32},{32,40},{40,48},{48,56},{56,64},{64,7... | collective-permute-start | bytes 393224 | tf_op jit(solution)/shard_map/while/body/eval_jaxpr/ppermute | solution.py:11
  239.9 9.4 %collective-permute-start.7 = (f32[512,128]{1,0:T(8,128)S(1)}, f32[512,128]{1,0:T(8,128)S(1)}, u32[]{:S(2)}, u32[]{:S(2)}) collective-permute-start(f32[512,128]{1,0:T(8,128)S(1)} %multiply_add_fusion.8), channel_id=1, source_target_pairs={{0,8},{8,16},{16,24},{24,32},{32,40},{40,48},{48,56},{56,64},{64,7... | collective-permute-start | bytes 786440 | tf_op jit(solution)/shard_map/while/body/eval_jaxpr/ppermute | solution.py:11
  239.9 9.3 %collective-permute-start.1 = (bf16[512,128]{1,0:T(8,128)(2,1)S(1)}, bf16[512,128]{1,0:T(8,128)(2,1)S(1)}, u32[]{:S(2)}, u32[]{:S(2)}) collective-permute-start(bf16[512,128]{1,0:T(8,128)(2,1)S(1)} %collective-permute-done), channel_id=1, source_target_pairs={{0,8},{8,16},{16,24},{24,32},{32,40},{40,48},{48,56},{56,64},{64,7... | collective-permute-start | bytes 393224 | tf_op jit(solution)/shard_map/while/body/eval_jaxpr/ppermute | solution.py:11
  263.9 9.4 %collective-permute-start.7 = (f32[512,128]{1,0:T(8,128)S(1)}, f32[512,128]{1,0:T(8,128)S(1)}, u32[]{:S(2)}, u32[]{:S(2)}) collective-permute-start(f32[512,128]{1,0:T(8,128)S(1)} %multiply_add_fusion.8), channel_id=1, source_target_pairs={{0,8},{8,16},{16,24},{24,32},{32,40},{40,48},{48,56},{56,64},{64,7... | collective-permute-start | bytes 786440 | tf_op jit(solution)/shard_map/while/body/eval_jaxpr/ppermute | solution.py:11
  287.9 9.4 %collective-permute-start.7 = (f32[512,128]{1,0:T(8,128)S(1)}, f32[512,128]{1,0:T(8,128)S(1)}, u32[]{:S(2)}, u32[]{:S(2)}) collective-permute-start(f32[512,128]{1,0:T(8,128)S(1)} %multiply_add_fusion.8), channel_id=1, source_target_pairs={{0,8},{8,16},{16,24},{24,32},{32,40},{40,48},{48,56},{56,64},{64,7... | collective-permute-start | bytes 786440 | tf_op jit(solution)/shard_map/while/body/eval_jaxpr/ppermute | solution.py:11
  288.0 9.3 %collective-permute-start.1 = (bf16[512,128]{1,0:T(8,128)(2,1)S(1)}, bf16[512,128]{1,0:T(8,128)(2,1)S(1)}, u32[]{:S(2)}, u32[]{:S(2)}) collective-permute-start(bf16[512,128]{1,0:T(8,128)(2,1)S(1)} %collective-permute-done), channel_id=1, source_target_pairs={{0,8},{8,16},{16,24},{24,32},{32,40},{40,48},{48,56},{56,64},{64,7... | collective-permute-start | bytes 393224 | tf_op jit(solution)/shard_map/while/body/eval_jaxpr/ppermute | solution.py:11
  312.0 9.4 %collective-permute-start.7 = (f32[512,128]{1,0:T(8,128)S(1)}, f32[512,128]{1,0:T(8,128)S(1)}, u32[]{:S(2)}, u32[]{:S(2)}) collective-permute-start(f32[512,128]{1,0:T(8,128)S(1)} %multiply_add_fusion.8), channel_id=1, source_target_pairs={{0,8},{8,16},{16,24},{24,32},{32,40},{40,48},{48,56},{56,64},{64,7... | collective-permute-start | bytes 786440 | tf_op jit(solution)/shard_map/while/body/eval_jaxpr/ppermute | solution.py:11
  312.1 9.3 %collective-permute-start.1 = (bf16[512,128]{1,0:T(8,128)(2,1)S(1)}, bf16[512,128]{1,0:T(8,128)(2,1)S(1)}, u32[]{:S(2)}, u32[]{:S(2)}) collective-permute-start(bf16[512,128]{1,0:T(8,128)(2,1)S(1)} %collective-permute-done), channel_id=1, source_target_pairs={{0,8},{8,16},{16,24},{24,32},{32,40},{40,48},{48,56},{56,64},{64,7... | collective-permute-start | bytes 393224 | tf_op jit(solution)/shard_map/while/body/eval_jaxpr/ppermute | solution.py:11
  336.0 9.4 %collective-permute-start.7 = (f32[512,128]{1,0:T(8,128)S(1)}, f32[512,128]{1,0:T(8,128)S(1)}, u32[]{:S(2)}, u32[]{:S(2)}) collective-permute-start(f32[512,128]{1,0:T(8,128)S(1)} %multiply_add_fusion.8), channel_id=1, source_target_pairs={{0,8},{8,16},{16,24},{24,32},{32,40},{40,48},{48,56},{56,64},{64,7... | collective-permute-start | bytes 786440 | tf_op jit(solution)/shard_map/while/body/eval_jaxpr/ppermute | solution.py:11
  336.1 9.3 %collective-permute-start.1 = (bf16[512,128]{1,0:T(8,128)(2,1)S(1)}, bf16[512,128]{1,0:T(8,128)(2,1)S(1)}, u32[]{:S(2)}, u32[]{:S(2)}) collective-permute-start(bf16[512,128]{1,0:T(8,128)(2,1)S(1)} %collective-permute-done), channel_id=1, source_target_pairs={{0,8},{8,16},{16,24},{24,32},{32,40},{40,48},{48,56},{56,64},{64,7... | collective-permute-start | bytes 393224 | tf_op jit(solution)/shard_map/while/body/eval_jaxpr/ppermute | solution.py:11
  360.1 9.4 %collective-permute-start.7 = (f32[512,128]{1,0:T(8,128)S(1)}, f32[512,128]{1,0:T(8,128)S(1)}, u32[]{:S(2)}, u32[]{:S(2)}) collective-permute-start(f32[512,128]{1,0:T(8,128)S(1)} %multiply_add_fusion.8), channel_id=1, source_target_pairs={{0,8},{8,16},{16,24},{24,32},{32,40},{40,48},{48,56},{56,64},{64,7... | collective-permute-start | bytes 786440 | tf_op jit(solution)/shard_map/while/body/eval_jaxpr/ppermute | solution.py:11
  360.2 9.3 %collective-permute-start.1 = (bf16[512,128]{1,0:T(8,128)(2,1)S(1)}, bf16[512,128]{1,0:T(8,128)(2,1)S(1)}, u32[]{:S(2)}, u32[]{:S(2)}) collective-permute-start(bf16[512,128]{1,0:T(8,128)(2,1)S(1)} %collective-permute-done), channel_id=1, source_target_pairs={{0,8},{8,16},{16,24},{24,32},{32,40},{40,48},{48,56},{56,64},{64,7... | collective-permute-start | bytes 393224 | tf_op jit(solution)/shard_map/while/body/eval_jaxpr/ppermute | solution.py:11
  384.1 9.4 %collective-permute-start.7 = (f32[512,128]{1,0:T(8,128)S(1)}, f32[512,128]{1,0:T(8,128)S(1)}, u32[]{:S(2)}, u32[]{:S(2)}) collective-permute-start(f32[512,128]{1,0:T(8,128)S(1)} %multiply_add_fusion.8), channel_id=1, source_target_pairs={{0,8},{8,16},{16,24},{24,32},{32,40},{40,48},{48,56},{56,64},{64,7... | collective-permute-start | bytes 786440 | tf_op jit(solution)/shard_map/while/body/eval_jaxpr/ppermute | solution.py:11
  384.2 9.3 %collective-permute-start.1 = (bf16[512,128]{1,0:T(8,128)(2,1)S(1)}, bf16[512,128]{1,0:T(8,128)(2,1)S(1)}, u32[]{:S(2)}, u32[]{:S(2)}) collective-permute-start(bf16[512,128]{1,0:T(8,128)(2,1)S(1)} %collective-permute-done), channel_id=1, source_target_pairs={{0,8},{8,16},{16,24},{24,32},{32,40},{40,48},{48,56},{56,64},{64,7... | collective-permute-start | bytes 393224 | tf_op jit(solution)/shard_map/while/body/eval_jaxpr/ppermute | solution.py:11
  408.2 9.4 %collective-permute-start.7 = (f32[512,128]{1,0:T(8,128)S(1)}, f32[512,128]{1,0:T(8,128)S(1)}, u32[]{:S(2)}, u32[]{:S(2)}) collective-permute-start(f32[512,128]{1,0:T(8,128)S(1)} %multiply_add_fusion.8), channel_id=1, source_target_pairs={{0,8},{8,16},{16,24},{24,32},{32,40},{40,48},{48,56},{56,64},{64,7... | collective-permute-start | bytes 786440 | tf_op jit(solution)/shard_map/while/body/eval_jaxpr/ppermute | solution.py:11
  408.3 9.3 %collective-permute-start.1 = (bf16[512,128]{1,0:T(8,128)(2,1)S(1)}, bf16[512,128]{1,0:T(8,128)(2,1)S(1)}, u32[]{:S(2)}, u32[]{:S(2)}) collective-permute-start(bf16[512,128]{1,0:T(8,128)(2,1)S(1)} %collective-permute-done), channel_id=1, source_target_pairs={{0,8},{8,16},{16,24},{24,32},{32,40},{40,48},{48,56},{56,64},{64,7... | collective-permute-start | bytes 393224 | tf_op jit(solution)/shard_map/while/body/eval_jaxpr/ppermute | solution.py:11
  (130 other events, 821.0 us)
Sparse Core Ops, SparseCore 0:
  424.6 85.6 reduce-scatter.1
where the time goes:
time: 521 us; the launch traced here: 519 us
  waiting for transfers between devices  334 us (64%)
  matrix products  66.9 us (13%)
  other arithmetic  53 us (10%)
  blocking collectives  19.5 us (4%)
  local copies, waits for them, and re-layouts  15.7 us (3%)
  between operations  14.8 us (3%)
  starting transfers between devices  12.7 us (2%)
    ppermute x128, waiting for transfers between devices, shifted(): return lax.ppermute(x, axis, [(i, (i + by) % count) for i in range(count)])  248 us
    reduce_scatter x1, waiting for transfers between devices, shards(): lax.psum_scatter(projected, 'heads', scatter_dimension=1, tiled=True)  85.8 us
    dot_general x33, matrix products, absorb(): lax.dot_general(query_rows, key_rows, (((1,), (1,)), ((), ())), preferred...  38.6 us
    dot_general x33, matrix products, absorb(): jnp.dot(weights.astype(jnp.bfloat16), value_rows, preferred_element_type=...  21.7 us
    unnamed x1, blocking collectives  19.5 us
    eq x16, other arithmetic, cache_allowed(): leaf_ids[:, None, None] == node_ids[None, :, None]  19.1 us
    reduce_sum x33, other arithmetic, absorb(): totals = totals * rescale + jnp.sum(weights, axis=1)  18.2 us
    reduce_sum x16, other arithmetic, cache_allowed(): jnp.sum(jnp.where(leaf_ids[:, None, None] == node_ids[None, :, None], anc...  13 us
  transfers between devices with their start and end apart: 129, of which 64 were waited for; matrix products, arithmetic and copies ran while one was open for 22% of the time, Pallas kernels for 0%

commit v1 on v0

v1 whole, which is shorter than its diff:
```python
import math

import jax
import jax.numpy as jnp
from jax import lax
from jax.experimental import pallas as pl
from jax.experimental.pallas import tpu as pltpu
from jax.sharding import PartitionSpec as P

BF16 = jnp.bfloat16
F32 = jnp.float32
NY, NZ, NC = 2, 8, 2
NX, NW = 4, 2
HD = 128
BLK = 128
QPG = 4
ROWS = QPG * BLK
EMPTY = -1e30
SCALE2 = math.log2(math.e) / math.sqrt(HD)
OFFSETS = (0, 1, -1, 2, -2, 3, -3, 4)
NEAR = 5
RELATIVE = tuple((dx, dw) for dx in (0, 2, 1, 3) for dw in (0, 1))
PAYLOAD = BLK + 16
PER_SOURCE = 12
KEYS_AT, VALUES_AT, MASK_AT = 0, PER_SOURCE * BLK, 2 * PER_SOURCE * BLK
SOURCE = MASK_AT + 16


def cache_step(x, dy, dz, dc):
    pairs = []
    for y in range(NY):
        for z in range(NZ):
            for c in range(NC):
                there = (((y + dy) % NY) * NZ + (z + dz) % NZ) * NC + (c + dc) % NC
                pairs.append(((y * NZ + z) * NC + c, there))
    return lax.ppermute(x, "cache", pairs)


def heads_step(x, dx, dw):
    pairs = []
    for a in range(NX):
        for w in range(NW):
            pairs.append((a * NW + w, ((a + dx) % NX) * NW + (w + dw) % NW))
    return lax.ppermute(x, "heads", pairs)


def z_ways(x, even, odd):
    pairs = []
    for y in range(NY):
        for z in range(NZ):
            for c in range(NC):
                there = (y * NZ + (z + (odd if z % 2 else even)) % NZ) * NC + c
                pairs.append(((y * NZ + z) * NC + c, there))
    return lax.ppermute(x, "cache", pairs)


def scores_of(keys, rows):
    return lax.dot_general(keys, rows, (((1,), (1,)), ((), ())), preferred_element_type=F32)


def weighted(values, weights):
    return lax.dot_general(
        values, weights.astype(BF16), (((0,), (0,)), ((), ())), preferred_element_type=F32
    )


def softmax_part(scores):
    peak = jnp.max(scores, axis=0, keepdims=True)
    weights = jnp.exp2((scores - peak) * SCALE2)
    return peak, jnp.sum(weights, axis=0, keepdims=True), weights


def fetch(packed, sources, qbuf, lbuf, sbuf, qsem, ssem):
    copies = []
    for b, ref in enumerate(packed):
        for h in range(QPG):
            copies.append(
                pltpu.make_async_copy(
                    ref.at[pl.ds(0, BLK), pl.ds(h * HD, HD)],
                    qbuf.at[b, pl.ds(h * BLK, BLK), :],
                    qsem.at[b * (QPG + 1) + h],
                )
            )
        copies.append(
            pltpu.make_async_copy(
                ref.at[pl.ds(BLK, 16), pl.ds(0, HD)], lbuf.at[b], qsem.at[b * (QPG + 1) + QPG]
            )
        )
    for s, ref in enumerate(sources):
        copies.append(pltpu.make_async_copy(ref, sbuf.at[s], ssem.at[s]))
    return copies


def list_items(wanted, lbuf, sbuf, vis_v, vis_s, todo, dummy, vsem):
    blocks = sorted({b for b, _ in wanted})
    leaf = jnp.concatenate([lbuf[b].astype(F32)[0:1, :] for b in blocks], axis=0)
    node_at = lax.broadcasted_iota(jnp.int32, leaf.shape, 1).astype(F32)
    chosen = jnp.where(node_at == leaf, 1.0, 0.0).astype(BF16)
    for s in sorted({s for _, s in wanted}):
        seen = scores_of(chosen, sbuf[s, MASK_AT:SOURCE, :])
        vis_v[8 * s : 8 * s + len(blocks), 0:16] = seen.astype(jnp.int32)
    copy = pltpu.make_async_copy(vis_v, vis_s, vsem)
    copy.start()
    copy.wait()
    count = jnp.int32(0)
    for b, s in wanted:
        for c in range(PER_SOURCE):
            todo[count] = b * 64 + s * 16 + c
            count = count + vis_s[8 * s + b, c]
    todo[count] = dummy * 64
    return count


def work(count, todo, nq, qbuf, sbuf, state):
    def part(item):
        b = lax.shift_right_logical(item, 6)
        s = lax.bitwise_and(lax.shift_right_logical(item, 4), 3)
        row = pl.multiple_of(lax.bitwise_and(item, 15) * BLK, BLK)
        keys = sbuf[s, pl.ds(row, BLK), :]
        values = sbuf[s, pl.ds(VALUES_AT + row, BLK), :]
        peak, total, weights = softmax_part(scores_of(keys, qbuf[jnp.minimum(b, nq - 1)]))
        return b, peak, total, weighted(values, weights)

    def pair(i, carry):
        first = part(todo[2 * i])
        second = part(todo[2 * i + 1])
        merge(state, *first)
        merge(state, *second)
        return carry

    lax.fori_loop(0, lax.shift_right_logical(count + 1, 1), pair, 0)


def merge(state, b, peak, total, summed):
    peaks, totals, sums = state
    before = peaks[b]
    after = jnp.maximum(before, peak)
    keep = jnp.exp2((before - after) * SCALE2)
    take = jnp.exp2((peak - after) * SCALE2)
    peaks[b] = after
    totals[b] = totals[b] * keep + total * take
    sums[b] = sums[b] * keep + summed * take


def first_kernel(length, *refs):
    packed, sources = refs[0:NEAR], refs[NEAR : NEAR + 2]
    suffix_k, suffix_v = refs[NEAR + 2 : NEAR + 4]
    state = refs[NEAR + 4 : NEAR + 7]
    todo, vis_s, vis_v, qbuf, lbuf, sbuf, qsem, ssem, vsem = refs[NEAR + 7 :]
    copies = fetch(packed, sources, qbuf, lbuf, sbuf, qsem, ssem)
    for copy in copies:
        copy.start()
    peaks, totals, sums = state
    peaks[...] = jnp.full(peaks.shape, EMPTY, F32)
    totals[...] = jnp.zeros(totals.shape, F32)
    sums[...] = jnp.zeros(sums.shape, F32)
    for copy in copies:
        copy.wait()
    wanted = [(b, s) for b in range(NEAR) for s in range(2)]
    count = list_items(wanted, lbuf, sbuf, vis_v, vis_s, todo, NEAR, vsem)
    work(count, todo, NEAR, qbuf, sbuf, state)
    key_at = lax.broadcasted_iota(jnp.int32, (BLK, ROWS), 0)
    row_at = lax.bitwise_and(lax.broadcasted_iota(jnp.int32, (BLK, ROWS), 1), BLK - 1)
    scores = scores_of(suffix_k[...], qbuf[0])
    scores = jnp.where((key_at <= row_at) & (key_at < length[0]), scores, EMPTY)
    peak, total, weights = softmax_part(scores)
    merge(state, 0, peak, total, weighted(suffix_v[...], weights))


def lse_rows(lse):
    high = lse.astype(BF16).astype(F32)
    middle = (lse - high).astype(BF16).astype(F32)
    low = lse - high - middle
    at = lax.broadcasted_iota(jnp.int32, (16, ROWS), 0)
    return jnp.where(at == 0, high, jnp.where(at == 1, middle, low)).astype(BF16)


def lse_of(rows):
    pieces = rows.astype(F32)
    return pieces[0:1] + pieces[1:2] + pieces[2:3]


def second_kernel(*refs):
    nq = len(OFFSETS)
    packed, sources, known = refs[0:nq], refs[nq : nq + 4], refs[nq + 4 : nq + 7]
    own_out, own_lse = refs[nq + 7 : nq + 9]
    payloads = refs[nq + 9 : 2 * nq + 8]
    todo, vis_s, vis_v, qbuf, lbuf, sbuf, peaks, totals, sums, qsem, ssem, vsem, ksem = refs[
        2 * nq + 8 :
    ]
    state = (peaks, totals, sums)
    copies = fetch(packed, sources, qbuf, lbuf, sbuf, qsem, ssem)
    for i in range(3):
        copies.append(
            pltpu.make_async_copy(
                known[i].at[pl.ds(0, NEAR)], state[i].at[pl.ds(0, NEAR)], ksem.at[i]
            )
        )
    for copy in copies:
        copy.start()
    for b in range(NEAR, nq + 1):
        peaks[b] = jnp.full((1, ROWS), EMPTY, F32)
        totals[b] = jnp.zeros((1, ROWS), F32)
        sums[b] = jnp.zeros((HD, ROWS), F32)
    for copy in copies:
        copy.wait()
    wanted = [(b, s) for b in range(NEAR, nq) for s in range(4)]
    wanted += [(b, s) for b in range(NEAR) for s in (2, 3)]
    count = list_items(wanted, lbuf, sbuf, vis_v, vis_s, todo, nq, vsem)
    work(count, todo, nq, qbuf, sbuf, state)
    for b in range(nq):
        total = totals[b]
        seen = total > 0.0
        safe = jnp.where(seen, total, 1.0)
        lse = jnp.where(seen, peaks[b] * SCALE2 + jnp.log2(safe), EMPTY)
        out = sums[b] * (1.0 / safe)
        if b == 0:
            own_out[...] = out
            own_lse[...] = jnp.broadcast_to(lse, own_lse.shape)
        else:
            payloads[b - 1][0:BLK, :] = out.astype(BF16)
            payloads[b - 1][BLK:PAYLOAD, :] = lse_rows(lse)


SMEM = pl.BlockSpec(memory_space=pltpu.SMEM)
VMEM = pl.BlockSpec(memory_space=pltpu.VMEM)
HBM = pl.BlockSpec(memory_space=pltpu.HBM)


def state_shapes(count):
    return [(count, 1, ROWS), (count, 1, ROWS), (count, HD, ROWS)]


def buffers(nq, ns):
    return [
        pltpu.SMEM((nq * 4 * PER_SOURCE + 8,), jnp.int32),
        pltpu.SMEM((32, HD), jnp.int32),
        pltpu.VMEM((32, HD), jnp.int32),
        pltpu.VMEM((nq, ROWS, HD), BF16),
        pltpu.VMEM((nq, 16, HD), BF16),
        pltpu.VMEM((ns, SOURCE, HD), BF16),
    ]


def semaphores(nq, ns):
    return [
        pltpu.SemaphoreType.DMA((nq * (QPG + 1),)),
        pltpu.SemaphoreType.DMA((ns,)),
        pltpu.SemaphoreType.DMA,
    ]


def first_part(length, packed, sources, suffix_k, suffix_v):
    return pl.pallas_call(
        first_kernel,
        out_shape=[jax.ShapeDtypeStruct(s, F32) for s in state_shapes(NEAR + 1)],
        in_specs=[SMEM] + [HBM] * (NEAR + 2) + [VMEM] * 2,
        out_specs=[VMEM] * 3,
        scratch_shapes=buffers(NEAR, 2) + semaphores(NEAR, 2),
        compiler_params=pltpu.CompilerParams(vmem_limit_bytes=24 << 20),
        cost_estimate=pl.CostEstimate(
            flops=2_000_000_000, bytes_accessed=4 << 20, transcendentals=1_000_000
        ),
        name="first_part",
    )(length, *packed, *sources, suffix_k, suffix_v)


def second_part(packed, sources, known):
    nq = len(OFFSETS)
    return pl.pallas_call(
        second_kernel,
        out_shape=[
            jax.ShapeDtypeStruct((HD, ROWS), F32),
            jax.ShapeDtypeStruct((8, ROWS), F32),
        ]
        + [jax.ShapeDtypeStruct((PAYLOAD, ROWS), BF16)] * (nq - 1),
        in_specs=[HBM] * (nq + 7),
        out_specs=[VMEM] * (nq + 1),
        scratch_shapes=buffers(nq, 4)
        + [pltpu.VMEM(s, F32) for s in state_shapes(nq + 1)]
        + semaphores(nq, 4)
        + [pltpu.SemaphoreType.DMA((3,))],
        compiler_params=pltpu.CompilerParams(vmem_limit_bytes=24 << 20),
        cost_estimate=pl.CostEstimate(
            flops=4_000_000_000, bytes_accessed=6 << 20, transcendentals=3_000_000
        ),
        name="second_part",
    )(*packed, *sources, *known)


def join_kernel(place, ahead, back, from_ahead, from_back, from_far, ahead_out, back_out):
    odd = lax.bitwise_and(place[0], 1)
    for own, other, out, far_here in (
        (ahead, from_back, ahead_out, odd == 0),
        (back, from_ahead, back_out, odd == 1),
    ):
        parts = (own, other, from_far)
        lses = [lse_of(part[BLK:PAYLOAD, :]) for part in parts]
        lses[2] = jnp.where(far_here, lses[2], EMPTY)
        top = jnp.maximum(jnp.maximum(lses[0], lses[1]), lses[2])
        shares = [jnp.exp2(lse - top) for lse in lses]
        total = shares[0] + shares[1] + shares[2]
        inverse = 1.0 / total
        summed = parts[0][0:BLK, :].astype(F32) * (shares[0] * inverse)
        for part, share in zip(parts[1:], shares[1:]):
            summed = summed + part[0:BLK, :].astype(F32) * (share * inverse)
        out[0:BLK, :] = summed.astype(BF16)
        out[BLK:PAYLOAD, :] = lse_rows(jnp.maximum(top + jnp.log2(total), EMPTY))


def join(place, *parts):
    return pl.pallas_call(
        join_kernel,
        out_shape=[jax.ShapeDtypeStruct((PAYLOAD, ROWS), BF16)] * 2,
        in_specs=[SMEM] + [VMEM] * 5,
        out_specs=[VMEM] * 2,
        compiler_params=pltpu.CompilerParams(vmem_limit_bytes=16 << 20),
        cost_estimate=pl.CostEstimate(
            flops=2_000_000, bytes_accessed=1 << 20, transcendentals=4096
        ),
        name="join",
    )(place, *parts)


def projection_kernel(*refs):
    place, own_out, own_lse = refs[0:3]
    payloads = refs[3:7]
    weight = refs[7]
    shares = refs[8 : 8 + NX * NW]
    wbuf, sem = refs[8 + NX * NW :]
    width = wbuf.shape[2]
    here = place[0]
    x, w = lax.shift_right_logical(here, 1), lax.bitwise_and(here, 1)
    copies = []
    order = list(range(1, NX * NW)) + [0]
    for j, (dx, dw) in enumerate(RELATIVE):
        column = lax.bitwise_and(x + dx, NX - 1) * NW + lax.bitwise_and(w + dw, NW - 1)
        columns = pl.ds(pl.multiple_of(column * width, width), width)
        copies.append(pltpu.make_async_copy(weight.at[:, columns], wbuf.at[j], sem.at[j]))
    for j in order:
        copies[j].start()
    lses = [own_lse[0:1, :]] + [lse_of(payload[BLK:PAYLOAD, :]) for payload in payloads]
    top = lses[0]
    for lse in lses[1:]:
        top = jnp.maximum(top, lse)
    parts_of = [jnp.exp2(lse - top) for lse in lses]
    total = parts_of[0]
    for part in parts_of[1:]:
        total = total + part
    inverse = 1.0 / total
    mixed = own_out[...] * (parts_of[0] * inverse)
    for payload, part in zip(payloads, parts_of[1:]):
        mixed = mixed + payload[0:BLK, :].astype(F32) * (part * inverse)
    attended = jnp.concatenate(
        [mixed[:, h * BLK : (h + 1) * BLK].T for h in range(QPG)], axis=1
    ).astype(BF16)
    for j in order:
        copies[j].wait()
        shares[j][...] = jnp.dot(attended, wbuf[j], preferred_element_type=F32).astype(
            shares[j].dtype
        )


def projection(place, own_out, own_lse, payloads, weight):
    groups = NX * NW
    width = weight.shape[1] // groups
    return pl.pallas_call(
        projection_kernel,
        out_shape=[
            jax.ShapeDtypeStruct((BLK, width), F32 if j == 0 else BF16) for j in range(groups)
        ],
        in_specs=[SMEM] + [VMEM] * (2 + len(payloads)) + [HBM],
        out_specs=[VMEM] * groups,
        scratch_shapes=[
            pltpu.VMEM((groups, weight.shape[0], width), BF16),
            pltpu.SemaphoreType.DMA((groups,)),
        ],
        compiler_params=pltpu.CompilerParams(vmem_limit_bytes=54 << 20),
        cost_estimate=pl.CostEstimate(
            flops=1_100_000_000, bytes_accessed=10 << 20, transcendentals=4096
        ),
        name="projection",
    )(place, own_out, own_lse, *payloads, weight)


def shards(
    queries,
    cache_keys,
    cache_values,
    suffix_keys,
    suffix_values,
    out_weight,
    ancestor_mask,
    leaf_node,
    suffix_len,
):
    z = lax.bitwise_and(lax.shift_right_logical(lax.axis_index("cache"), 1), NZ - 1)
    z_place = z.astype(jnp.int32).reshape(1)
    head_place = lax.axis_index("heads").astype(jnp.int32).reshape(1)
    leaf_rows = jnp.broadcast_to(leaf_node.astype(BF16)[:, None], (16, ROWS))
    own = jnp.concatenate([queries, leaf_rows], axis=0)
    mask = jnp.pad(ancestor_mask.T.astype(BF16), ((0, 16 - PER_SOURCE), (0, HD - ancestor_mask.shape[0])))
    source = jnp.concatenate([cache_keys, cache_values, mask], axis=0)
    across = cache_step(source, 1, 0, 0)
    p1, m1 = cache_step(own, 0, -1, 0), cache_step(own, 0, 1, 0)
    p2, m2 = cache_step(own, 0, -2, 0), cache_step(own, 0, 2, 0)
    near = cache_step(source, 0, 0, 1)
    p3, m3 = cache_step(p2, 0, -1, 0), cache_step(m2, 0, 1, 0)
    p4 = z_ways(jnp.where(lax.bitwise_and(z, 1) == 0, m2, p2), 2, -2)
    known = first_part(
        suffix_len, [own, p1, m1, p2, m2], [source, near], suffix_keys, suffix_values
    )
    across, p3, m3, p4, *known = lax.optimization_barrier((across, p3, m3, p4, *known))
    far = cache_step(across, 0, 0, 1)
    own_out, own_lse, o_p1, o_m1, o_p2, o_m2, o_p3, o_m3, o_p4 = second_part(
        [own, p1, m1, p2, m2, p3, m3, p4], [source, near, across, far], known
    )
    from_far = z_ways(o_p4, 2, -2)
    from_back = cache_step(o_p3, 0, 1, 0)
    from_ahead = cache_step(o_m3, 0, -1, 0)
    r_p1, r_m1 = cache_step(o_p1, 0, 1, 0), cache_step(o_m1, 0, -1, 0)
    ahead, back = join(z_place, o_p2, o_m2, from_ahead, from_back, from_far)
    r_p2, r_m2 = cache_step(ahead, 0, 2, 0), cache_step(back, 0, -2, 0)
    shares = projection(head_place, own_out, own_lse, [r_p1, r_m1, r_p2, r_m2], out_weight)
    mixed = shares[0]
    for share, (dx, dw) in zip(shares[1:], RELATIVE[1:]):
        mixed = mixed + heads_step(share, dx, dw).astype(F32)
    return mixed.astype(BF16)


def solution(mesh):
    return jax.shard_map(
        shards,
        mesh=mesh,
        in_specs=(
            P("cache", "heads"),
            P("cache", "heads"),
            P("cache", "heads"),
            P("cache", "heads"),
            P("cache", "heads"),
            P("heads", None),
            P(None, "cache"),
            P("cache"),
            P("cache"),
        ),
        out_specs=P("cache", "heads"),
        check_vma=False,
    )
```

time: 521 us -> 113 us (0.22)
  waiting for transfers between devices: 334 us -> 39 us
  matrix products: 66.9 us -> 0 us
  other arithmetic: 53 us -> 3.99 us
  starting transfers between devices: 12.7 us -> 44.2 us
  Pallas kernels: 0 us -> 22.7 us
  blocking collectives: 19.5 us -> 0 us
  local copies, waits for them, and re-layouts: 15.7 us -> 1.4 us
  between operations: 14.8 us -> 1.47 us
    ppermute x128 -> x24, waiting for transfers between devices: 248 us -> 39 us  [the longest x7 20.7 us: heads_step(): return lax.ppermute(x, 'heads', pairs)]
    reduce_scatter x1 -> x0, waiting for transfers between devices: 85.8 us -> none  [shards(): lax.psum_scatter(projected, 'heads', scatter_dimension=1, tiled=True)]
    dot_general x67 -> x0, matrix products: 66.9 us -> none  [the longest x33 38.6 us: absorb(): lax.dot_general(query_rows, key_rows, (((1,), (1,)), ((), ())), preferred...]
    ppermute x128 -> x24, starting transfers between devices: 12.7 us -> 44.2 us  [the longest x15 27.5 us: cache_step(): return lax.ppermute(x, 'cache', pairs)]
    reduce_sum x49 -> x0, other arithmetic: 31.2 us -> none  [the longest x33 18.2 us: absorb(): totals = totals * rescale + jnp.sum(weights, axis=1)]
    pallas_call x0 -> x4, Pallas kernels: none -> 22.7 us  [the longest x1 9.41 us: second_part(): pl.pallas_call(second_kernel, out_shape=[jax.ShapeDtypeStruct((HD, ROWS),...]
    unnamed x1 -> x0, blocking collectives: 19.5 us -> none
    eq x16 -> x0, other arithmetic: 19.1 us -> none  [cache_allowed(): leaf_ids[:, None, None] == node_ids[None, :, None]]
  transfers between devices with their start and end apart: 129 -> 24, of which waited for: 64 -> 11; matrix products, arithmetic and copies ran while one was open for 22% -> 0% of each run, Pallas kernels for 0% -> 6%
where the time goes in v1:
time: 113 us
  starting transfers between devices  44.2 us (39%)
  waiting for transfers between devices  39 us (35%)
  Pallas kernels  22.7 us (20%)
  other arithmetic  3.99 us (4%)
  between operations  1.47 us (1%)
  local copies, waits for them, and re-layouts  1.4 us (1%)
    ppermute x15, starting transfers between devices, cache_step(): return lax.ppermute(x, 'cache', pairs)  27.5 us
    ppermute x7, waiting for transfers between devices, heads_step(): return lax.ppermute(x, 'heads', pairs)  20.7 us
    ppermute x15, waiting for transfers between devices, cache_step(): return lax.ppermute(x, 'cache', pairs)  15.3 us
    ppermute x7, starting transfers between devices, heads_step(): return lax.ppermute(x, 'heads', pairs)  12.4 us
    pallas_call x1, Pallas kernels, second_part(): pl.pallas_call(second_kernel, out_shape=[jax.ShapeDtypeStruct((HD, ROWS),...  9.41 us
    pallas_call x1, Pallas kernels, first_part(): pl.pallas_call(first_kernel, out_shape=[jax.ShapeDtypeStruct(s, F32) for...  6.92 us
    pallas_call x1, Pallas kernels, projection(): pl.pallas_call(projection_kernel, out_shape=[jax.ShapeDtypeStruct((BLK, w...  6.12 us
    ppermute x2, starting transfers between devices, z_ways(): return lax.ppermute(x, 'cache', pairs)  4.27 us
  transfers between devices with their start and end apart: 24, of which 11 were waited for; matrix products, arithmetic and copies ran while one was open for 0% of the time, Pallas kernels for 6%

profile of v1, /device:TPU:6, one launch (start us, length us, event | category | flops | bytes accessed | tf_op | source)
XLA Modules:
  0.0 112.7 jit_solution(7330768667653658015)
XLA Ops:
  0.7 1.2 %fusion.1.refs_5_.refs_8_ = bf16[3088,128]{1,0:T(8,128)(2,1)S(1)} fusion(bf16[12,64]{1,0:T(8,128)(2,1)S(1)} %convert_bitcast_fusion, bf16[1536,128]{1,0:T(8,128)(2,1)} %param.11, bf16[1536,128]{1,0:T(8,128)(2,1)} %param.10), kind=kLoop, calls=%fused_computation.2 | loop fusion | flops 3162112 | bytes 1578496 | tf_op jit(solution)/shard_map/concatenate | solution.py:403
  2.0 1.7 %collective-permute-start.4 = (bf16[3088,128]{1,0:T(8,128)(2,1)S(1)}, bf16[3088,128]{1,0:T(8,128)(2,1)S(1)}, u32[]{:S(2)}, u32[]{:S(2)}) collective-permute-start(bf16[3088,128]{1,0:T(8,128)(2,1)S(1)} %fusion.1.refs_5_.refs_8_), channel_id=1, source_target_pairs={{0,128},{8,136},{16,144},{24,152},{32,160},{40,168},{48,176},{56,1... | collective-permute-start | bytes 2371592 | tf_op jit(solution)/shard_map/ppermute | solution.py:36
  4.4 3.3 %collective-permute-start.3 = (bf16[144,512]{1,0:T(8,128)(2,1)S(1)}, bf16[144,512]{1,0:T(8,128)(2,1)S(1)}, u32[]{:S(2)}, u32[]{:S(2)}) collective-permute-start(bf16[144,512]{1,0:T(8,128)(2,1)S(1)} %concatenate.6.refs_0_), channel_id=1, source_target_pairs={{0,32},{8,40},{16,48},{24,56},{32,64},{40,72},{48,80},{56,88},{64,... | collective-permute-start | bytes 442376 | tf_op jit(solution)/shard_map/ppermute | solution.py:36
  7.7 3.1 %collective-permute-start.2 = (bf16[144,512]{1,0:T(8,128)(2,1)S(1)}, bf16[144,512]{1,0:T(8,128)(2,1)S(1)}, u32[]{:S(2)}, u32[]{:S(2)}) collective-permute-start(bf16[144,512]{1,0:T(8,128)(2,1)S(1)} %concatenate.6.refs_0_), channel_id=1, source_target_pairs={{0,96},{8,104},{16,112},{24,120},{32,0},{40,8},{48,16},{56,24},{64... | collective-permute-start | bytes 442376 | tf_op jit(solution)/shard_map/ppermute | solution.py:36
  10.8 1.0 collective-permute-start.1
  12.5 4.1 %collective-permute-done.3.refs_4_ = bf16[144,512]{1,0:T(8,128)(2,1)S(1)} collective-permute-done((bf16[144,512]{1,0:T(8,128)(2,1)S(1)}, bf16[144,512]{1,0:T(8,128)(2,1)S(1)}, u32[]{:S(2)}, u32[]{:S(2)}) %collective-permute-start.3) | collective-permute-done | bytes 147488 | tf_op jit(solution)/shard_map/ppermute | solution.py:36
  16.6 3.8 %collective-permute-start = (bf16[144,512]{1,0:T(8,128)(2,1)S(1)}, bf16[144,512]{1,0:T(8,128)(2,1)S(1)}, u32[]{:S(2)}, u32[]{:S(2)}) collective-permute-start(bf16[144,512]{1,0:T(8,128)(2,1)S(1)} %concatenate.6.refs_0_), channel_id=1, source_target_pairs={{0,112},{8,120},{16,0},{24,8},{32,16},{40,24},{48,32},{56,40},{64,... | collective-permute-start | bytes 442376 | tf_op jit(solution)/shard_map/ppermute | solution.py:36
  20.4 2.8 %collective-permute-start.7 = (bf16[144,512]{1,0:T(8,128)(2,1)S(1)}, bf16[144,512]{1,0:T(8,128)(2,1)S(1)}, u32[]{:S(2)}, u32[]{:S(2)}) collective-permute-start(bf16[144,512]{1,0:T(8,128)(2,1)S(1)} %broadcast_select_fusion), channel_id=1, source_target_pairs={{0,32},{8,40},{16,112},{24,120},{32,64},{40,72},{48,16},{56,24},{6... | collective-permute-start | bytes 442376 | tf_op jit(solution)/shard_map/ppermute | solution.py:54
  24.2 3.7 %collective-permute-start.5 = (bf16[144,512]{1,0:T(8,128)(2,1)S(1)}, bf16[144,512]{1,0:T(8,128)(2,1)S(1)}, u32[]{:S(2)}, u32[]{:S(2)}) collective-permute-start(bf16[144,512]{1,0:T(8,128)(2,1)S(1)} %collective-permute-done.2.refs_3_), channel_id=1, source_target_pairs={{0,112},{8,120},{16,0},{24,8},{32,16},{40,24},{48,32},{56,40},{64,... | collective-permute-start | bytes 442376 | tf_op jit(solution)/shard_map/ppermute | solution.py:36
  27.9 6.9 %first_part.1 = (f32[6,1,512]{2,1,0:T(1,128)S(1)}, f32[6,1,512]{2,1,0:T(1,128)S(1)}, f32[6,128,512]{2,1,0:T(8,128)S(1)}) custom-call(s32[1]{0:T(128)S(6)} %copy.11.length, bf16[144,512]{1,0:T(8,128)(2,1)S(1)} %concatenate.6.refs_0_, bf16[144,512]{1,0:T(8,128)(2,1)S(1)} %collective-permute-done.refs_1_, bf16[144,512]{1,0:T(8,128)(2,1)S(1)} %collective-permute-done.1.refs_2_, ...), custom_call_target="tpu_custom_call" | custom-call | flops 2000000000 | bytes 4194304 | tf_op jit(solution)/shard_map/first_part/pallas_call | solution.py:254
  34.9 2.3 %collective-permute-done.9.refs_11_ = bf16[3088,128]{1,0:T(8,128)(2,1)S(1)} collective-permute-done((bf16[3088,128]{1,0:T(8,128)(2,1)S(1)}, bf16[3088,128]{1,0:T(8,128)(2,1)S(1)}, u32[]{:S(2)}, u32[]{:S(2)}) %collective-permute-start.9) | collective-permute-done | bytes 790560 | tf_op jit(solution)/shard_map/ppermute | solution.py:36
  37.2 9.4 %second_part.1 = (f32[128,512]{1,0:T(8,128)S(1)}, f32[8,512]{1,0:T(8,128)S(1)}, bf16[144,512]{1,0:T(8,128)(2,1)S(1)}, bf16[144,512]{1,0:T(8,128)(2,1)S(1)}, bf16...) custom-call(bf16[144,512]{1,0:T(8,128)(2,1)S(1)} %concatenate.6.refs, ...), custom_call_target="tpu_custom_call" | custom-call | flops 4000000000 | bytes 6291456 | tf_op jit(solution)/shard_map/second_part/pallas_call | solution.py:270
  47.3 2.8 %collective-permute-start.13 = (bf16[144,512]{1,0:T(8,128)(2,1)S(1)}, bf16[144,512]{1,0:T(8,128)(2,1)S(1)}, u32[]{:S(2)}, u32[]{:S(2)}) collective-permute-start(bf16[144,512]{1,0:T(8,128)(2,1)S(1)} %get-tuple-element.51), channel_id=1, source_target_pairs={{0,16},{8,24},{16,32},{24,40},{32,48},{40,56},{48,64},{56,72},{64,... | collective-permute-start | bytes 442376 | tf_op jit(solution)/shard_map/ppermute | solution.py:36
  50.2 1.5 %collective-permute-start.14 = (bf16[144,512]{1,0:T(8,128)(2,1)S(1)}, bf16[144,512]{1,0:T(8,128)(2,1)S(1)}, u32[]{:S(2)}, u32[]{:S(2)}) collective-permute-start(bf16[144,512]{1,0:T(8,128)(2,1)S(1)} %get-tuple-element.52), channel_id=1, source_target_pairs={{0,32},{8,40},{16,112},{24,120},{32,64},{40,72},{48,16},{56,24},{6... | collective-permute-start | bytes 442376 | tf_op jit(solution)/shard_map/ppermute | solution.py:54
  52.2 2.7 %collective-permute-start.11 = (bf16[144,512]{1,0:T(8,128)(2,1)S(1)}, bf16[144,512]{1,0:T(8,128)(2,1)S(1)}, u32[]{:S(2)}, u32[]{:S(2)}) collective-permute-start(bf16[144,512]{1,0:T(8,128)(2,1)S(1)} %get-tuple-element.47), channel_id=1, source_target_pairs={{0,112},{8,120},{16,0},{24,8},{32,16},{40,24},{48,32},{56,40},{64,... | collective-permute-start | bytes 442376 | tf_op jit(solution)/shard_map/ppermute | solution.py:36
  54.9 3.0 %collective-permute-done.14.from_far = bf16[144,512]{1,0:T(8,128)(2,1)S(1)} collective-permute-done((bf16[144,512]{1,0:T(8,128)(2,1)S(1)}, bf16[144,512]{1,0:T(8,128)(2,1)S(1)}, u32[]{:S(2)}, u32[]{:S(2)}) %collective-permute-start.14) | collective-permute-done | bytes 147488 | tf_op jit(solution)/shard_map/ppermute | solution.py:54
  58.1 2.7 %collective-permute-start.15 = (bf16[144,512]{1,0:T(8,128)(2,1)S(1)}, bf16[144,512]{1,0:T(8,128)(2,1)S(1)}, u32[]{:S(2)}, u32[]{:S(2)}) collective-permute-start(bf16[144,512]{1,0:T(8,128)(2,1)S(1)} %get-tuple-element.53), channel_id=1, source_target_pairs={{0,32},{8,40},{16,48},{24,56},{32,64},{40,72},{48,80},{56,88},{64,... | collective-permute-start | bytes 442376 | tf_op jit(solution)/shard_map/ppermute | solution.py:36
  60.8 1.5 %collective-permute-start.16 = (bf16[144,512]{1,0:T(8,128)(2,1)S(1)}, bf16[144,512]{1,0:T(8,128)(2,1)S(1)}, u32[]{:S(2)}, u32[]{:S(2)}) collective-permute-start(bf16[144,512]{1,0:T(8,128)(2,1)S(1)} %get-tuple-element.54), channel_id=1, source_target_pairs={{0,96},{8,104},{16,112},{24,120},{32,0},{40,8},{48,16},{56,24},{64... | collective-permute-start | bytes 442376 | tf_op jit(solution)/shard_map/ppermute | solution.py:36
  62.4 6.8 %collective-permute-done.15.refs_5_ = bf16[144,512]{1,0:T(8,128)(2,1)S(1)} collective-permute-done((bf16[144,512]{1,0:T(8,128)(2,1)S(1)}, bf16[144,512]{1,0:T(8,128)(2,1)S(1)}, u32[]{:S(2)}, u32[]{:S(2)}) %collective-permute-start.15) | collective-permute-done | bytes 147488 | tf_op jit(solution)/shard_map/ppermute | solution.py:36
  69.2 1.5 %collective-permute-done.16.refs_6_ = bf16[144,512]{1,0:T(8,128)(2,1)S(1)} collective-permute-done((bf16[144,512]{1,0:T(8,128)(2,1)S(1)}, bf16[144,512]{1,0:T(8,128)(2,1)S(1)}, u32[]{:S(2)}, u32[]{:S(2)}) %collective-permute-start.16) | collective-permute-done | bytes 147488 | tf_op jit(solution)/shard_map/ppermute | solution.py:36
  71.4 6.1 %projection.1 = (f32[128,1024]{1,0:T(8,128)}, bf16[128,1024]{1,0:T(8,128)(2,1)}, bf16[128,1024]{1,0:T(8,128)(2,1)}, bf16[128,1024]{1,0:T(8,128)(2,1)}, bf16[128,...) custom-call(s32[1]{0:T(128)} %bitcast.refs_0_, ...), custom_call_target="tpu_custom_call" | custom-call | flops 1100000000 | bytes 10485760 | tf_op jit(solution)/shard_map/projection/pallas_call | solution.py:367
  77.5 3.0 %collective-permute-start.17 = (bf16[128,1024]{1,0:T(8,128)(2,1)}, bf16[128,1024]{1,0:T(8,128)(2,1)S(1)}, u32[]{:S(2)}, u32[]{:S(2)}) collective-permute-start(bf16[128,1024]{1,0:T(8,128)(2,1)} %get-tuple-element.56), channel_id=1, source_target_pairs={{0,1},{1,0},{2,3},{3,2},{4,5},{5,4},{6,7},{7,6},{8,9},{9,8},{10,11... | collective-permute-start | bytes 786440 | tf_op jit(solution)/shard_map/ppermute | solution.py:44
  80.5 1.4 %collective-permute-start.18 = (bf16[128,1024]{1,0:T(8,128)(2,1)}, bf16[128,1024]{1,0:T(8,128)(2,1)S(1)}, u32[]{:S(2)}, u32[]{:S(2)}) collective-permute-start(bf16[128,1024]{1,0:T(8,128)(2,1)} %get-tuple-element.57), channel_id=1, source_target_pairs={{0,4},{1,5},{2,6},{3,7},{4,0},{5,1},{6,2},{7,3},{8,12},{9,13},{10,... | collective-permute-start | bytes 786440 | tf_op jit(solution)/shard_map/ppermute | solution.py:44
  81.9 2.2 %collective-permute-start.19 = (bf16[128,1024]{1,0:T(8,128)(2,1)}, bf16[128,1024]{1,0:T(8,128)(2,1)S(1)}, u32[]{:S(2)}, u32[]{:S(2)}) collective-permute-start(bf16[128,1024]{1,0:T(8,128)(2,1)} %get-tuple-element.58), channel_id=1, source_target_pairs={{0,5},{1,4},{2,7},{3,6},{4,1},{5,0},{6,3},{7,2},{8,13},{9,12},{10,... | collective-permute-start | bytes 786440 | tf_op jit(solution)/shard_map/ppermute | solution.py:44
  84.6 3.8 %collective-permute-start.21 = (bf16[128,1024]{1,0:T(8,128)(2,1)}, bf16[128,1024]{1,0:T(8,128)(2,1)S(1)}, u32[]{:S(2)}, u32[]{:S(2)}) collective-permute-start(bf16[128,1024]{1,0:T(8,128)(2,1)} %get-tuple-element.60), channel_id=1, source_target_pairs={{0,3},{1,2},{2,5},{3,4},{4,7},{5,6},{6,1},{7,0},{8,11},{9,10},{10,... | collective-permute-start | bytes 786440 | tf_op jit(solution)/shard_map/ppermute | solution.py:44
  89.0 2.5 %collective-permute-done.18 = bf16[128,1024]{1,0:T(8,128)(2,1)S(1)} collective-permute-done((bf16[128,1024]{1,0:T(8,128)(2,1)}, bf16[128,1024]{1,0:T(8,128)(2,1)S(1)}, u32[]{:S(2)}, u32[]{:S(2)}) %collective-permute-start.18) | collective-permute-done | bytes 262176 | tf_op jit(solution)/shard_map/ppermute | solution.py:44
  91.5 1.0 collective-permute-start.23
  92.4 4.7 %collective-permute-done.19 = bf16[128,1024]{1,0:T(8,128)(2,1)S(1)} collective-permute-done((bf16[128,1024]{1,0:T(8,128)(2,1)}, bf16[128,1024]{1,0:T(8,128)(2,1)S(1)}, u32[]{:S(2)}, u32[]{:S(2)}) %collective-permute-start.19) | collective-permute-done | bytes 262176 | tf_op jit(solution)/shard_map/ppermute | solution.py:44
  97.1 3.4 %collective-permute-done.20 = bf16[128,1024]{1,0:T(8,128)(2,1)S(1)} collective-permute-done((bf16[128,1024]{1,0:T(8,128)(2,1)}, bf16[128,1024]{1,0:T(8,128)(2,1)S(1)}, u32[]{:S(2)}, u32[]{:S(2)}) %collective-permute-start.20) | collective-permute-done | bytes 262176 | tf_op jit(solution)/shard_map/ppermute | solution.py:44
  100.5 9.4 %collective-permute-done.21 = bf16[128,1024]{1,0:T(8,128)(2,1)S(1)} collective-permute-done((bf16[128,1024]{1,0:T(8,128)(2,1)}, bf16[128,1024]{1,0:T(8,128)(2,1)S(1)}, u32[]{:S(2)}, u32[]{:S(2)}) %collective-permute-start.21) | collective-permute-done | bytes 262176 | tf_op jit(solution)/shard_map/ppermute | solution.py:44
  109.9 0.7 collective-permute-done.23
  110.7 2.1 %add_convert_fusion = bf16[128,1024]{1,0:T(8,128)(2,1)} fusion(bf16[128,1024]{1,0:T(8,128)(2,1)S(1)} %collective-permute-done.23, bf16[128,1024]{1,0:T(8,128)(2,1)S(1)} %collective-permute-done.22, bf16[128,1024]{1,0:T(8,128)(2,1)S(1)} %collective-permute-done.21, bf16[128,1024]{1,0:T(8,128)(2,1)S(1)} %collective-permute-done.20, ...), kind=kLoop, calls=%fused_computation.3 | loop fusion | flops 1966080 | bytes 2621440 | tf_op jit(solution)/shard_map/convert_element_type | solution.py:428
  (43 shorter events, 5.2 us)
Async XLA Ops:
  0.0 4.3 %copy-start.8 = (bf16[128,512]{1,0:T(8,128)(2,1)S(1)}, bf16[128,512]{1,0:T(8,128)(2,1)}, u32[]{:S(2)}) copy-start(bf16[128,512]{1,0:T(8,128)(2,1)} %param.9) | copy-start | bytes 393220
  0.0 27.9 %copy-start.3 = (bf16[128,128]{1,0:T(8,128)(2,1)S(1)}, bf16[128,128]{1,0:T(8,128)(2,1)}, u32[]{:S(2)}) copy-start(bf16[128,128]{1,0:T(8,128)(2,1)} %refs_8_.1) | copy-start | bytes 98308
  0.0 27.9 %copy-start.2 = (bf16[128,128]{1,0:T(8,128)(2,1)S(1)}, bf16[128,128]{1,0:T(8,128)(2,1)}, u32[]{:S(2)}) copy-start(bf16[128,128]{1,0:T(8,128)(2,1)} %refs_7_.2) | copy-start | bytes 98308
  1.9 25.9 %collective-permute-start.8 = (bf16[3088,128]{1,0:T(8,128)(2,1)S(1)}, bf16[3088,128]{1,0:T(8,128)(2,1)S(1)}, u32[]{:S(2)}, u32[]{:S(2)}) collective-permute-start(bf16[3088,128]{1,0:T(8,128)(2,1)S(1)} %fusion.1.refs_5_.refs_8_), channel_id=1, source_target_pairs={{0,8},{8,0},{16,24},{24,16},{32,40},{40,32},{48,56},{56,48},{64,72... | collective-permute-start | bytes 2371592 | tf_op jit(solution)/shard_map/ppermute | solution.py:36
  2.0 32.8 %collective-permute-start.4 = (bf16[3088,128]{1,0:T(8,128)(2,1)S(1)}, bf16[3088,128]{1,0:T(8,128)(2,1)S(1)}, u32[]{:S(2)}, u32[]{:S(2)}) collective-permute-start(bf16[3088,128]{1,0:T(8,128)(2,1)S(1)} %fusion.1.refs_5_.refs_8_), channel_id=1, source_target_pairs={{0,128},{8,136},{16,144},{24,152},{32,160},{40,168},{48,176},{56,1... | collective-permute-start | bytes 2371592 | tf_op jit(solution)/shard_map/ppermute | solution.py:36
  4.4 12.2 %collective-permute-start.3 = (bf16[144,512]{1,0:T(8,128)(2,1)S(1)}, bf16[144,512]{1,0:T(8,128)(2,1)S(1)}, u32[]{:S(2)}, u32[]{:S(2)}) collective-permute-start(bf16[144,512]{1,0:T(8,128)(2,1)S(1)} %concatenate.6.refs_0_), channel_id=1, source_target_pairs={{0,32},{8,40},{16,48},{24,56},{32,64},{40,72},{48,80},{56,88},{64,... | collective-permute-start | bytes 442376 | tf_op jit(solution)/shard_map/ppermute | solution.py:36
  7.7 12.6 %collective-permute-start.2 = (bf16[144,512]{1,0:T(8,128)(2,1)S(1)}, bf16[144,512]{1,0:T(8,128)(2,1)S(1)}, u32[]{:S(2)}, u32[]{:S(2)}) collective-permute-start(bf16[144,512]{1,0:T(8,128)(2,1)S(1)} %concatenate.6.refs_0_), channel_id=1, source_target_pairs={{0,96},{8,104},{16,112},{24,120},{32,0},{40,8},{48,16},{56,24},{64... | collective-permute-start | bytes 442376 | tf_op jit(solution)/shard_map/ppermute | solution.py:36
  10.8 12.3 %collective-permute-start.1 = (bf16[144,512]{1,0:T(8,128)(2,1)S(1)}, bf16[144,512]{1,0:T(8,128)(2,1)S(1)}, u32[]{:S(2)}, u32[]{:S(2)}) collective-permute-start(bf16[144,512]{1,0:T(8,128)(2,1)S(1)} %concatenate.6.refs_0_), channel_id=1, source_target_pairs={{0,16},{8,24},{16,32},{24,40},{32,48},{40,56},{48,64},{56,72},{64,... | collective-permute-start | bytes 442376 | tf_op jit(solution)/shard_map/ppermute | solution.py:36
  16.6 7.6 %collective-permute-start = (bf16[144,512]{1,0:T(8,128)(2,1)S(1)}, bf16[144,512]{1,0:T(8,128)(2,1)S(1)}, u32[]{:S(2)}, u32[]{:S(2)}) collective-permute-start(bf16[144,512]{1,0:T(8,128)(2,1)S(1)} %concatenate.6.refs_0_), channel_id=1, source_target_pairs={{0,112},{8,120},{16,0},{24,8},{32,16},{40,24},{48,32},{56,40},{64,... | collective-permute-start | bytes 442376 | tf_op jit(solution)/shard_map/ppermute | solution.py:36
  20.4 14.4 %collective-permute-start.7 = (bf16[144,512]{1,0:T(8,128)(2,1)S(1)}, bf16[144,512]{1,0:T(8,128)(2,1)S(1)}, u32[]{:S(2)}, u32[]{:S(2)}) collective-permute-start(bf16[144,512]{1,0:T(8,128)(2,1)S(1)} %broadcast_select_fusion), channel_id=1, source_target_pairs={{0,32},{8,40},{16,112},{24,120},{32,64},{40,72},{48,16},{56,24},{6... | collective-permute-start | bytes 442376 | tf_op jit(solution)/shard_map/ppermute | solution.py:54
  23.2 11.6 %collective-permute-start.6 = (bf16[144,512]{1,0:T(8,128)(2,1)S(1)}, bf16[144,512]{1,0:T(8,128)(2,1)S(1)}, u32[]{:S(2)}, u32[]{:S(2)}) collective-permute-start(bf16[144,512]{1,0:T(8,128)(2,1)S(1)} %collective-permute-done.3.refs_4_), channel_id=1, source_target_pairs={{0,16},{8,24},{16,32},{24,40},{32,48},{40,56},{48,64},{56,72},{64,... | collective-permute-start | bytes 442376 | tf_op jit(solution)/shard_map/ppermute | solution.py:36
  24.2 10.6 %collective-permute-start.5 = (bf16[144,512]{1,0:T(8,128)(2,1)S(1)}, bf16[144,512]{1,0:T(8,128)(2,1)S(1)}, u32[]{:S(2)}, u32[]{:S(2)}) collective-permute-start(bf16[144,512]{1,0:T(8,128)(2,1)S(1)} %collective-permute-done.2.refs_3_), channel_id=1, source_target_pairs={{0,112},{8,120},{16,0},{24,8},{32,16},{40,24},{48,32},{56,40},{64,... | collective-permute-start | bytes 442376 | tf_op jit(solution)/shard_map/ppermute | solution.py:36
  34.8 2.4 %collective-permute-start.9 = (bf16[3088,128]{1,0:T(8,128)(2,1)S(1)}, bf16[3088,128]{1,0:T(8,128)(2,1)S(1)}, u32[]{:S(2)}, u32[]{:S(2)}) collective-permute-start(bf16[3088,128]{1,0:T(8,128)(2,1)S(1)} %collective-permute-done.4.refs_10_), channel_id=1, source_target_pairs={{0,8},{8,0},{16,24},{24,16},{32,40},{40,32},{48,56},{56,48},{64,72... | collective-permute-start | bytes 2371592 | tf_op jit(solution)/shard_map/ppermute | solution.py:36
  46.6 0.7 copy-start
  47.3 10.8 %copy-start.1 = (f32[8,512]{1,0:T(8,128)}, f32[8,512]{1,0:T(8,128)S(1)}, u32[]{:S(2)}) copy-start(f32[8,512]{1,0:T(8,128)S(1)} %get-tuple-element.45.refs_2_) | copy-start | bytes 49156
  47.3 7.5 %collective-permute-start.12 = (bf16[144,512]{1,0:T(8,128)(2,1)S(1)}, bf16[144,512]{1,0:T(8,128)(2,1)S(1)}, u32[]{:S(2)}, u32[]{:S(2)}) collective-permute-start(bf16[144,512]{1,0:T(8,128)(2,1)S(1)} %get-tuple-element.50), channel_id=1, source_target_pairs={{0,112},{8,120},{16,0},{24,8},{32,16},{40,24},{48,32},{56,40},{64,... | collective-permute-start | bytes 442376 | tf_op jit(solution)/shard_map/ppermute | solution.py:36
  47.3 7.5 %collective-permute-start.13 = (bf16[144,512]{1,0:T(8,128)(2,1)S(1)}, bf16[144,512]{1,0:T(8,128)(2,1)S(1)}, u32[]{:S(2)}, u32[]{:S(2)}) collective-permute-start(bf16[144,512]{1,0:T(8,128)(2,1)S(1)} %get-tuple-element.51), channel_id=1, source_target_pairs={{0,16},{8,24},{16,32},{24,40},{32,48},{40,56},{48,64},{56,72},{64,... | collective-permute-start | bytes 442376 | tf_op jit(solution)/shard_map/ppermute | solution.py:36
  50.2 7.7 %collective-permute-start.14 = (bf16[144,512]{1,0:T(8,128)(2,1)S(1)}, bf16[144,512]{1,0:T(8,128)(2,1)S(1)}, u32[]{:S(2)}, u32[]{:S(2)}) collective-permute-start(bf16[144,512]{1,0:T(8,128)(2,1)S(1)} %get-tuple-element.52), channel_id=1, source_target_pairs={{0,32},{8,40},{16,112},{24,120},{32,64},{40,72},{48,16},{56,24},{6... | collective-permute-start | bytes 442376 | tf_op jit(solution)/shard_map/ppermute | solution.py:54
  51.6 10.7 %collective-permute-start.10 = (bf16[144,512]{1,0:T(8,128)(2,1)S(1)}, bf16[144,512]{1,0:T(8,128)(2,1)S(1)}, u32[]{:S(2)}, u32[]{:S(2)}) collective-permute-start(bf16[144,512]{1,0:T(8,128)(2,1)S(1)} %get-tuple-element.46), channel_id=1, source_target_pairs={{0,16},{8,24},{16,32},{24,40},{32,48},{40,56},{48,64},{56,72},{64,... | collective-permute-start | bytes 442376 | tf_op jit(solution)/shard_map/ppermute | solution.py:36
  52.2 10.2 %collective-permute-start.11 = (bf16[144,512]{1,0:T(8,128)(2,1)S(1)}, bf16[144,512]{1,0:T(8,128)(2,1)S(1)}, u32[]{:S(2)}, u32[]{:S(2)}) collective-permute-start(bf16[144,512]{1,0:T(8,128)(2,1)S(1)} %get-tuple-element.47), channel_id=1, source_target_pairs={{0,112},{8,120},{16,0},{24,8},{32,16},{40,24},{48,32},{56,40},{64,... | collective-permute-start | bytes 442376 | tf_op jit(solution)/shard_map/ppermute | solution.py:36
  58.1 11.1 %collective-permute-start.15 = (bf16[144,512]{1,0:T(8,128)(2,1)S(1)}, bf16[144,512]{1,0:T(8,128)(2,1)S(1)}, u32[]{:S(2)}, u32[]{:S(2)}) collective-permute-start(bf16[144,512]{1,0:T(8,128)(2,1)S(1)} %get-tuple-element.53), channel_id=1, source_target_pairs={{0,32},{8,40},{16,48},{24,56},{32,64},{40,72},{48,80},{56,88},{64,... | collective-permute-start | bytes 442376 | tf_op jit(solution)/shard_map/ppermute | solution.py:36
  60.8 9.9 %collective-permute-start.16 = (bf16[144,512]{1,0:T(8,128)(2,1)S(1)}, bf16[144,512]{1,0:T(8,128)(2,1)S(1)}, u32[]{:S(2)}, u32[]{:S(2)}) collective-permute-start(bf16[144,512]{1,0:T(8,128)(2,1)S(1)} %get-tuple-element.54), channel_id=1, source_target_pairs={{0,96},{8,104},{16,112},{24,120},{32,0},{40,8},{48,16},{56,24},{64... | collective-permute-start | bytes 442376 | tf_op jit(solution)/shard_map/ppermute | solution.py:36
  62.4 8.4 %copy-start.4 = (bf16[144,512]{1,0:T(8,128)(2,1)}, bf16[144,512]{1,0:T(8,128)(2,1)S(1)}, u32[]{:S(2)}) copy-start(bf16[144,512]{1,0:T(8,128)(2,1)S(1)} %collective-permute-done.10.refs_3_) | copy-start | bytes 442372
  62.4 8.4 %copy-start.5 = (bf16[144,512]{1,0:T(8,128)(2,1)}, bf16[144,512]{1,0:T(8,128)(2,1)S(1)}, u32[]{:S(2)}) copy-start(bf16[144,512]{1,0:T(8,128)(2,1)S(1)} %collective-permute-done.11.refs_4_) | copy-start | bytes 442372
  69.2 1.5 %copy-start.6 = (bf16[144,512]{1,0:T(8,128)(2,1)}, bf16[144,512]{1,0:T(8,128)(2,1)S(1)}, u32[]{:S(2)}) copy-start(bf16[144,512]{1,0:T(8,128)(2,1)S(1)} %collective-permute-done.15.refs_5_) | copy-start | bytes 442372
  77.5 10.9 %collective-permute-start.17 = (bf16[128,1024]{1,0:T(8,128)(2,1)}, bf16[128,1024]{1,0:T(8,128)(2,1)S(1)}, u32[]{:S(2)}, u32[]{:S(2)}) collective-permute-start(bf16[128,1024]{1,0:T(8,128)(2,1)} %get-tuple-element.56), channel_id=1, source_target_pairs={{0,1},{1,0},{2,3},{3,2},{4,5},{5,4},{6,7},{7,6},{8,9},{9,8},{10,11... | collective-permute-start | bytes 786440 | tf_op jit(solution)/shard_map/ppermute | solution.py:44
  80.5 10.9 %collective-permute-start.18 = (bf16[128,1024]{1,0:T(8,128)(2,1)}, bf16[128,1024]{1,0:T(8,128)(2,1)S(1)}, u32[]{:S(2)}, u32[]{:S(2)}) collective-permute-start(bf16[128,1024]{1,0:T(8,128)(2,1)} %get-tuple-element.57), channel_id=1, source_target_pairs={{0,4},{1,5},{2,6},{3,7},{4,0},{5,1},{6,2},{7,3},{8,12},{9,13},{10,... | collective-permute-start | bytes 786440 | tf_op jit(solution)/shard_map/ppermute | solution.py:44
  81.9 15.2 %collective-permute-start.19 = (bf16[128,1024]{1,0:T(8,128)(2,1)}, bf16[128,1024]{1,0:T(8,128)(2,1)S(1)}, u32[]{:S(2)}, u32[]{:S(2)}) collective-permute-start(bf16[128,1024]{1,0:T(8,128)(2,1)} %get-tuple-element.58), channel_id=1, source_target_pairs={{0,5},{1,4},{2,7},{3,6},{4,1},{5,0},{6,3},{7,2},{8,13},{9,12},{10,... | collective-permute-start | bytes 786440 | tf_op jit(solution)/shard_map/ppermute | solution.py:44
  84.1 16.4 %collective-permute-start.20 = (bf16[128,1024]{1,0:T(8,128)(2,1)}, bf16[128,1024]{1,0:T(8,128)(2,1)S(1)}, u32[]{:S(2)}, u32[]{:S(2)}) collective-permute-start(bf16[128,1024]{1,0:T(8,128)(2,1)} %get-tuple-element.59), channel_id=1, source_target_pairs={{0,2},{1,3},{2,4},{3,5},{4,6},{5,7},{6,0},{7,1},{8,10},{9,11},{10,... | collective-permute-start | bytes 786440 | tf_op jit(solution)/shard_map/ppermute | solution.py:44
  84.6 25.3 %collective-permute-start.21 = (bf16[128,1024]{1,0:T(8,128)(2,1)}, bf16[128,1024]{1,0:T(8,128)(2,1)S(1)}, u32[]{:S(2)}, u32[]{:S(2)}) collective-permute-start(bf16[128,1024]{1,0:T(8,128)(2,1)} %get-tuple-element.60), channel_id=1, source_target_pairs={{0,3},{1,2},{2,5},{3,4},{4,7},{5,6},{6,1},{7,0},{8,11},{9,10},{10,... | collective-permute-start | bytes 786440 | tf_op jit(solution)/shard_map/ppermute | solution.py:44
  88.4 21.5 %collective-permute-start.22 = (bf16[128,1024]{1,0:T(8,128)(2,1)}, bf16[128,1024]{1,0:T(8,128)(2,1)S(1)}, u32[]{:S(2)}, u32[]{:S(2)}) collective-permute-start(bf16[128,1024]{1,0:T(8,128)(2,1)} %get-tuple-element.61), channel_id=1, source_target_pairs={{0,6},{1,7},{2,0},{3,1},{4,2},{5,3},{6,4},{7,5},{8,14},{9,15},{10,... | collective-permute-start | bytes 786440 | tf_op jit(solution)/shard_map/ppermute | solution.py:44
  91.5 19.2 %collective-permute-start.23 = (bf16[128,1024]{1,0:T(8,128)(2,1)}, bf16[128,1024]{1,0:T(8,128)(2,1)S(1)}, u32[]{:S(2)}, u32[]{:S(2)}) collective-permute-start(bf16[128,1024]{1,0:T(8,128)(2,1)} %get-tuple-element.62), channel_id=1, source_target_pairs={{0,7},{1,6},{2,1},{3,0},{4,3},{5,2},{6,5},{7,4},{8,15},{9,14},{10,... | collective-permute-start | bytes 786440 | tf_op jit(solution)/shard_map/ppermute | solution.py:44
  (1 other events, 0.7 us)

commit v2 on v1

v2 whole, which is shorter than its diff:
```python
import math

import jax
import jax.numpy as jnp
from jax import lax
from jax.experimental import pallas as pl
from jax.experimental.pallas import tpu as pltpu
from jax.sharding import PartitionSpec as P

BF16 = jnp.bfloat16
F32 = jnp.float32
NY, NZ, NC = 2, 8, 2
NX, NW = 4, 2
HD = 128
BLK = 128
QPG = 4
ROWS = QPG * BLK
EMPTY = -1e30
SCALE2 = math.log2(math.e) / math.sqrt(HD)
OFFSETS = (0, 1, -1, 2, -2, 3, -3, 4)
NEAR = 5
STEPS = (2, 1, 3, 0)
PAYLOAD = BLK + 16
PER_SOURCE = 12
KEYS_AT, VALUES_AT, MASK_AT = 0, PER_SOURCE * BLK, 2 * PER_SOURCE * BLK
SOURCE = MASK_AT + 16


def cache_step(x, dy, dz, dc):
    pairs = []
    for y in range(NY):
        for z in range(NZ):
            for c in range(NC):
                there = (((y + dy) % NY) * NZ + (z + dz) % NZ) * NC + (c + dc) % NC
                pairs.append(((y * NZ + z) * NC + c, there))
    return lax.ppermute(x, "cache", pairs)


def heads_step(x, dx, dw):
    pairs = []
    for a in range(NX):
        for w in range(NW):
            pairs.append((a * NW + w, ((a + dx) % NX) * NW + (w + dw) % NW))
    return lax.ppermute(x, "heads", pairs)


def z_ways(x, even, odd):
    pairs = []
    for y in range(NY):
        for z in range(NZ):
            for c in range(NC):
                there = (y * NZ + (z + (odd if z % 2 else even)) % NZ) * NC + c
                pairs.append(((y * NZ + z) * NC + c, there))
    return lax.ppermute(x, "cache", pairs)


def scores_of(keys, rows):
    return lax.dot_general(keys, rows, (((1,), (1,)), ((), ())), preferred_element_type=F32)


def weighted(values, weights):
    return lax.dot_general(
        values, weights.astype(BF16), (((0,), (0,)), ((), ())), preferred_element_type=F32
    )


def softmax_part(scores):
    peak = jnp.max(scores, axis=0, keepdims=True)
    weights = jnp.exp2((scores - peak) * SCALE2)
    return peak, jnp.sum(weights, axis=0, keepdims=True), weights


def fetch(packed, qbuf, qsem):
    copies = []
    for b, ref in enumerate(packed):
        for h in range(QPG):
            copies.append(
                pltpu.make_async_copy(
                    ref.at[pl.ds(0, BLK), pl.ds(h * HD, HD)],
                    qbuf.at[b, pl.ds(h * BLK, BLK), :],
                    qsem.at[b * QPG + h],
                )
            )
    for copy in copies:
        copy.start()
    return copies


def list_items(wanted, packed, sources, vis_v, vis_s, todo, dummy, vsem):
    blocks = sorted({b for b, _ in wanted})
    leaves = [packed[b][BLK:PAYLOAD, 0:HD].astype(F32)[0:1, :] for b in blocks]
    leaf = jnp.concatenate(leaves, axis=0)
    node_at = lax.broadcasted_iota(jnp.int32, leaf.shape, 1).astype(F32)
    chosen = jnp.where(node_at == leaf, 1.0, 0.0).astype(BF16)
    for s in sorted({s for _, s in wanted}):
        seen = scores_of(chosen, sources[s][MASK_AT:SOURCE, :])
        vis_v[8 * s : 8 * s + len(blocks), 0:16] = seen.astype(jnp.int32)
    copy = pltpu.make_async_copy(vis_v, vis_s, vsem)
    copy.start()
    copy.wait()
    count = jnp.int32(0)
    for b, s in wanted:
        for c in range(PER_SOURCE):
            todo[count] = b * 64 + s * 16 + c
            count = count + vis_s[8 * s + b, c]
    for i in range(6):
        todo[count + i] = dummy * 64
    return count


def work(count, todo, nq, qbuf, sources, state, ahead):
    def place(item):
        b = lax.shift_right_logical(item, 6)
        s = lax.bitwise_and(lax.shift_right_logical(item, 4), 3)
        return b, s, pl.multiple_of(lax.bitwise_and(item, 15) * BLK, BLK)

    def rows_of(s, row):
        rows = sources[0][pl.ds(row, BLK), :]
        for i in range(1, len(sources)):
            rows = jnp.where(s == i, sources[i][pl.ds(row, BLK), :], rows)
        return rows

    def scored(item):
        b, s, row = place(item)
        return scores_of(rows_of(s, row), qbuf[jnp.minimum(b, nq - 1)])

    def taken(item, scores):
        b, s, row = place(item)
        peak, total, weights = softmax_part(scores)
        return b, peak, total, weighted(rows_of(s, VALUES_AT + row), weights)

    def score_two(slot, at):
        ahead[slot, 0] = scored(todo[at])
        ahead[slot, 1] = scored(todo[at + 1])

    def take_two(slot, at):
        first = taken(todo[at], ahead[slot, 0])
        second = taken(todo[at + 1], ahead[slot, 1])
        merge(state, *first)
        merge(state, *second)

    def four(i, carry):
        score_two(1, 4 * i + 2)
        take_two(0, 4 * i)
        score_two(0, 4 * i + 4)
        take_two(1, 4 * i + 2)
        return carry

    score_two(0, 0)
    lax.fori_loop(0, lax.shift_right_logical(count + 3, 2), four, 0)


def merge(state, b, peak, total, summed):
    peaks, totals, sums = state
    before = peaks[b]
    after = jnp.maximum(before, peak)
    keep = jnp.exp2((before - after) * SCALE2)
    take = jnp.exp2((peak - after) * SCALE2)
    peaks[b] = after
    totals[b] = totals[b] * keep + total * take
    sums[b] = sums[b] * keep + summed * take


def column_copies(weight, out, sem, other_w):
    x = lax.shift_right_logical(lax.axis_index("heads"), 1)
    w = lax.bitwise_xor(lax.bitwise_and(lax.axis_index("heads"), 1), other_w)
    width = out.shape[2]
    copies = []
    for j, dx in enumerate(STEPS):
        column = lax.bitwise_and(x + dx, NX - 1) * NW + w
        columns = pl.ds(pl.multiple_of(column * width, width), width)
        copies.append(pltpu.make_async_copy(weight.at[:, columns], out.at[j], sem.at[j]))
    for copy in copies:
        copy.start()
    return copies


def early_kernel(length, own, suffix_k, suffix_v, weight, peak, total, summed, far_w, sem):
    copies = column_copies(weight, far_w, sem, 1)
    rows = jnp.concatenate([own[0:BLK, h * HD : (h + 1) * HD] for h in range(QPG)], axis=0)
    key_at = lax.broadcasted_iota(jnp.int32, (BLK, ROWS), 0)
    row_at = lax.bitwise_and(lax.broadcasted_iota(jnp.int32, (BLK, ROWS), 1), BLK - 1)
    scores = scores_of(suffix_k[...], rows)
    scores = jnp.where((key_at <= row_at) & (key_at < length[0]), scores, EMPTY)
    peak[...], total[...], weights = softmax_part(scores)
    summed[...] = weighted(suffix_v[...], weights)
    for copy in copies:
        copy.wait()


def laid_out(weight):
    return jax.ShapeDtypeStruct((NX, weight.shape[0], weight.shape[1] // (NX * NW)), BF16)


def early(length, own, suffix_k, suffix_v, weight):
    return pl.pallas_call(
        early_kernel,
        out_shape=[
            jax.ShapeDtypeStruct((1, ROWS), F32),
            jax.ShapeDtypeStruct((1, ROWS), F32),
            jax.ShapeDtypeStruct((HD, ROWS), F32),
            laid_out(weight),
        ],
        in_specs=[SMEM] + [VMEM] * 3 + [HBM],
        out_specs=[VMEM] * 4,
        scratch_shapes=[pltpu.SemaphoreType.DMA((NX,))],
        compiler_params=pltpu.CompilerParams(vmem_limit_bytes=46 << 20),
        cost_estimate=pl.CostEstimate(
            flops=40_000_000, bytes_accessed=9 << 20, transcendentals=70_000
        ),
        name="early",
    )(length, own, suffix_k, suffix_v, weight)


def late_kernel(weight, home_w, sem):
    for copy in column_copies(weight, home_w, sem, 0):
        copy.wait()


def late(weight):
    return pl.pallas_call(
        late_kernel,
        out_shape=laid_out(weight),
        in_specs=[HBM],
        out_specs=VMEM,
        scratch_shapes=[pltpu.SemaphoreType.DMA((NX,))],
        compiler_params=pltpu.CompilerParams(vmem_limit_bytes=46 << 20),
        cost_estimate=pl.CostEstimate(flops=0, bytes_accessed=8 << 20, transcendentals=0),
        name="late",
    )(weight)


def first_kernel(*refs):
    packed, sources = refs[0:NEAR], refs[NEAR : NEAR + 2]
    suffix = refs[NEAR + 2 : NEAR + 5]
    state = refs[NEAR + 5 : NEAR + 8]
    todo, vis_s, vis_v, qbuf, ahead, qsem, vsem = refs[NEAR + 8 :]
    copies = fetch(packed, qbuf, qsem)
    wanted = [(b, s) for b in range(NEAR) for s in range(2)]
    count = list_items(wanted, packed, sources, vis_v, vis_s, todo, NEAR, vsem)
    peaks, totals, sums = state
    peaks[0], totals[0], sums[0] = suffix[0][...], suffix[1][...], suffix[2][...]
    clear(state, range(1, NEAR + 1))
    for copy in copies:
        copy.wait()
    work(count, todo, NEAR, qbuf, sources, state, ahead)


def clear(state, blocks):
    peaks, totals, sums = state
    for b in blocks:
        peaks[b] = jnp.full((1, ROWS), EMPTY, F32)
        totals[b] = jnp.zeros((1, ROWS), F32)
        sums[b] = jnp.zeros((HD, ROWS), F32)


def lse_rows(lse):
    high = lse.astype(BF16).astype(F32)
    middle = (lse - high).astype(BF16).astype(F32)
    low = lse - high - middle
    at = lax.broadcasted_iota(jnp.int32, (16, ROWS), 0)
    return jnp.where(at == 0, high, jnp.where(at == 1, middle, low)).astype(BF16)


def lse_of(rows):
    pieces = rows.astype(F32)
    return pieces[0:1] + pieces[1:2] + pieces[2:3]


def second_kernel(*refs):
    nq = len(OFFSETS)
    packed, sources, known = refs[0:nq], refs[nq : nq + 4], refs[nq + 4 : nq + 7]
    own_out, own_lse, p_out, m_out, far_out, ahead_out, back_out = refs[nq + 7 : nq + 14]
    todo, vis_s, vis_v, qbuf, ahead, peaks, totals, sums, qsem, vsem = refs[nq + 14 :]
    state = (peaks, totals, sums)
    copies = fetch(packed, qbuf, qsem)
    wanted = [(b, s) for b in range(NEAR, nq) for s in range(4)]
    wanted += [(b, s) for b in range(NEAR) for s in (2, 3)]
    count = list_items(wanted, packed, sources, vis_v, vis_s, todo, nq, vsem)
    clear(state, range(nq + 1))
    for copy in copies:
        copy.wait()
    work(count, todo, nq, qbuf, sources, state, ahead)
    places = {1: (p_out, 0), 5: (p_out, PAYLOAD), 2: (m_out, 0), 6: (m_out, PAYLOAD)}
    places |= {7: (far_out, 0), 3: (ahead_out, 0), 4: (back_out, 0)}
    for b in (5, 6, 7, 1, 2, 3, 4, 0):
        if b < NEAR:
            merge(state, b, known[0][b], known[1][b], known[2][b])
        total = totals[b]
        seen = total > 0.0
        safe = jnp.where(seen, total, 1.0)
        lse = jnp.where(seen, peaks[b] * SCALE2 + jnp.log2(safe), EMPTY)
        out = sums[b] * (1.0 / safe)
        if b == 0:
            own_out[...] = out
            own_lse[...] = jnp.broadcast_to(lse, own_lse.shape)
        else:
            ref, at = places[b]
            ref[at : at + BLK, :] = out.astype(BF16)
            ref[at + BLK : at + PAYLOAD, :] = lse_rows(lse)


SMEM = pl.BlockSpec(memory_space=pltpu.SMEM)
VMEM = pl.BlockSpec(memory_space=pltpu.VMEM)
HBM = pl.BlockSpec(memory_space=pltpu.HBM)


def state_shapes(count):
    return [(count, 1, ROWS), (count, 1, ROWS), (count, HD, ROWS)]


def buffers(nq):
    return [
        pltpu.SMEM((nq * 4 * PER_SOURCE + 8,), jnp.int32),
        pltpu.SMEM((32, HD), jnp.int32),
        pltpu.VMEM((32, HD), jnp.int32),
        pltpu.VMEM((nq, ROWS, HD), BF16),
        pltpu.VMEM((2, 2, BLK, ROWS), F32),
    ]


def semaphores(nq):
    return [pltpu.SemaphoreType.DMA((nq * QPG,)), pltpu.SemaphoreType.DMA]


def first_part(packed, sources, suffix):
    return pl.pallas_call(
        first_kernel,
        out_shape=[jax.ShapeDtypeStruct(s, F32) for s in state_shapes(NEAR + 1)],
        in_specs=[VMEM] * (NEAR + 5),
        out_specs=[VMEM] * 3,
        scratch_shapes=buffers(NEAR) + semaphores(NEAR),
        compiler_params=pltpu.CompilerParams(vmem_limit_bytes=12 << 20),
        cost_estimate=pl.CostEstimate(
            flops=2_000_000_000, bytes_accessed=4 << 20, transcendentals=1_000_000
        ),
        name="first_part",
    )(*packed, *sources, *suffix)


def second_part(packed, sources, known):
    nq = len(OFFSETS)
    payload = jax.ShapeDtypeStruct((PAYLOAD, ROWS), BF16)
    double = jax.ShapeDtypeStruct((2 * PAYLOAD, ROWS), BF16)
    return pl.pallas_call(
        second_kernel,
        out_shape=[
            jax.ShapeDtypeStruct((HD, ROWS), F32),
            jax.ShapeDtypeStruct((8, ROWS), F32),
            double,
            double,
            payload,
            payload,
            payload,
        ],
        in_specs=[VMEM] * (nq + 7),
        out_specs=[VMEM] * 7,
        scratch_shapes=buffers(nq)
        + [pltpu.VMEM(s, F32) for s in state_shapes(nq + 1)]
        + semaphores(nq),
        compiler_params=pltpu.CompilerParams(vmem_limit_bytes=16 << 20),
        cost_estimate=pl.CostEstimate(
            flops=4_000_000_000, bytes_accessed=6 << 20, transcendentals=3_000_000
        ),
        name="second_part",
    )(*packed, *sources, *known)


def join_kernel(ahead, back, from_ahead, from_back, from_far, ahead_out, back_out):
    odd = lax.bitwise_and(lax.shift_right_logical(lax.axis_index("cache"), 1), 1)
    from_ahead, from_back = from_ahead.at[PAYLOAD:], from_back.at[PAYLOAD:]
    for own, other, out, far_here in (
        (ahead, from_back, ahead_out, odd == 0),
        (back, from_ahead, back_out, odd == 1),
    ):
        parts = (own, other, from_far)
        lses = [lse_of(part[BLK:PAYLOAD, :]) for part in parts]
        lses[2] = jnp.where(far_here, lses[2], EMPTY)
        top = jnp.maximum(jnp.maximum(lses[0], lses[1]), lses[2])
        shares = [jnp.exp2(lse - top) for lse in lses]
        total = shares[0] + shares[1] + shares[2]
        inverse = 1.0 / total
        summed = parts[0][0:BLK, :].astype(F32) * (shares[0] * inverse)
        for part, share in zip(parts[1:], shares[1:]):
            summed = summed + part[0:BLK, :].astype(F32) * (share * inverse)
        out[0:BLK, :] = summed.astype(BF16)
        out[BLK:PAYLOAD, :] = lse_rows(jnp.maximum(top + jnp.log2(total), EMPTY))


def join(*parts):
    return pl.pallas_call(
        join_kernel,
        out_shape=[jax.ShapeDtypeStruct((PAYLOAD, ROWS), BF16)] * 2,
        in_specs=[VMEM] * 5,
        out_specs=[VMEM] * 2,
        compiler_params=pltpu.CompilerParams(vmem_limit_bytes=6 << 20),
        cost_estimate=pl.CostEstimate(
            flops=2_000_000, bytes_accessed=1 << 20, transcendentals=4096
        ),
        name="join",
    )(*parts)


def merged_rows(own_out, own_lse, payloads):
    lses = [own_lse[0:1, :]] + [lse_of(payload[BLK:PAYLOAD, :]) for payload in payloads]
    top = lses[0]
    for lse in lses[1:]:
        top = jnp.maximum(top, lse)
    parts_of = [jnp.exp2(lse - top) for lse in lses]
    total = parts_of[0]
    for part in parts_of[1:]:
        total = total + part
    inverse = 1.0 / total
    mixed = own_out[...] * (parts_of[0] * inverse)
    for payload, part in zip(payloads, parts_of[1:]):
        mixed = mixed + payload[0:BLK, :].astype(F32) * (part * inverse)
    return mixed


def project(rows, weight, outs):
    tile = 256
    for j, out in enumerate(outs):
        for t in range(weight.shape[2] // tile):
            columns = slice(t * tile, (t + 1) * tile)
            out[:, columns] = jnp.dot(
                rows, weight[j, :, columns], preferred_element_type=F32
            ).astype(out.dtype)


def away_kernel(own_out, own_lse, p1, m1, p2, m2, weight, rows_out, *outs):
    mixed = merged_rows(own_out, own_lse, (p1, m1, p2, m2))
    for h in range(QPG):
        columns = slice(h * BLK, (h + 1) * BLK)
        rows_out[:, columns] = mixed[:, columns].T.astype(BF16)
    project(rows_out[...], weight, outs)


def home_kernel(rows, weight, *outs):
    project(rows[...], weight, outs)


def projected(kernel, name, operands, weight, more):
    return pl.pallas_call(
        kernel,
        out_shape=more
        + [jax.ShapeDtypeStruct((BLK, weight.shape[2]), F32 if dx == 0 else BF16) for dx in STEPS],
        in_specs=[VMEM] * (len(operands) + 1),
        out_specs=[VMEM] * (len(more) + NX),
        compiler_params=pltpu.CompilerParams(vmem_limit_bytes=12 << 20),
        cost_estimate=pl.CostEstimate(
            flops=550_000_000, bytes_accessed=5 << 20, transcendentals=4096
        ),
        name=name,
    )(*operands, weight)


def add_kernel(first, *refs):
    others, out = refs[:-1], refs[-1]
    total = first[...]
    for other in others:
        total = total + other[...].astype(F32)
    out[...] = total.astype(out.dtype)


def sum_of(name, first, others):
    return pl.pallas_call(
        add_kernel,
        out_shape=jax.ShapeDtypeStruct(first.shape, BF16),
        in_specs=[VMEM] * (1 + len(others)),
        out_specs=VMEM,
        compiler_params=pltpu.CompilerParams(vmem_limit_bytes=6 << 20),
        cost_estimate=pl.CostEstimate(
            flops=1_000_000, bytes_accessed=2 << 20, transcendentals=0
        ),
        name=name,
    )(first, *others)


def shards(
    queries,
    cache_keys,
    cache_values,
    suffix_keys,
    suffix_values,
    out_weight,
    ancestor_mask,
    leaf_node,
    suffix_len,
):
    z = lax.bitwise_and(lax.shift_right_logical(lax.axis_index("cache"), 1), NZ - 1)
    leaf_rows = jnp.broadcast_to(leaf_node.astype(BF16)[:, None], (16, ROWS))
    own = jnp.concatenate([queries, leaf_rows], axis=0)
    count, nodes = ancestor_mask.shape[1], ancestor_mask.shape[0]
    mask = jnp.pad(ancestor_mask.T.astype(BF16), ((0, 16 - count), (0, HD - nodes)))
    source = jnp.concatenate([cache_keys, cache_values, mask], axis=0)
    across = cache_step(source, 1, 0, 0)
    p2, m2 = cache_step(own, 0, -2, 0), cache_step(own, 0, 2, 0)
    near = cache_step(source, 0, 0, 1)
    near, own = lax.optimization_barrier((near, own))
    p1, m1 = cache_step(own, 0, -1, 0), cache_step(own, 0, 1, 0)
    *suffix, far_w = early(suffix_len, own, suffix_keys, suffix_values, out_weight)
    p2, m2, *suffix = lax.optimization_barrier((p2, m2, *suffix))
    p3, m3 = cache_step(p2, 0, -1, 0), cache_step(m2, 0, 1, 0)
    p4 = z_ways(jnp.where(lax.bitwise_and(z, 1) == 0, m2, p2), 2, -2)
    known = first_part([own, p1, m1, p2, m2], [source, near], suffix)
    across, p3, m3, p4, *known = lax.optimization_barrier((across, p3, m3, p4, *known))
    far = cache_step(across, 0, 0, 1)
    own_out, own_lse, o_p, o_m, o_far, o_p2, o_m2 = second_part(
        [own, p1, m1, p2, m2, p3, m3, p4], [source, near, across, far], known
    )
    from_far = z_ways(o_far, 2, -2)
    later_weight, own_lse = lax.optimization_barrier((out_weight, own_lse))
    home_w = late(later_weight)
    from_back, from_ahead = cache_step(o_p, 0, 1, 0), cache_step(o_m, 0, -1, 0)
    from_far, home_w = lax.optimization_barrier((from_far, home_w))
    ahead, back = join(o_p2, o_m2, from_ahead, from_back, from_far)
    r_p2, r_m2 = cache_step(ahead, 0, 2, 0), cache_step(back, 0, -2, 0)
    merged, *shares = projected(
        away_kernel,
        "away",
        [own_out, own_lse, from_back, from_ahead, r_p2, r_m2],
        far_w,
        [jax.ShapeDtypeStruct((BLK, ROWS), BF16)],
    )
    arrived = [heads_step(share, dx, 0) for share, dx in zip(shares[:-1], STEPS)]
    kept = projected(home_kernel, "home", [merged], home_w, [])
    passed = heads_step(sum_of("pass_on", shares[-1], arrived), 0, 1)
    arrived = [heads_step(share, dx, 0) for share, dx in zip(kept[:-1], STEPS)]
    return sum_of("finish", kept[-1], [*arrived, passed])


def solution(mesh):
    return jax.shard_map(
        shards,
        mesh=mesh,
        in_specs=(
            P("cache", "heads"),
            P("cache", "heads"),
            P("cache", "heads"),
            P("cache", "heads"),
            P("cache", "heads"),
            P("heads", None),
            P(None, "cache"),
            P("cache"),
            P("cache"),
        ),
        out_specs=P("cache", "heads"),
        check_vma=False,
    )
```

time: 113 us -> 93.9 us (0.83)
  starting transfers between devices: 44.2 us -> 36.3 us
  Pallas kernels: 22.7 us -> 16.7 us
  other arithmetic: 3.99 us -> 1.92 us
  waiting for transfers between devices: 39 us -> 37.1 us
  local copies, waits for them, and re-layouts: 1.4 us -> 0.02 us
    ppermute x15 -> x13, starting transfers between devices: 27.5 us -> 21.1 us  [cache_step(): return lax.ppermute(x, 'cache', pairs)]
    ppermute x2, waiting for transfers between devices: 3.04 us -> 8.3 us  [z_ways(): return lax.ppermute(x, 'cache', pairs)]
    ppermute x7, waiting for transfers between devices: 20.7 us -> 16.1 us  [heads_step(): return lax.ppermute(x, 'heads', pairs)]
    pallas_call x1, Pallas kernels: 9.41 us -> 5.81 us  [second_part(): pl.pallas_call(second_kernel, out_shape=[jax.ShapeDtypeStruct((HD, ROWS),...]
    pallas_call x1, Pallas kernels: 6.92 us -> 3.41 us  [first_part(): pl.pallas_call(first_kernel, out_shape=[jax.ShapeDtypeStruct(s, F32) for...]
    ppermute x15 -> x13, waiting for transfers between devices: 15.3 us -> 12.7 us  [cache_step(): return lax.ppermute(x, 'cache', pairs)]
    convert_element_type x1 -> x0, other arithmetic: 2.07 us -> none  [shards(): return mixed.astype(BF16)]
    ppermute x7, starting transfers between devices: 12.4 us -> 10.8 us  [heads_step(): return lax.ppermute(x, 'heads', pairs)]
  transfers between devices with their start and end apart: 24 -> 22, of which waited for: 11 -> 12; matrix products, arithmetic and copies ran while one was open for 0% -> 0% of each run, Pallas kernels for 6% -> 10%
where the time goes in v2:
time: 93.9 us; the launch traced here: 93.6 us
  waiting for transfers between devices  37.1 us (40%)
  starting transfers between devices  36.3 us (39%)
  Pallas kernels  16.7 us (18%)
  other arithmetic  1.92 us (2%)
  between operations  1.46 us (2%)
    ppermute x13, starting transfers between devices, cache_step(): return lax.ppermute(x, 'cache', pairs)  21.1 us
    ppermute x7, waiting for transfers between devices, heads_step(): return lax.ppermute(x, 'heads', pairs)  16.1 us
    ppermute x13, waiting for transfers between devices, cache_step(): return lax.ppermute(x, 'cache', pairs)  12.7 us
    ppermute x7, starting transfers between devices, heads_step(): return lax.ppermute(x, 'heads', pairs)  10.8 us
    ppermute x2, waiting for transfers between devices, z_ways(): return lax.ppermute(x, 'cache', pairs)  8.3 us
    pallas_call x1, Pallas kernels, second_part(): pl.pallas_call(second_kernel, out_shape=[jax.ShapeDtypeStruct((HD, ROWS),...  5.81 us
    ppermute x2, starting transfers between devices, z_ways(): return lax.ppermute(x, 'cache', pairs)  4.44 us
    pallas_call x1, Pallas kernels, first_part(): pl.pallas_call(first_kernel, out_shape=[jax.ShapeDtypeStruct(s, F32) for...  3.41 us
  transfers between devices with their start and end apart: 22, of which 12 were waited for; matrix products, arithmetic and copies ran while one was open for 0% of the time, Pallas kernels for 10%

profile of v2, /device:TPU:6, one launch (start us, length us, event | category | flops | bytes accessed | tf_op | source)
XLA Modules:
  0.0 93.6 jit_solution(6021289202455081900)
XLA Ops:
  0.7 1.2 %fusion.1.refs_5_.refs_8_ = bf16[3088,128]{1,0:T(8,128)(2,1)S(1)} fusion(bf16[12,64]{1,0:T(8,128)(2,1)S(1)} %convert_bitcast_fusion, bf16[1536,128]{1,0:T(8,128)(2,1)} %param.11, bf16[1536,128]{1,0:T(8,128)(2,1)} %param.10), kind=kLoop, calls=%fused_computation.2 | loop fusion | flops 3162112 | bytes 1578496 | tf_op jit(solution)/shard_map/concatenate | solution.py:495
  2.0 1.7 %collective-permute-start.5 = (bf16[3088,128]{1,0:T(8,128)(2,1)S(1)}, bf16[3088,128]{1,0:T(8,128)(2,1)S(1)}, u32[]{:S(2)}, u32[]{:S(2)}) collective-permute-start(bf16[3088,128]{1,0:T(8,128)(2,1)S(1)} %fusion.1.refs_5_.refs_8_), channel_id=1, source_target_pairs={{0,128},{8,136},{16,144},{24,152},{32,160},{40,168},{48,176},{56,1... | collective-permute-start | bytes 2371592 | tf_op jit(solution)/shard_map/ppermute | solution.py:36
  4.4 3.3 %collective-permute-start.4 = (bf16[144,512]{1,0:T(8,128)(2,1)S(1)}, bf16[144,512]{1,0:T(8,128)(2,1)S(1)}, u32[]{:S(2)}, u32[]{:S(2)}) collective-permute-start(bf16[144,512]{1,0:T(8,128)(2,1)S(1)} %concatenate.7.own.refs_0_), channel_id=1, source_target_pairs={{0,32},{8,40},{16,48},{24,56},{32,64},{40,72},{48,80},{56,88},{64,... | collective-permute-start | bytes 442376 | tf_op jit(solution)/shard_map/ppermute | solution.py:36
  7.7 3.1 %collective-permute-start.3 = (bf16[144,512]{1,0:T(8,128)(2,1)S(1)}, bf16[144,512]{1,0:T(8,128)(2,1)S(1)}, u32[]{:S(2)}, u32[]{:S(2)}) collective-permute-start(bf16[144,512]{1,0:T(8,128)(2,1)S(1)} %concatenate.7.own.refs_0_), channel_id=1, source_target_pairs={{0,96},{8,104},{16,112},{24,120},{32,0},{40,8},{48,16},{56,24},{64... | collective-permute-start | bytes 442376 | tf_op jit(solution)/shard_map/ppermute | solution.py:36
  11.5 1.1 %collective-permute-start.2 = (bf16[144,512]{1,0:T(8,128)(2,1)S(1)}, bf16[144,512]{1,0:T(8,128)(2,1)S(1)}, u32[]{:S(2)}, u32[]{:S(2)}) collective-permute-start(bf16[144,512]{1,0:T(8,128)(2,1)S(1)} %concatenate.7.own.refs_0_), channel_id=1, source_target_pairs={{0,16},{8,24},{16,32},{24,40},{32,48},{40,56},{48,64},{56,72},{64,... | collective-permute-start | bytes 442376 | tf_op jit(solution)/shard_map/ppermute | solution.py:36
  12.6 2.2 %collective-permute-start.1 = (bf16[144,512]{1,0:T(8,128)(2,1)S(1)}, bf16[144,512]{1,0:T(8,128)(2,1)S(1)}, u32[]{:S(2)}, u32[]{:S(2)}) collective-permute-start(bf16[144,512]{1,0:T(8,128)(2,1)S(1)} %concatenate.7.own.refs_0_), channel_id=1, source_target_pairs={{0,112},{8,120},{16,0},{24,8},{32,16},{40,24},{48,32},{56,40},{64,... | collective-permute-start | bytes 442376 | tf_op jit(solution)/shard_map/ppermute | solution.py:36
  14.8 2.5 %early.1 = (f32[1,512]{1,0:T(1,128)S(1)}, f32[1,512]{1,0:T(1,128)S(1)}, f32[128,512]{1,0:T(8,128)S(1)}, bf16[4,512,1024]{2,1,0:T(8,128)(2,1)S(1)}) custom-call(s32[1]{0:T(128)S(6)} %copy.11.length, bf16[144,512]{1,0:T(8,128)(2,1)S(1)} %concatenate.7.own.refs_0_, bf16[128,128]{1,0:T(8,128)(2,1)S(1)} %copy-done, bf16[128,128]{1,0:T(8,128)(2,1)S(1)} %copy-done.1, ...), custom_call_target="tpu_custom_call" | custom-call | flops 40000000 | bytes 9437184 | tf_op jit(solution)/shard_map/early/pallas_call | solution.py:196
  17.3 2.4 %collective-permute-done.3.refs_3_ = bf16[144,512]{1,0:T(8,128)(2,1)S(1)} collective-permute-done((bf16[144,512]{1,0:T(8,128)(2,1)S(1)}, bf16[144,512]{1,0:T(8,128)(2,1)S(1)}, u32[]{:S(2)}, u32[]{:S(2)}) %collective-permute-start.3) | collective-permute-done | bytes 147488 | tf_op jit(solution)/shard_map/ppermute | solution.py:36
  19.8 1.8 %collective-permute-start.6 = (bf16[144,512]{1,0:T(8,128)(2,1)S(1)}, bf16[144,512]{1,0:T(8,128)(2,1)S(1)}, u32[]{:S(2)}, u32[]{:S(2)}) collective-permute-start(bf16[144,512]{1,0:T(8,128)(2,1)S(1)} %collective-permute-done.3.refs_3_), channel_id=1, source_target_pairs={{0,112},{8,120},{16,0},{24,8},{32,16},{40,24},{48,32},{56,40},{64,... | collective-permute-start | bytes 442376 | tf_op jit(solution)/shard_map/ppermute | solution.py:36
  21.8 4.0 %collective-permute-start.8 = (bf16[144,512]{1,0:T(8,128)(2,1)S(1)}, bf16[144,512]{1,0:T(8,128)(2,1)S(1)}, u32[]{:S(2)}, u32[]{:S(2)}) collective-permute-start(bf16[144,512]{1,0:T(8,128)(2,1)S(1)} %broadcast_select_fusion), channel_id=1, source_target_pairs={{0,32},{8,40},{16,112},{24,120},{32,64},{40,72},{48,16},{56,24},{6... | collective-permute-start | bytes 442376 | tf_op jit(solution)/shard_map/ppermute | solution.py:54
  25.8 3.4 %first_part.1 = (f32[6,1,512]{2,1,0:T(1,128)S(1)}, f32[6,1,512]{2,1,0:T(1,128)S(1)}, f32[6,128,512]{2,1,0:T(8,128)S(1)}) custom-call(bf16[144,512]{1,0:T(8,128)(2,1)S(1)} %concatenate.7.own.refs_0_, bf16[144,512]{1,0:T(8,128)(2,1)S(1)} %collective-permute-done.1.refs_1_, bf16[144,512]{1,0:T(8,128)(2,1)S(1)} %collective-permute-done.2.refs_2_, ...), custom_call_target="tpu_custom_call" | custom-call | flops 2000000000 | bytes 4194304 | tf_op jit(solution)/shard_map/first_part/pallas_call | solution.py:327
  29.2 1.0 %collective-permute-done.8.refs_7_ = bf16[144,512]{1,0:T(8,128)(2,1)S(1)} collective-permute-done((bf16[144,512]{1,0:T(8,128)(2,1)S(1)}, bf16[144,512]{1,0:T(8,128)(2,1)S(1)}, u32[]{:S(2)}, u32[]{:S(2)}) %collective-permute-start.8) | collective-permute-done | bytes 147488 | tf_op jit(solution)/shard_map/ppermute | solution.py:54
  30.3 2.3 %collective-permute-done.9.refs_11_ = bf16[3088,128]{1,0:T(8,128)(2,1)S(1)} collective-permute-done((bf16[3088,128]{1,0:T(8,128)(2,1)S(1)}, bf16[3088,128]{1,0:T(8,128)(2,1)S(1)}, u32[]{:S(2)}, u32[]{:S(2)}) %collective-permute-start.9) | collective-permute-done | bytes 790560 | tf_op jit(solution)/shard_map/ppermute | solution.py:36
  32.6 5.8 %second_part.1 = (f32[128,512]{1,0:T(8,128)S(1)}, f32[8,512]{1,0:T(8,128)S(1)}, bf16[288,512]{1,0:T(8,128)(2,1)S(1)}, bf16[288,512]{1,0:T(8,128)(2,1)S(1)}, bf16...) custom-call(bf16[144,512]{1,0:T(8,128)(2,1)S(1)} %concatenate.7.own.refs_0_, ...), custom_call_target="tpu_custom_call" | custom-call | flops 4000000000 | bytes 6291456 | tf_op jit(solution)/shard_map/second_part/pallas_call | solution.py:345
  38.7 3.0 %collective-permute-start.11 = (bf16[288,512]{1,0:T(8,128)(2,1)S(1)}, bf16[288,512]{1,0:T(8,128)(2,1)S(1)}, u32[]{:S(2)}, u32[]{:S(2)}) collective-permute-start(bf16[288,512]{1,0:T(8,128)(2,1)S(1)} %get-tuple-element.72), channel_id=1, source_target_pairs={{0,112},{8,120},{16,0},{24,8},{32,16},{40,24},{48,32},{56,40},{64,... | collective-permute-start | bytes 884744 | tf_op jit(solution)/shard_map/ppermute | solution.py:36
  42.2 2.2 %late.1.weight = bf16[4,512,1024]{2,1,0:T(8,128)(2,1)S(1)} custom-call(bf16[512,8192]{1,0:T(8,128)(2,1)} %weight.2), custom_call_target="tpu_custom_call" | custom-call | bytes 8388608 | tf_op jit(solution)/shard_map/late/pallas_call | solution.py:221
  44.4 7.3 %collective-permute-done.12.from_far = bf16[144,512]{1,0:T(8,128)(2,1)S(1)} collective-permute-done((bf16[144,512]{1,0:T(8,128)(2,1)S(1)}, bf16[144,512]{1,0:T(8,128)(2,1)S(1)}, u32[]{:S(2)}, u32[]{:S(2)}) %collective-permute-start.12) | collective-permute-done | bytes 147488 | tf_op jit(solution)/shard_map/ppermute | solution.py:54
  52.4 3.7 %collective-permute-start.14 = (bf16[144,512]{1,0:T(8,128)(2,1)S(1)}, bf16[144,512]{1,0:T(8,128)(2,1)S(1)}, u32[]{:S(2)}, u32[]{:S(2)}) collective-permute-start(bf16[144,512]{1,0:T(8,128)(2,1)S(1)} %get-tuple-element.79), channel_id=1, source_target_pairs={{0,96},{8,104},{16,112},{24,120},{32,0},{40,8},{48,16},{56,24},{64... | collective-permute-start | bytes 442376 | tf_op jit(solution)/shard_map/ppermute | solution.py:36
  56.1 6.0 %collective-permute-done.13.p2 = bf16[144,512]{1,0:T(8,128)(2,1)S(1)} collective-permute-done((bf16[144,512]{1,0:T(8,128)(2,1)S(1)}, bf16[144,512]{1,0:T(8,128)(2,1)S(1)}, u32[]{:S(2)}, u32[]{:S(2)}) %collective-permute-start.13) | collective-permute-done | bytes 147488 | tf_op jit(solution)/shard_map/ppermute | solution.py:36
  62.1 2.0 %collective-permute-done.14.m2 = bf16[144,512]{1,0:T(8,128)(2,1)S(1)} collective-permute-done((bf16[144,512]{1,0:T(8,128)(2,1)S(1)}, bf16[144,512]{1,0:T(8,128)(2,1)S(1)}, u32[]{:S(2)}, u32[]{:S(2)}) %collective-permute-start.14) | collective-permute-done | bytes 147488 | tf_op jit(solution)/shard_map/ppermute | solution.py:36
  64.1 0.9 away.1
  65.0 1.5 %collective-permute-start.18 = (bf16[128,1024]{1,0:T(8,128)(2,1)S(1)}, bf16[128,1024]{1,0:T(8,128)(2,1)S(1)}, u32[]{:S(2)}, u32[]{:S(2)}) collective-permute-start(bf16[128,1024]{1,0:T(8,128)(2,1)S(1)} %get-tuple-element.88), channel_id=1, source_target_pairs={{0,4},{1,5},{2,6},{3,7},{4,0},{5,1},{6,2},{7,3},{8,12},{9,13},{10,... | collective-permute-start | bytes 786440 | tf_op jit(solution)/shard_map/ppermute | solution.py:44
  66.4 2.1 %collective-permute-start.19 = (bf16[128,1024]{1,0:T(8,128)(2,1)S(1)}, bf16[128,1024]{1,0:T(8,128)(2,1)S(1)}, u32[]{:S(2)}, u32[]{:S(2)}) collective-permute-start(bf16[128,1024]{1,0:T(8,128)(2,1)S(1)} %get-tuple-element.89), channel_id=1, source_target_pairs={{0,2},{1,3},{2,4},{3,5},{4,6},{5,7},{6,0},{7,1},{8,10},{9,11},{10,... | collective-permute-start | bytes 786440 | tf_op jit(solution)/shard_map/ppermute | solution.py:44
  69.3 2.1 %collective-permute-start.15 = (bf16[128,1024]{1,0:T(8,128)(2,1)S(1)}, bf16[128,1024]{1,0:T(8,128)(2,1)S(1)}, u32[]{:S(2)}, u32[]{:S(2)}) collective-permute-start(bf16[128,1024]{1,0:T(8,128)(2,1)S(1)} %get-tuple-element.84), channel_id=1, source_target_pairs={{0,4},{1,5},{2,6},{3,7},{4,0},{5,1},{6,2},{7,3},{8,12},{9,13},{10,... | collective-permute-start | bytes 786440 | tf_op jit(solution)/shard_map/ppermute | solution.py:44
  71.4 1.3 %collective-permute-start.16 = (bf16[128,1024]{1,0:T(8,128)(2,1)S(1)}, bf16[128,1024]{1,0:T(8,128)(2,1)S(1)}, u32[]{:S(2)}, u32[]{:S(2)}) collective-permute-start(bf16[128,1024]{1,0:T(8,128)(2,1)S(1)} %get-tuple-element.85), channel_id=1, source_target_pairs={{0,2},{1,3},{2,4},{3,5},{4,6},{5,7},{6,0},{7,1},{8,10},{9,11},{10,... | collective-permute-start | bytes 786440 | tf_op jit(solution)/shard_map/ppermute | solution.py:44
  72.7 3.1 %collective-permute-done.18.refs_0_ = bf16[128,1024]{1,0:T(8,128)(2,1)S(1)} collective-permute-done((bf16[128,1024]{1,0:T(8,128)(2,1)S(1)}, bf16[128,1024]{1,0:T(8,128)(2,1)S(1)}, u32[]{:S(2)}, u32[]{:S(2)}) %collective-permute-start.18) | collective-permute-done | bytes 262176 | tf_op jit(solution)/shard_map/ppermute | solution.py:44
  76.6 3.8 %collective-permute-done.19.refs_1_ = bf16[128,1024]{1,0:T(8,128)(2,1)S(1)} collective-permute-done((bf16[128,1024]{1,0:T(8,128)(2,1)S(1)}, bf16[128,1024]{1,0:T(8,128)(2,1)S(1)}, u32[]{:S(2)}, u32[]{:S(2)}) %collective-permute-start.19) | collective-permute-done | bytes 262176 | tf_op jit(solution)/shard_map/ppermute | solution.py:44
  80.4 4.2 %collective-permute-done.20.refs_2_ = bf16[128,1024]{1,0:T(8,128)(2,1)S(1)} collective-permute-done((bf16[128,1024]{1,0:T(8,128)(2,1)S(1)}, bf16[128,1024]{1,0:T(8,128)(2,1)S(1)}, u32[]{:S(2)}, u32[]{:S(2)}) %collective-permute-start.20) | collective-permute-done | bytes 262176 | tf_op jit(solution)/shard_map/ppermute | solution.py:44
  84.8 3.0 %collective-permute-start.21 = (bf16[128,1024]{1,0:T(8,128)(2,1)S(1)}, bf16[128,1024]{1,0:T(8,128)(2,1)S(1)}, u32[]{:S(2)}, u32[]{:S(2)}) collective-permute-start(bf16[128,1024]{1,0:T(8,128)(2,1)S(1)} %pass_on.1), channel_id=1, source_target_pairs={{0,1},{1,0},{2,3},{3,2},{4,5},{5,4},{6,7},{7,6},{8,9},{9,8},{10,11... | collective-permute-start | bytes 786440 | tf_op jit(solution)/shard_map/ppermute | solution.py:44
  87.7 0.9 collective-permute-done.16.refs_1_
  88.6 2.2 %collective-permute-done.17.refs_2_ = bf16[128,1024]{1,0:T(8,128)(2,1)S(1)} collective-permute-done((bf16[128,1024]{1,0:T(8,128)(2,1)S(1)}, bf16[128,1024]{1,0:T(8,128)(2,1)S(1)}, u32[]{:S(2)}, u32[]{:S(2)}) %collective-permute-start.17) | collective-permute-done | bytes 262176 | tf_op jit(solution)/shard_map/ppermute | solution.py:44
  90.8 2.0 %collective-permute-done.21.refs_3_ = bf16[128,1024]{1,0:T(8,128)(2,1)S(1)} collective-permute-done((bf16[128,1024]{1,0:T(8,128)(2,1)S(1)}, bf16[128,1024]{1,0:T(8,128)(2,1)S(1)}, u32[]{:S(2)}, u32[]{:S(2)}) %collective-permute-start.21) | collective-permute-done | bytes 262176 | tf_op jit(solution)/shard_map/ppermute | solution.py:44
  (31 shorter events, 5.2 us)
Async XLA Ops:
  0.0 4.3 %copy-start.2 = (bf16[128,512]{1,0:T(8,128)(2,1)S(1)}, bf16[128,512]{1,0:T(8,128)(2,1)}, u32[]{:S(2)}) copy-start(bf16[128,512]{1,0:T(8,128)(2,1)} %param.9) | copy-start | bytes 393220
  0.0 14.8 %copy-start.1 = (bf16[128,128]{1,0:T(8,128)(2,1)S(1)}, bf16[128,128]{1,0:T(8,128)(2,1)}, u32[]{:S(2)}) copy-start(bf16[128,128]{1,0:T(8,128)(2,1)} %suffix_v.1) | copy-start | bytes 98308
  0.0 14.8 %copy-start = (bf16[128,128]{1,0:T(8,128)(2,1)S(1)}, bf16[128,128]{1,0:T(8,128)(2,1)}, u32[]{:S(2)}) copy-start(bf16[128,128]{1,0:T(8,128)(2,1)} %suffix_k.1) | copy-start | bytes 98308
  1.9 9.6 %collective-permute-start = (bf16[3088,128]{1,0:T(8,128)(2,1)S(1)}, bf16[3088,128]{1,0:T(8,128)(2,1)S(1)}, u32[]{:S(2)}, u32[]{:S(2)}) collective-permute-start(bf16[3088,128]{1,0:T(8,128)(2,1)S(1)} %fusion.1.refs_5_.refs_8_), channel_id=1, source_target_pairs={{0,8},{8,0},{16,24},{24,16},{32,40},{40,32},{48,56},{56,48},{64,72... | collective-permute-start | bytes 2371592 | tf_op jit(solution)/shard_map/ppermute | solution.py:36
  2.0 27.2 %collective-permute-start.5 = (bf16[3088,128]{1,0:T(8,128)(2,1)S(1)}, bf16[3088,128]{1,0:T(8,128)(2,1)S(1)}, u32[]{:S(2)}, u32[]{:S(2)}) collective-permute-start(bf16[3088,128]{1,0:T(8,128)(2,1)S(1)} %fusion.1.refs_5_.refs_8_), channel_id=1, source_target_pairs={{0,128},{8,136},{16,144},{24,152},{32,160},{40,168},{48,176},{56,1... | collective-permute-start | bytes 2371592 | tf_op jit(solution)/shard_map/ppermute | solution.py:36
  4.4 13.0 %collective-permute-start.4 = (bf16[144,512]{1,0:T(8,128)(2,1)S(1)}, bf16[144,512]{1,0:T(8,128)(2,1)S(1)}, u32[]{:S(2)}, u32[]{:S(2)}) collective-permute-start(bf16[144,512]{1,0:T(8,128)(2,1)S(1)} %concatenate.7.own.refs_0_), channel_id=1, source_target_pairs={{0,32},{8,40},{16,48},{24,56},{32,64},{40,72},{48,80},{56,88},{64,... | collective-permute-start | bytes 442376 | tf_op jit(solution)/shard_map/ppermute | solution.py:36
  7.7 12.0 %collective-permute-start.3 = (bf16[144,512]{1,0:T(8,128)(2,1)S(1)}, bf16[144,512]{1,0:T(8,128)(2,1)S(1)}, u32[]{:S(2)}, u32[]{:S(2)}) collective-permute-start(bf16[144,512]{1,0:T(8,128)(2,1)S(1)} %concatenate.7.own.refs_0_), channel_id=1, source_target_pairs={{0,96},{8,104},{16,112},{24,120},{32,0},{40,8},{48,16},{56,24},{64... | collective-permute-start | bytes 442376 | tf_op jit(solution)/shard_map/ppermute | solution.py:36
  11.5 10.3 %collective-permute-start.2 = (bf16[144,512]{1,0:T(8,128)(2,1)S(1)}, bf16[144,512]{1,0:T(8,128)(2,1)S(1)}, u32[]{:S(2)}, u32[]{:S(2)}) collective-permute-start(bf16[144,512]{1,0:T(8,128)(2,1)S(1)} %concatenate.7.own.refs_0_), channel_id=1, source_target_pairs={{0,16},{8,24},{16,32},{24,40},{32,48},{40,56},{48,64},{56,72},{64,... | collective-permute-start | bytes 442376 | tf_op jit(solution)/shard_map/ppermute | solution.py:36
  12.6 13.2 %collective-permute-start.1 = (bf16[144,512]{1,0:T(8,128)(2,1)S(1)}, bf16[144,512]{1,0:T(8,128)(2,1)S(1)}, u32[]{:S(2)}, u32[]{:S(2)}) collective-permute-start(bf16[144,512]{1,0:T(8,128)(2,1)S(1)} %concatenate.7.own.refs_0_), channel_id=1, source_target_pairs={{0,112},{8,120},{16,0},{24,8},{32,16},{40,24},{48,32},{56,40},{64,... | collective-permute-start | bytes 442376 | tf_op jit(solution)/shard_map/ppermute | solution.py:36
  19.8 10.5 %collective-permute-start.6 = (bf16[144,512]{1,0:T(8,128)(2,1)S(1)}, bf16[144,512]{1,0:T(8,128)(2,1)S(1)}, u32[]{:S(2)}, u32[]{:S(2)}) collective-permute-start(bf16[144,512]{1,0:T(8,128)(2,1)S(1)} %collective-permute-done.3.refs_3_), channel_id=1, source_target_pairs={{0,112},{8,120},{16,0},{24,8},{32,16},{40,24},{48,32},{56,40},{64,... | collective-permute-start | bytes 442376 | tf_op jit(solution)/shard_map/ppermute | solution.py:36
  21.5 8.7 %collective-permute-start.7 = (bf16[144,512]{1,0:T(8,128)(2,1)S(1)}, bf16[144,512]{1,0:T(8,128)(2,1)S(1)}, u32[]{:S(2)}, u32[]{:S(2)}) collective-permute-start(bf16[144,512]{1,0:T(8,128)(2,1)S(1)} %collective-permute-done.4.refs_4_), channel_id=1, source_target_pairs={{0,16},{8,24},{16,32},{24,40},{32,48},{40,56},{48,64},{56,72},{64,... | collective-permute-start | bytes 442376 | tf_op jit(solution)/shard_map/ppermute | solution.py:36
  21.8 8.4 %collective-permute-start.8 = (bf16[144,512]{1,0:T(8,128)(2,1)S(1)}, bf16[144,512]{1,0:T(8,128)(2,1)S(1)}, u32[]{:S(2)}, u32[]{:S(2)}) collective-permute-start(bf16[144,512]{1,0:T(8,128)(2,1)S(1)} %broadcast_select_fusion), channel_id=1, source_target_pairs={{0,32},{8,40},{16,112},{24,120},{32,64},{40,72},{48,16},{56,24},{6... | collective-permute-start | bytes 442376 | tf_op jit(solution)/shard_map/ppermute | solution.py:54
  30.3 2.3 %collective-permute-start.9 = (bf16[3088,128]{1,0:T(8,128)(2,1)S(1)}, bf16[3088,128]{1,0:T(8,128)(2,1)S(1)}, u32[]{:S(2)}, u32[]{:S(2)}) collective-permute-start(bf16[3088,128]{1,0:T(8,128)(2,1)S(1)} %collective-permute-done.5.refs_10_), channel_id=1, source_target_pairs={{0,8},{8,0},{16,24},{24,16},{32,40},{40,32},{48,56},{56,48},{64,72... | collective-permute-start | bytes 2371592 | tf_op jit(solution)/shard_map/ppermute | solution.py:36
  38.4 13.3 %collective-permute-start.10 = (bf16[288,512]{1,0:T(8,128)(2,1)S(1)}, bf16[288,512]{1,0:T(8,128)(2,1)S(1)}, u32[]{:S(2)}, u32[]{:S(2)}) collective-permute-start(bf16[288,512]{1,0:T(8,128)(2,1)S(1)} %get-tuple-element.71), channel_id=1, source_target_pairs={{0,16},{8,24},{16,32},{24,40},{32,48},{40,56},{48,64},{56,72},{64,... | collective-permute-start | bytes 884744 | tf_op jit(solution)/shard_map/ppermute | solution.py:36
  38.7 13.0 %collective-permute-start.11 = (bf16[288,512]{1,0:T(8,128)(2,1)S(1)}, bf16[288,512]{1,0:T(8,128)(2,1)S(1)}, u32[]{:S(2)}, u32[]{:S(2)}) collective-permute-start(bf16[288,512]{1,0:T(8,128)(2,1)S(1)} %get-tuple-element.72), channel_id=1, source_target_pairs={{0,112},{8,120},{16,0},{24,8},{32,16},{40,24},{48,32},{56,40},{64,... | collective-permute-start | bytes 884744 | tf_op jit(solution)/shard_map/ppermute | solution.py:36
  41.7 10.0 %collective-permute-start.12 = (bf16[144,512]{1,0:T(8,128)(2,1)S(1)}, bf16[144,512]{1,0:T(8,128)(2,1)S(1)}, u32[]{:S(2)}, u32[]{:S(2)}) collective-permute-start(bf16[144,512]{1,0:T(8,128)(2,1)S(1)} %get-tuple-element.75), channel_id=1, source_target_pairs={{0,32},{8,40},{16,112},{24,120},{32,64},{40,72},{48,16},{56,24},{6... | collective-permute-start | bytes 442376 | tf_op jit(solution)/shard_map/ppermute | solution.py:54
  51.9 10.2 %collective-permute-start.13 = (bf16[144,512]{1,0:T(8,128)(2,1)S(1)}, bf16[144,512]{1,0:T(8,128)(2,1)S(1)}, u32[]{:S(2)}, u32[]{:S(2)}) collective-permute-start(bf16[144,512]{1,0:T(8,128)(2,1)S(1)} %get-tuple-element.78), channel_id=1, source_target_pairs={{0,32},{8,40},{16,48},{24,56},{32,64},{40,72},{48,80},{56,88},{64,... | collective-permute-start | bytes 442376 | tf_op jit(solution)/shard_map/ppermute | solution.py:36
  52.4 11.6 %collective-permute-start.14 = (bf16[144,512]{1,0:T(8,128)(2,1)S(1)}, bf16[144,512]{1,0:T(8,128)(2,1)S(1)}, u32[]{:S(2)}, u32[]{:S(2)}) collective-permute-start(bf16[144,512]{1,0:T(8,128)(2,1)S(1)} %get-tuple-element.79), channel_id=1, source_target_pairs={{0,96},{8,104},{16,112},{24,120},{32,0},{40,8},{48,16},{56,24},{64... | collective-permute-start | bytes 442376 | tf_op jit(solution)/shard_map/ppermute | solution.py:36
  65.0 10.8 %collective-permute-start.18 = (bf16[128,1024]{1,0:T(8,128)(2,1)S(1)}, bf16[128,1024]{1,0:T(8,128)(2,1)S(1)}, u32[]{:S(2)}, u32[]{:S(2)}) collective-permute-start(bf16[128,1024]{1,0:T(8,128)(2,1)S(1)} %get-tuple-element.88), channel_id=1, source_target_pairs={{0,4},{1,5},{2,6},{3,7},{4,0},{5,1},{6,2},{7,3},{8,12},{9,13},{10,... | collective-permute-start | bytes 786440 | tf_op jit(solution)/shard_map/ppermute | solution.py:44
  66.4 14.0 %collective-permute-start.19 = (bf16[128,1024]{1,0:T(8,128)(2,1)S(1)}, bf16[128,1024]{1,0:T(8,128)(2,1)S(1)}, u32[]{:S(2)}, u32[]{:S(2)}) collective-permute-start(bf16[128,1024]{1,0:T(8,128)(2,1)S(1)} %get-tuple-element.89), channel_id=1, source_target_pairs={{0,2},{1,3},{2,4},{3,5},{4,6},{5,7},{6,0},{7,1},{8,10},{9,11},{10,... | collective-permute-start | bytes 786440 | tf_op jit(solution)/shard_map/ppermute | solution.py:44
  68.5 16.1 %collective-permute-start.20 = (bf16[128,1024]{1,0:T(8,128)(2,1)S(1)}, bf16[128,1024]{1,0:T(8,128)(2,1)S(1)}, u32[]{:S(2)}, u32[]{:S(2)}) collective-permute-start(bf16[128,1024]{1,0:T(8,128)(2,1)S(1)} %get-tuple-element.90), channel_id=1, source_target_pairs={{0,6},{1,7},{2,0},{3,1},{4,2},{5,3},{6,4},{7,5},{8,14},{9,15},{10,... | collective-permute-start | bytes 786440 | tf_op jit(solution)/shard_map/ppermute | solution.py:44
  69.3 18.5 %collective-permute-start.15 = (bf16[128,1024]{1,0:T(8,128)(2,1)S(1)}, bf16[128,1024]{1,0:T(8,128)(2,1)S(1)}, u32[]{:S(2)}, u32[]{:S(2)}) collective-permute-start(bf16[128,1024]{1,0:T(8,128)(2,1)S(1)} %get-tuple-element.84), channel_id=1, source_target_pairs={{0,4},{1,5},{2,6},{3,7},{4,0},{5,1},{6,2},{7,3},{8,12},{9,13},{10,... | collective-permute-start | bytes 786440 | tf_op jit(solution)/shard_map/ppermute | solution.py:44
  71.4 17.2 %collective-permute-start.16 = (bf16[128,1024]{1,0:T(8,128)(2,1)S(1)}, bf16[128,1024]{1,0:T(8,128)(2,1)S(1)}, u32[]{:S(2)}, u32[]{:S(2)}) collective-permute-start(bf16[128,1024]{1,0:T(8,128)(2,1)S(1)} %get-tuple-element.85), channel_id=1, source_target_pairs={{0,2},{1,3},{2,4},{3,5},{4,6},{5,7},{6,0},{7,1},{8,10},{9,11},{10,... | collective-permute-start | bytes 786440 | tf_op jit(solution)/shard_map/ppermute | solution.py:44
  75.8 15.0 %collective-permute-start.17 = (bf16[128,1024]{1,0:T(8,128)(2,1)S(1)}, bf16[128,1024]{1,0:T(8,128)(2,1)S(1)}, u32[]{:S(2)}, u32[]{:S(2)}) collective-permute-start(bf16[128,1024]{1,0:T(8,128)(2,1)S(1)} %get-tuple-element.86), channel_id=1, source_target_pairs={{0,6},{1,7},{2,0},{3,1},{4,2},{5,3},{6,4},{7,5},{8,14},{9,15},{10,... | collective-permute-start | bytes 786440 | tf_op jit(solution)/shard_map/ppermute | solution.py:44
  84.8 8.0 %collective-permute-start.21 = (bf16[128,1024]{1,0:T(8,128)(2,1)S(1)}, bf16[128,1024]{1,0:T(8,128)(2,1)S(1)}, u32[]{:S(2)}, u32[]{:S(2)}) collective-permute-start(bf16[128,1024]{1,0:T(8,128)(2,1)S(1)} %pass_on.1), channel_id=1, source_target_pairs={{0,1},{1,0},{2,3},{3,2},{4,5},{5,4},{6,7},{7,6},{8,9},{9,8},{10,11... | collective-permute-start | bytes 786440 | tf_op jit(solution)/shard_map/ppermute | solution.py:44

commit v3 on v2

--- a/solution.py
+++ b/solution.py
@@ -1,3 +1,4 @@
+import functools
 import math
 
 import jax
@@ -161,12 +162,12 @@
     sums[b] = sums[b] * keep + summed * take
 
 
-def column_copies(weight, out, sem, other_w):
+def column_copies(weight, out, sem, other_w, steps):
     x = lax.shift_right_logical(lax.axis_index("heads"), 1)
     w = lax.bitwise_xor(lax.bitwise_and(lax.axis_index("heads"), 1), other_w)
     width = out.shape[2]
     copies = []
-    for j, dx in enumerate(STEPS):
+    for j, dx in enumerate(steps):
         column = lax.bitwise_and(x + dx, NX - 1) * NW + w
         columns = pl.ds(pl.multiple_of(column * width, width), width)
         copies.append(pltpu.make_async_copy(weight.at[:, columns], out.at[j], sem.at[j]))
@@ -175,8 +176,11 @@
     return copies
 
 
-def early_kernel(length, own, suffix_k, suffix_v, weight, peak, total, summed, far_w, sem):
-    copies = column_copies(weight, far_w, sem, 1)
+def early_kernel(
+    length, own, suffix_k, suffix_v, weight, peak, total, summed, far_w, home_w, sem, home_sem
+):
+    copies = column_copies(weight, far_w, sem, 1, STEPS)
+    copies += column_copies(weight, home_w, home_sem, 0, STEPS[:-1])
     rows = jnp.concatenate([own[0:BLK, h * HD : (h + 1) * HD] for h in range(QPG)], axis=0)
     key_at = lax.broadcasted_iota(jnp.int32, (BLK, ROWS), 0)
     row_at = lax.bitwise_and(lax.broadcasted_iota(jnp.int32, (BLK, ROWS), 1), BLK - 1)
@@ -188,8 +192,9 @@
         copy.wait()
 
 
-def laid_out(weight):
-    return jax.ShapeDtypeStruct((NX, weight.shape[0], weight.shape[1] // (NX * NW)), BF16)
+def laid_out(weight, steps):
+    shape = (len(steps), weight.shape[0], weight.shape[1] // (NX * NW))
+    return jax.ShapeDtypeStruct(shape, BF16)
 
 
 def early(length, own, suffix_k, suffix_v, weight):
@@ -199,11 +204,15 @@
             jax.ShapeDtypeStruct((1, ROWS), F32),
             jax.ShapeDtypeStruct((1, ROWS), F32),
             jax.ShapeDtypeStruct((HD, ROWS), F32),
-            laid_out(weight),
+            laid_out(weight, STEPS),
+            laid_out(weight, STEPS[:-1]),
         ],
         in_specs=[SMEM] + [VMEM] * 3 + [HBM],
-        out_specs=[VMEM] * 4,
-        scratch_shapes=[pltpu.SemaphoreType.DMA((NX,))],
+        out_specs=[VMEM] * 5,
+        scratch_shapes=[
+            pltpu.SemaphoreType.DMA((len(STEPS),)),
+            pltpu.SemaphoreType.DMA((len(STEPS) - 1,)),
+        ],
         compiler_params=pltpu.CompilerParams(vmem_limit_bytes=46 << 20),
         cost_estimate=pl.CostEstimate(
             flops=40_000_000, bytes_accessed=9 << 20, transcendentals=70_000
@@ -212,21 +221,21 @@
     )(length, own, suffix_k, suffix_v, weight)
 
 
-def late_kernel(weight, home_w, sem):
-    for copy in column_copies(weight, home_w, sem, 0):
+def late_kernel(steps, weight, home_w, sem):
+    for copy in column_copies(weight, home_w, sem, 0, steps):
         copy.wait()
 
 
-def late(weight):
-    return pl.pallas_call(
-        late_kernel,
-        out_shape=laid_out(weight),
+def late(name, weight, steps):
+    return pl.pallas_call(
+        functools.partial(late_kernel, steps),
+        out_shape=laid_out(weight, steps),
         in_specs=[HBM],
         out_specs=VMEM,
-        scratch_shapes=[pltpu.SemaphoreType.DMA((NX,))],
+        scratch_shapes=[pltpu.SemaphoreType.DMA((len(steps),))],
         compiler_params=pltpu.CompilerParams(vmem_limit_bytes=46 << 20),
         cost_estimate=pl.CostEstimate(flops=0, bytes_accessed=8 << 20, transcendentals=0),
-        name="late",
+        name=name,
     )(weight)
 
 
@@ -267,37 +276,61 @@
     return pieces[0:1] + pieces[1:2] + pieces[2:3]
 
 
-def second_kernel(*refs):
-    nq = len(OFFSETS)
-    packed, sources, known = refs[0:nq], refs[nq : nq + 4], refs[nq + 4 : nq + 7]
-    own_out, own_lse, p_out, m_out, far_out, ahead_out, back_out = refs[nq + 7 : nq + 14]
-    todo, vis_s, vis_v, qbuf, ahead, peaks, totals, sums, qsem, vsem = refs[nq + 14 :]
-    state = (peaks, totals, sums)
+def solve(wanted, packed, sources, scratch):
+    todo, vis_s, vis_v, qbuf, ahead, peaks, totals, sums, qsem, vsem = scratch
+    nq, state = len(packed), (peaks, totals, sums)
     copies = fetch(packed, qbuf, qsem)
-    wanted = [(b, s) for b in range(NEAR, nq) for s in range(4)]
-    wanted += [(b, s) for b in range(NEAR) for s in (2, 3)]
     count = list_items(wanted, packed, sources, vis_v, vis_s, todo, nq, vsem)
     clear(state, range(nq + 1))
     for copy in copies:
         copy.wait()
     work(count, todo, nq, qbuf, sources, state, ahead)
-    places = {1: (p_out, 0), 5: (p_out, PAYLOAD), 2: (m_out, 0), 6: (m_out, PAYLOAD)}
-    places |= {7: (far_out, 0), 3: (ahead_out, 0), 4: (back_out, 0)}
-    for b in (5, 6, 7, 1, 2, 3, 4, 0):
-        if b < NEAR:
-            merge(state, b, known[0][b], known[1][b], known[2][b])
-        total = totals[b]
-        seen = total > 0.0
-        safe = jnp.where(seen, total, 1.0)
-        lse = jnp.where(seen, peaks[b] * SCALE2 + jnp.log2(safe), EMPTY)
-        out = sums[b] * (1.0 / safe)
+    return state
+
+
+def outcome(state, b):
+    peaks, totals, sums = state
+    total = totals[b]
+    seen = total > 0.0
+    safe = jnp.where(seen, total, 1.0)
+    lse = jnp.where(seen, peaks[b] * SCALE2 + jnp.log2(safe), EMPTY)
+    return sums[b] * (1.0 / safe), lse
+
+
+def write_payload(state, b, ref):
+    out, lse = outcome(state, b)
+    ref[0:BLK, :] = out.astype(BF16)
+    ref[BLK:PAYLOAD, :] = lse_rows(lse)
+
+
+def far_kernel(*refs):
+    packed, sources, state, scratch = refs[0:3], refs[3:6], refs[6:9], refs[9:]
+    wanted = [(b, s) for b in range(3) for s in range(3)]
+    solve(wanted, packed, sources, (*scratch[0:5], *state, *scratch[5:]))
+
+
+def last_kernel(*refs):
+    packed, sources, known, outs, scratch = refs[0:3], refs[3:4], refs[4:7], refs[7:10], refs[10:]
+    state = solve([(b, 0) for b in range(3)], packed, sources, scratch)
+    for b, ref in enumerate(outs):
+        merge(state, b, known[0][b], known[1][b], known[2][b])
+        write_payload(state, b, ref)
+
+
+def near_kernel(*refs):
+    packed, sources = refs[0:NEAR], refs[NEAR : NEAR + 2]
+    known, outs = refs[NEAR + 2 : NEAR + 5], refs[NEAR + 5 : 2 * NEAR + 6]
+    state = solve(
+        [(b, s) for b in range(NEAR) for s in range(2)], packed, sources, refs[2 * NEAR + 6 :]
+    )
+    for b in range(NEAR):
+        merge(state, b, known[0][b], known[1][b], known[2][b])
         if b == 0:
-            own_out[...] = out
-            own_lse[...] = jnp.broadcast_to(lse, own_lse.shape)
+            out, lse = outcome(state, b)
+            outs[0][...] = out
+            outs[1][...] = jnp.broadcast_to(lse, outs[1].shape)
         else:
-            ref, at = places[b]
-            ref[at : at + BLK, :] = out.astype(BF16)
-            ref[at + BLK : at + PAYLOAD, :] = lse_rows(lse)
+            write_payload(state, b, outs[b + 1])
 
 
 SMEM = pl.BlockSpec(memory_space=pltpu.SMEM)
@@ -338,37 +371,45 @@
     )(*packed, *sources, *suffix)
 
 
-def second_part(packed, sources, known):
-    nq = len(OFFSETS)
-    payload = jax.ShapeDtypeStruct((PAYLOAD, ROWS), BF16)
-    double = jax.ShapeDtypeStruct((2 * PAYLOAD, ROWS), BF16)
-    return pl.pallas_call(
-        second_kernel,
-        out_shape=[
-            jax.ShapeDtypeStruct((HD, ROWS), F32),
-            jax.ShapeDtypeStruct((8, ROWS), F32),
-            double,
-            double,
-            payload,
-            payload,
-            payload,
-        ],
-        in_specs=[VMEM] * (nq + 7),
-        out_specs=[VMEM] * 7,
-        scratch_shapes=buffers(nq)
-        + [pltpu.VMEM(s, F32) for s in state_shapes(nq + 1)]
-        + semaphores(nq),
-        compiler_params=pltpu.CompilerParams(vmem_limit_bytes=16 << 20),
+def solved(kernel, name, packed, sources, known, outs, flops, own_state):
+    nq = len(packed)
+    scratch = buffers(nq) + semaphores(nq)
+    if own_state:
+        scratch[5:5] = [pltpu.VMEM(s, F32) for s in state_shapes(nq + 1)]
+    return pl.pallas_call(
+        kernel,
+        out_shape=outs,
+        in_specs=[VMEM] * (nq + len(sources) + len(known)),
+        out_specs=[VMEM] * len(outs),
+        scratch_shapes=scratch,
+        compiler_params=pltpu.CompilerParams(vmem_limit_bytes=14 << 20),
         cost_estimate=pl.CostEstimate(
-            flops=4_000_000_000, bytes_accessed=6 << 20, transcendentals=3_000_000
-        ),
-        name="second_part",
+            flops=flops, bytes_accessed=4 << 20, transcendentals=2_000_000
+        ),
+        name=name,
     )(*packed, *sources, *known)
+
+
+def far_part(packed, sources):
+    outs = [jax.ShapeDtypeStruct(s, F32) for s in state_shapes(len(packed) + 1)]
+    return solved(far_kernel, "far_part", packed, sources, [], outs, 20_000_000_000, False)
+
+
+def last_part(packed, sources, known):
+    outs = [jax.ShapeDtypeStruct((PAYLOAD, ROWS), BF16)] * len(packed)
+    return solved(last_kernel, "last_part", packed, sources, known, outs, 1_500_000_000, True)
+
+
+def near_part(packed, sources, known):
+    outs = [jax.ShapeDtypeStruct((HD, ROWS), F32), jax.ShapeDtypeStruct((8, ROWS), F32)]
+    outs += [jax.ShapeDtypeStruct((PAYLOAD, ROWS), BF16)] * (len(packed) - 1)
+    return solved(
+        near_kernel, "near_part", packed, sources, known, outs, 2_500_000_000, True
+    )
 
 
 def join_kernel(ahead, back, from_ahead, from_back, from_far, ahead_out, back_out):
     odd = lax.bitwise_and(lax.shift_right_logical(lax.axis_index("cache"), 1), 1)
-    from_ahead, from_back = from_ahead.at[PAYLOAD:], from_back.at[PAYLOAD:]
     for own, other, out, far_here in (
         (ahead, from_back, ahead_out, odd == 0),
         (back, from_ahead, back_out, odd == 1),
@@ -417,13 +458,13 @@
     return mixed
 
 
-def project(rows, weight, outs):
+def project(rows, weights, outs):
     tile = 256
-    for j, out in enumerate(outs):
-        for t in range(weight.shape[2] // tile):
+    for weight, out in zip(weights, outs):
+        for t in range(weight.shape[1] // tile):
             columns = slice(t * tile, (t + 1) * tile)
             out[:, columns] = jnp.dot(
-                rows, weight[j, :, columns], preferred_element_type=F32
+                rows, weight[:, columns], preferred_element_type=F32
             ).astype(out.dtype)
 
 
@@ -432,26 +473,28 @@
     for h in range(QPG):
         columns = slice(h * BLK, (h + 1) * BLK)
         rows_out[:, columns] = mixed[:, columns].T.astype(BF16)
-    project(rows_out[...], weight, outs)
-
-
-def home_kernel(rows, weight, *outs):
-    project(rows[...], weight, outs)
-
-
-def projected(kernel, name, operands, weight, more):
+    project(rows_out[...], [weight.at[j] for j in range(len(outs))], outs)
+
+
+def home_kernel(rows, weight, own_weight, *outs):
+    weights = [weight.at[j] for j in range(len(outs) - 1)] + [own_weight.at[0]]
+    project(rows[...], weights, outs)
+
+
+def projected(kernel, name, operands, more):
+    width = operands[-1].shape[2]
     return pl.pallas_call(
         kernel,
         out_shape=more
-        + [jax.ShapeDtypeStruct((BLK, weight.shape[2]), F32 if dx == 0 else BF16) for dx in STEPS],
-        in_specs=[VMEM] * (len(operands) + 1),
-        out_specs=[VMEM] * (len(more) + NX),
+        + [jax.ShapeDtypeStruct((BLK, width), F32 if dx == 0 else BF16) for dx in STEPS],
+        in_specs=[VMEM] * len(operands),
+        out_specs=[VMEM] * (len(more) + len(STEPS)),
         compiler_params=pltpu.CompilerParams(vmem_limit_bytes=12 << 20),
         cost_estimate=pl.CostEstimate(
             flops=550_000_000, bytes_accessed=5 << 20, transcendentals=4096
         ),
         name=name,
-    )(*operands, weight)
+    )(*operands)
 
 
 def add_kernel(first, *refs):
@@ -498,32 +541,35 @@
     near = cache_step(source, 0, 0, 1)
     near, own = lax.optimization_barrier((near, own))
     p1, m1 = cache_step(own, 0, -1, 0), cache_step(own, 0, 1, 0)
-    *suffix, far_w = early(suffix_len, own, suffix_keys, suffix_values, out_weight)
+    *suffix, far_w, home_w = early(suffix_len, own, suffix_keys, suffix_values, out_weight)
     p2, m2, *suffix = lax.optimization_barrier((p2, m2, *suffix))
     p3, m3 = cache_step(p2, 0, -1, 0), cache_step(m2, 0, 1, 0)
     p4 = z_ways(jnp.where(lax.bitwise_and(z, 1) == 0, m2, p2), 2, -2)
     known = first_part([own, p1, m1, p2, m2], [source, near], suffix)
-    across, p3, m3, p4, *known = lax.optimization_barrier((across, p3, m3, p4, *known))
+    across, *known = lax.optimization_barrier((across, *known))
     far = cache_step(across, 0, 0, 1)
-    own_out, own_lse, o_p, o_m, o_far, o_p2, o_m2 = second_part(
-        [own, p1, m1, p2, m2, p3, m3, p4], [source, near, across, far], known
+    far_known = far_part([p3, m3, p4], [source, near, across])
+    o_p3, o_m3, o_p4 = last_part([p3, m3, p4], [far], far_known)
+    from_far = z_ways(o_p4, 2, -2)
+    from_back, from_ahead = cache_step(o_p3, 0, 1, 0), cache_step(o_m3, 0, -1, 0)
+    o_p4, *known = lax.optimization_barrier((o_p4, *known))
+    own_out, own_lse, o_p1, o_m1, o_p2, o_m2 = near_part(
+        [own, p1, m1, p2, m2], [across, far], known
     )
-    from_far = z_ways(o_far, 2, -2)
-    later_weight, own_lse = lax.optimization_barrier((out_weight, own_lse))
-    home_w = late(later_weight)
-    from_back, from_ahead = cache_step(o_p, 0, 1, 0), cache_step(o_m, 0, -1, 0)
-    from_far, home_w = lax.optimization_barrier((from_far, home_w))
+    r_p1, r_m1 = cache_step(o_p1, 0, 1, 0), cache_step(o_m1, 0, -1, 0)
+    near_weight, own_lse = lax.optimization_barrier((out_weight, own_lse))
+    own_w = late("late_own", near_weight, STEPS[-1:])
+    from_far, own_w = lax.optimization_barrier((from_far, own_w))
     ahead, back = join(o_p2, o_m2, from_ahead, from_back, from_far)
     r_p2, r_m2 = cache_step(ahead, 0, 2, 0), cache_step(back, 0, -2, 0)
     merged, *shares = projected(
         away_kernel,
         "away",
-        [own_out, own_lse, from_back, from_ahead, r_p2, r_m2],
-        far_w,
+        [own_out, own_lse, r_p1, r_m1, r_p2, r_m2, far_w],
         [jax.ShapeDtypeStruct((BLK, ROWS), BF16)],
     )
     arrived = [heads_step(share, dx, 0) for share, dx in zip(shares[:-1], STEPS)]
-    kept = projected(home_kernel, "home", [merged], home_w, [])
+    kept = projected(home_kernel, "home", [merged, home_w, own_w], [])
     passed = heads_step(sum_of("pass_on", shares[-1], arrived), 0, 1)
     arrived = [heads_step(share, dx, 0) for share, dx in zip(kept[:-1], STEPS)]
     return sum_of("finish", kept[-1], [*arrived, passed])

time: 93.9 us -> 87.4 us (0.931); the launches traced: 93.6 us -> 86 us
  waiting for transfers between devices: 37.1 us -> 24 us
  starting transfers between devices: 36.3 us -> 40.4 us
  Pallas kernels: 16.7 us -> 18.1 us
    ppermute x2, waiting for transfers between devices: 8.3 us -> 2.11 us  [z_ways(): return lax.ppermute(x, 'cache', pairs)]
    ppermute x7, waiting for transfers between devices: 16.1 us -> 12.3 us  [heads_step(): return lax.ppermute(x, 'heads', pairs)]
    ppermute x13 -> x15, starting transfers between devices: 21.1 us -> 24.5 us  [cache_step(): return lax.ppermute(x, 'cache', pairs)]
    ppermute x13 -> x15, waiting for transfers between devices: 12.7 us -> 9.6 us  [cache_step(): return lax.ppermute(x, 'cache', pairs)]
    pallas_call x4 -> x6, Pallas kernels: 9.64 us -> 11.2 us  [the longest x3 8.3 us: solved(): pl.pallas_call(kernel, out_shape=outs, in_specs=[VMEM] * (nq + len(source...]
    pallas_call x1, Pallas kernels: 3.41 us -> 2.25 us  [first_part(): pl.pallas_call(first_kernel, out_shape=[jax.ShapeDtypeStruct(s, F32) for...]
    pallas_call x1, Pallas kernels: 2.5 us -> 3.47 us  [early(): pl.pallas_call(early_kernel, out_shape=[jax.ShapeDtypeStruct((1, ROWS), F...]
  transfers between devices with their start and end apart: 22 -> 24, of which waited for: 12 -> 10; matrix products, arithmetic and copies ran while one was open for 0% -> 0% of each run, Pallas kernels for 10% -> 16%
where the time goes in v3:
time: 87.4 us; the launch traced here: 86 us
  starting transfers between devices  40.4 us (46%)
  waiting for transfers between devices  24 us (27%)
  Pallas kernels  18.1 us (21%)
  other arithmetic  1.92 us (2%)
  between operations  1.51 us (2%)
    ppermute x15, starting transfers between devices, cache_step(): return lax.ppermute(x, 'cache', pairs)  24.5 us
    ppermute x7, waiting for transfers between devices, heads_step(): return lax.ppermute(x, 'heads', pairs)  12.3 us
    ppermute x7, starting transfers between devices, heads_step(): return lax.ppermute(x, 'heads', pairs)  10.8 us
    ppermute x15, waiting for transfers between devices, cache_step(): return lax.ppermute(x, 'cache', pairs)  9.6 us
    pallas_call x3, Pallas kernels, solved(): pl.pallas_call(kernel, out_shape=outs, in_specs=[VMEM] * (nq + len(source...  8.3 us
    ppermute x2, starting transfers between devices, z_ways(): return lax.ppermute(x, 'cache', pairs)  5.18 us
    pallas_call x1, Pallas kernels, early(): pl.pallas_call(early_kernel, out_shape=[jax.ShapeDtypeStruct((1, ROWS), F...  3.47 us
    pallas_call x1, Pallas kernels, first_part(): pl.pallas_call(first_kernel, out_shape=[jax.ShapeDtypeStruct(s, F32) for...  2.25 us
  transfers between devices with their start and end apart: 24, of which 10 were waited for; matrix products, arithmetic and copies ran while one was open for 0% of the time, Pallas kernels for 16%

profile of v3, /device:TPU:6, one launch (start us, length us, event | category | flops | bytes accessed | tf_op | source)
XLA Modules:
  0.0 86.0 jit_solution(18267087222834042985)
XLA Ops:
  0.7 1.2 %fusion.1.refs_5_.refs_3_ = bf16[3088,128]{1,0:T(8,128)(2,1)S(1)} fusion(bf16[12,64]{1,0:T(8,128)(2,1)S(1)} %convert_bitcast_fusion, bf16[1536,128]{1,0:T(8,128)(2,1)} %param.11, bf16[1536,128]{1,0:T(8,128)(2,1)} %param.10), kind=kLoop, calls=%fused_computation.2 | loop fusion | flops 3162112 | bytes 1578496 | tf_op jit(solution)/shard_map/concatenate | solution.py:538
  2.0 1.7 %collective-permute-start.5 = (bf16[3088,128]{1,0:T(8,128)(2,1)S(1)}, bf16[3088,128]{1,0:T(8,128)(2,1)S(1)}, u32[]{:S(2)}, u32[]{:S(2)}) collective-permute-start(bf16[3088,128]{1,0:T(8,128)(2,1)S(1)} %fusion.1.refs_5_.refs_3_), channel_id=1, source_target_pairs={{0,128},{8,136},{16,144},{24,152},{32,160},{40,168},{48,176},{56,1... | collective-permute-start | bytes 2371592 | tf_op jit(solution)/shard_map/ppermute | solution.py:37
  4.4 3.3 %collective-permute-start.4 = (bf16[144,512]{1,0:T(8,128)(2,1)S(1)}, bf16[144,512]{1,0:T(8,128)(2,1)S(1)}, u32[]{:S(2)}, u32[]{:S(2)}) collective-permute-start(bf16[144,512]{1,0:T(8,128)(2,1)S(1)} %concatenate.7.own.refs_0_), channel_id=1, source_target_pairs={{0,32},{8,40},{16,48},{24,56},{32,64},{40,72},{48,80},{56,88},{64,... | collective-permute-start | bytes 442376 | tf_op jit(solution)/shard_map/ppermute | solution.py:37
  7.7 3.1 %collective-permute-start.3 = (bf16[144,512]{1,0:T(8,128)(2,1)S(1)}, bf16[144,512]{1,0:T(8,128)(2,1)S(1)}, u32[]{:S(2)}, u32[]{:S(2)}) collective-permute-start(bf16[144,512]{1,0:T(8,128)(2,1)S(1)} %concatenate.7.own.refs_0_), channel_id=1, source_target_pairs={{0,96},{8,104},{16,112},{24,120},{32,0},{40,8},{48,16},{56,24},{64... | collective-permute-start | bytes 442376 | tf_op jit(solution)/shard_map/ppermute | solution.py:37
  11.5 1.1 %collective-permute-start.2 = (bf16[144,512]{1,0:T(8,128)(2,1)S(1)}, bf16[144,512]{1,0:T(8,128)(2,1)S(1)}, u32[]{:S(2)}, u32[]{:S(2)}) collective-permute-start(bf16[144,512]{1,0:T(8,128)(2,1)S(1)} %concatenate.7.own.refs_0_), channel_id=1, source_target_pairs={{0,16},{8,24},{16,32},{24,40},{32,48},{40,56},{48,64},{56,72},{64,... | collective-permute-start | bytes 442376 | tf_op jit(solution)/shard_map/ppermute | solution.py:37
  12.6 2.2 %collective-permute-start.1 = (bf16[144,512]{1,0:T(8,128)(2,1)S(1)}, bf16[144,512]{1,0:T(8,128)(2,1)S(1)}, u32[]{:S(2)}, u32[]{:S(2)}) collective-permute-start(bf16[144,512]{1,0:T(8,128)(2,1)S(1)} %concatenate.7.own.refs_0_), channel_id=1, source_target_pairs={{0,112},{8,120},{16,0},{24,8},{32,16},{40,24},{48,32},{56,40},{64,... | collective-permute-start | bytes 442376 | tf_op jit(solution)/shard_map/ppermute | solution.py:37
  14.8 3.5 %early.1 = (f32[1,512]{1,0:T(1,128)S(1)}, f32[1,512]{1,0:T(1,128)S(1)}, f32[128,512]{1,0:T(8,128)S(1)}, bf16[4,512,1024]{2,1,0:T(8,128)(2,1)S(1)}, bf16[3,512,1024]{2,1,0:T(8,128)(2,1)S(1)}) custom-call(s32[1]{0:T(128)S(6)} %copy.11.length, bf16[144,512]{1,0:T(8,128)(2,1)S(1)} %concatenate.7.own.refs_0_, bf16[128,128]{1,0:T(8,128)(2,1)S(1)} %copy-done, ...), custom_call_target="tpu_custom_call" | custom-call | flops 40000000 | bytes 9437184 | tf_op jit(solution)/shard_map/early/pallas_call | solution.py:201
  18.3 1.4 %collective-permute-done.3.refs_3_ = bf16[144,512]{1,0:T(8,128)(2,1)S(1)} collective-permute-done((bf16[144,512]{1,0:T(8,128)(2,1)S(1)}, bf16[144,512]{1,0:T(8,128)(2,1)S(1)}, u32[]{:S(2)}, u32[]{:S(2)}) %collective-permute-start.3) | collective-permute-done | bytes 147488 | tf_op jit(solution)/shard_map/ppermute | solution.py:37
  19.8 1.8 %collective-permute-start.7 = (bf16[144,512]{1,0:T(8,128)(2,1)S(1)}, bf16[144,512]{1,0:T(8,128)(2,1)S(1)}, u32[]{:S(2)}, u32[]{:S(2)}) collective-permute-start(bf16[144,512]{1,0:T(8,128)(2,1)S(1)} %collective-permute-done.3.refs_3_), channel_id=1, source_target_pairs={{0,112},{8,120},{16,0},{24,8},{32,16},{40,24},{48,32},{56,40},{64,... | collective-permute-start | bytes 442376 | tf_op jit(solution)/shard_map/ppermute | solution.py:37
  21.8 4.0 %collective-permute-start.9 = (bf16[144,512]{1,0:T(8,128)(2,1)S(1)}, bf16[144,512]{1,0:T(8,128)(2,1)S(1)}, u32[]{:S(2)}, u32[]{:S(2)}) collective-permute-start(bf16[144,512]{1,0:T(8,128)(2,1)S(1)} %broadcast_select_fusion), channel_id=1, source_target_pairs={{0,32},{8,40},{16,112},{24,120},{32,64},{40,72},{48,16},{56,24},{6... | collective-permute-start | bytes 442376 | tf_op jit(solution)/shard_map/ppermute | solution.py:55
  25.8 2.3 %first_part.1 = (f32[6,1,512]{2,1,0:T(1,128)S(1)}, f32[6,1,512]{2,1,0:T(1,128)S(1)}, f32[6,128,512]{2,1,0:T(8,128)S(1)}) custom-call(bf16[144,512]{1,0:T(8,128)(2,1)S(1)} %concatenate.7.own.refs_0_, bf16[144,512]{1,0:T(8,128)(2,1)S(1)} %collective-permute-done.1.refs_1_, bf16[144,512]{1,0:T(8,128)(2,1)S(1)} %collective-permute-done.2.refs_2_, ...), custom_call_target="tpu_custom_call" | custom-call | flops 2000000000 | bytes 4194304 | tf_op jit(solution)/shard_map/first_part/pallas_call | solution.py:360
  28.2 2.1 %collective-permute-done.9.refs_2_ = bf16[144,512]{1,0:T(8,128)(2,1)S(1)} collective-permute-done((bf16[144,512]{1,0:T(8,128)(2,1)S(1)}, bf16[144,512]{1,0:T(8,128)(2,1)S(1)}, u32[]{:S(2)}, u32[]{:S(2)}) %collective-permute-start.9) | collective-permute-done | bytes 147488 | tf_op jit(solution)/shard_map/ppermute | solution.py:55
  30.3 2.8 %far_part.1 = (f32[4,1,512]{2,1,0:T(1,128)S(1)}, f32[4,1,512]{2,1,0:T(1,128)S(1)}, f32[4,128,512]{2,1,0:T(8,128)S(1)}) custom-call(bf16[144,512]{1,0:T(8,128)(2,1)S(1)} %collective-permute-done.7.refs_0_, bf16[144,512]{1,0:T(8,128)(2,1)S(1)} %collective-permute-done.8.refs_1_, bf16[144,512]{1,0:T(8,128)(2,1)S(1)} %collective-permute-done.9.refs_2_, ...), custom_call_target="tpu_custom_call" | custom-call | flops 20000000000 | bytes 4194304 | tf_op jit(solution)/shard_map/far_part/pallas_call | solution.py:379
  33.1 2.3 %last_part.1 = (bf16[144,512]{1,0:T(8,128)(2,1)S(1)}, bf16[144,512]{1,0:T(8,128)(2,1)S(1)}, bf16[144,512]{1,0:T(8,128)(2,1)S(1)}) custom-call(bf16[144,512]{1,0:T(8,128)(2,1)S(1)} %collective-permute-done.7.refs_0_, bf16[144,512]{1,0:T(8,128)(2,1)S(1)} %collective-permute-done.8.refs_1_, bf16[144,512]{1,0:T(8,128)(2,1)S(1)} %collective-permute-done.9.refs_2_, ...), custom_call_target="tpu_custom_call" | custom-call | flops 1500000000 | bytes 4194304 | tf_op jit(solution)/shard_map/last_part/pallas_call | solution.py:379
  35.3 1.2 %collective-permute-start.14 = (bf16[144,512]{1,0:T(8,128)(2,1)S(1)}, bf16[144,512]{1,0:T(8,128)(2,1)S(1)}, u32[]{:S(2)}, u32[]{:S(2)}) collective-permute-start(bf16[144,512]{1,0:T(8,128)(2,1)S(1)} %get-tuple-element.71), channel_id=1, source_target_pairs={{0,32},{8,40},{16,112},{24,120},{32,64},{40,72},{48,16},{56,24},{6... | collective-permute-start | bytes 442376 | tf_op jit(solution)/shard_map/ppermute | solution.py:55
  36.6 2.3 %collective-permute-start.12 = (bf16[144,512]{1,0:T(8,128)(2,1)S(1)}, bf16[144,512]{1,0:T(8,128)(2,1)S(1)}, u32[]{:S(2)}, u32[]{:S(2)}) collective-permute-start(bf16[144,512]{1,0:T(8,128)(2,1)S(1)} %get-tuple-element.85), channel_id=1, source_target_pairs={{0,112},{8,120},{16,0},{24,8},{32,16},{40,24},{48,32},{56,40},{64,... | collective-permute-start | bytes 442376 | tf_op jit(solution)/shard_map/ppermute | solution.py:37
  38.9 3.3 %near_part.1 = (f32[128,512]{1,0:T(8,128)S(1)}, f32[8,512]{1,0:T(8,128)S(1)}, bf16[144,512]{1,0:T(8,128)(2,1)S(1)}, bf16[144,512]{1,0:T(8,128)(2,1)S(1)}, bf16[1...) custom-call(bf16[144,512]{1,0:T(8,128)(2,1)S(1)} %concatenate.7.own.refs_0_, ...), custom_call_target="tpu_custom_call" | custom-call | flops 2500000000 | bytes 4194304 | tf_op jit(solution)/shard_map/near_part/pallas_call | solution.py:379
  42.1 3.3 %collective-permute-start.10 = (bf16[144,512]{1,0:T(8,128)(2,1)S(1)}, bf16[144,512]{1,0:T(8,128)(2,1)S(1)}, u32[]{:S(2)}, u32[]{:S(2)}) collective-permute-start(bf16[144,512]{1,0:T(8,128)(2,1)S(1)} %get-tuple-element.81), channel_id=1, source_target_pairs={{0,16},{8,24},{16,32},{24,40},{32,48},{40,56},{48,64},{56,72},{64,... | collective-permute-start | bytes 442376 | tf_op jit(solution)/shard_map/ppermute | solution.py:37
  46.1 1.2 %late_own.1.own_weight = bf16[1,512,1024]{2,1,0:T(8,128)(2,1)S(1)} custom-call(bf16[512,8192]{1,0:T(8,128)(2,1)} %weight.2), custom_call_target="tpu_custom_call" | custom-call | bytes 8388608 | tf_op jit(solution)/shard_map/late_own/pallas_call | solution.py:230
  47.6 3.5 %collective-permute-start.15 = (bf16[144,512]{1,0:T(8,128)(2,1)S(1)}, bf16[144,512]{1,0:T(8,128)(2,1)S(1)}, u32[]{:S(2)}, u32[]{:S(2)}) collective-permute-start(bf16[144,512]{1,0:T(8,128)(2,1)S(1)} %get-tuple-element.89), channel_id=1, source_target_pairs={{0,32},{8,40},{16,48},{24,56},{32,64},{40,72},{48,80},{56,88},{64,... | collective-permute-start | bytes 442376 | tf_op jit(solution)/shard_map/ppermute | solution.py:37
  52.1 5.2 %collective-permute-done.15.p2 = bf16[144,512]{1,0:T(8,128)(2,1)S(1)} collective-permute-done((bf16[144,512]{1,0:T(8,128)(2,1)S(1)}, bf16[144,512]{1,0:T(8,128)(2,1)S(1)}, u32[]{:S(2)}, u32[]{:S(2)}) %collective-permute-start.15) | collective-permute-done | bytes 147488 | tf_op jit(solution)/shard_map/ppermute | solution.py:37
  57.3 3.0 %collective-permute-done.16.m2 = bf16[144,512]{1,0:T(8,128)(2,1)S(1)} collective-permute-done((bf16[144,512]{1,0:T(8,128)(2,1)S(1)}, bf16[144,512]{1,0:T(8,128)(2,1)S(1)}, u32[]{:S(2)}, u32[]{:S(2)}) %collective-permute-start.16) | collective-permute-done | bytes 147488 | tf_op jit(solution)/shard_map/ppermute | solution.py:37
  61.2 1.5 %collective-permute-start.20 = (bf16[128,1024]{1,0:T(8,128)(2,1)S(1)}, bf16[128,1024]{1,0:T(8,128)(2,1)S(1)}, u32[]{:S(2)}, u32[]{:S(2)}) collective-permute-start(bf16[128,1024]{1,0:T(8,128)(2,1)S(1)} %get-tuple-element.100), channel_id=1, source_target_pairs={{0,4},{1,5},{2,6},{3,7},{4,0},{5,1},{6,2},{7,3},{8,12},{9,13},{10,... | collective-permute-start | bytes 786440 | tf_op jit(solution)/shard_map/ppermute | solution.py:45
  62.7 2.1 %collective-permute-start.21 = (bf16[128,1024]{1,0:T(8,128)(2,1)S(1)}, bf16[128,1024]{1,0:T(8,128)(2,1)S(1)}, u32[]{:S(2)}, u32[]{:S(2)}) collective-permute-start(bf16[128,1024]{1,0:T(8,128)(2,1)S(1)} %get-tuple-element.101), channel_id=1, source_target_pairs={{0,2},{1,3},{2,4},{3,5},{4,6},{5,7},{6,0},{7,1},{8,10},{9,11},{10,... | collective-permute-start | bytes 786440 | tf_op jit(solution)/shard_map/ppermute | solution.py:45
  65.5 2.1 %collective-permute-start.17 = (bf16[128,1024]{1,0:T(8,128)(2,1)S(1)}, bf16[128,1024]{1,0:T(8,128)(2,1)S(1)}, u32[]{:S(2)}, u32[]{:S(2)}) collective-permute-start(bf16[128,1024]{1,0:T(8,128)(2,1)S(1)} %get-tuple-element.96), channel_id=1, source_target_pairs={{0,4},{1,5},{2,6},{3,7},{4,0},{5,1},{6,2},{7,3},{8,12},{9,13},{10,... | collective-permute-start | bytes 786440 | tf_op jit(solution)/shard_map/ppermute | solution.py:45
  67.6 1.3 %collective-permute-start.18 = (bf16[128,1024]{1,0:T(8,128)(2,1)S(1)}, bf16[128,1024]{1,0:T(8,128)(2,1)S(1)}, u32[]{:S(2)}, u32[]{:S(2)}) collective-permute-start(bf16[128,1024]{1,0:T(8,128)(2,1)S(1)} %get-tuple-element.97), channel_id=1, source_target_pairs={{0,2},{1,3},{2,4},{3,5},{4,6},{5,7},{6,0},{7,1},{8,10},{9,11},{10,... | collective-permute-start | bytes 786440 | tf_op jit(solution)/shard_map/ppermute | solution.py:45
  68.9 3.2 %collective-permute-done.20.refs_0_ = bf16[128,1024]{1,0:T(8,128)(2,1)S(1)} collective-permute-done((bf16[128,1024]{1,0:T(8,128)(2,1)S(1)}, bf16[128,1024]{1,0:T(8,128)(2,1)S(1)}, u32[]{:S(2)}, u32[]{:S(2)}) %collective-permute-start.20) | collective-permute-done | bytes 262176 | tf_op jit(solution)/shard_map/ppermute | solution.py:45
  72.9 2.4 %collective-permute-done.21.refs_1_ = bf16[128,1024]{1,0:T(8,128)(2,1)S(1)} collective-permute-done((bf16[128,1024]{1,0:T(8,128)(2,1)S(1)}, bf16[128,1024]{1,0:T(8,128)(2,1)S(1)}, u32[]{:S(2)}, u32[]{:S(2)}) %collective-permute-start.21) | collective-permute-done | bytes 262176 | tf_op jit(solution)/shard_map/ppermute | solution.py:45
  75.3 1.8 %collective-permute-done.22.refs_2_ = bf16[128,1024]{1,0:T(8,128)(2,1)S(1)} collective-permute-done((bf16[128,1024]{1,0:T(8,128)(2,1)S(1)}, bf16[128,1024]{1,0:T(8,128)(2,1)S(1)}, u32[]{:S(2)}, u32[]{:S(2)}) %collective-permute-start.22) | collective-permute-done | bytes 262176 | tf_op jit(solution)/shard_map/ppermute | solution.py:45
  77.2 3.0 %collective-permute-start.23 = (bf16[128,1024]{1,0:T(8,128)(2,1)S(1)}, bf16[128,1024]{1,0:T(8,128)(2,1)S(1)}, u32[]{:S(2)}, u32[]{:S(2)}) collective-permute-start(bf16[128,1024]{1,0:T(8,128)(2,1)S(1)} %pass_on.1), channel_id=1, source_target_pairs={{0,1},{1,0},{2,3},{3,2},{4,5},{5,4},{6,7},{7,6},{8,9},{9,8},{10,11... | collective-permute-start | bytes 786440 | tf_op jit(solution)/shard_map/ppermute | solution.py:45
  81.1 1.6 %collective-permute-done.19.refs_2_ = bf16[128,1024]{1,0:T(8,128)(2,1)S(1)} collective-permute-done((bf16[128,1024]{1,0:T(8,128)(2,1)S(1)}, bf16[128,1024]{1,0:T(8,128)(2,1)S(1)}, u32[]{:S(2)}, u32[]{:S(2)}) %collective-permute-start.19) | collective-permute-done | bytes 262176 | tf_op jit(solution)/shard_map/ppermute | solution.py:45
  82.7 2.5 %collective-permute-done.23.refs_3_ = bf16[128,1024]{1,0:T(8,128)(2,1)S(1)} collective-permute-done((bf16[128,1024]{1,0:T(8,128)(2,1)S(1)}, bf16[128,1024]{1,0:T(8,128)(2,1)S(1)}, u32[]{:S(2)}, u32[]{:S(2)}) %collective-permute-start.23) | collective-permute-done | bytes 262176 | tf_op jit(solution)/shard_map/ppermute | solution.py:45
  (37 shorter events, 7.4 us)
Async XLA Ops:
  0.0 4.3 %copy-start.2 = (bf16[128,512]{1,0:T(8,128)(2,1)S(1)}, bf16[128,512]{1,0:T(8,128)(2,1)}, u32[]{:S(2)}) copy-start(bf16[128,512]{1,0:T(8,128)(2,1)} %param.9) | copy-start | bytes 393220
  0.0 14.8 %copy-start.1 = (bf16[128,128]{1,0:T(8,128)(2,1)S(1)}, bf16[128,128]{1,0:T(8,128)(2,1)}, u32[]{:S(2)}) copy-start(bf16[128,128]{1,0:T(8,128)(2,1)} %suffix_v.1) | copy-start | bytes 98308
  0.0 14.8 %copy-start = (bf16[128,128]{1,0:T(8,128)(2,1)S(1)}, bf16[128,128]{1,0:T(8,128)(2,1)}, u32[]{:S(2)}) copy-start(bf16[128,128]{1,0:T(8,128)(2,1)} %suffix_k.1) | copy-start | bytes 98308
  1.9 9.6 %collective-permute-start = (bf16[3088,128]{1,0:T(8,128)(2,1)S(1)}, bf16[3088,128]{1,0:T(8,128)(2,1)S(1)}, u32[]{:S(2)}, u32[]{:S(2)}) collective-permute-start(bf16[3088,128]{1,0:T(8,128)(2,1)S(1)} %fusion.1.refs_5_.refs_3_), channel_id=1, source_target_pairs={{0,8},{8,0},{16,24},{24,16},{32,40},{40,32},{48,56},{56,48},{64,72... | collective-permute-start | bytes 2371592 | tf_op jit(solution)/shard_map/ppermute | solution.py:37
  2.0 26.0 %collective-permute-start.5 = (bf16[3088,128]{1,0:T(8,128)(2,1)S(1)}, bf16[3088,128]{1,0:T(8,128)(2,1)S(1)}, u32[]{:S(2)}, u32[]{:S(2)}) collective-permute-start(bf16[3088,128]{1,0:T(8,128)(2,1)S(1)} %fusion.1.refs_5_.refs_3_), channel_id=1, source_target_pairs={{0,128},{8,136},{16,144},{24,152},{32,160},{40,168},{48,176},{56,1... | collective-permute-start | bytes 2371592 | tf_op jit(solution)/shard_map/ppermute | solution.py:37
  4.4 13.9 %collective-permute-start.4 = (bf16[144,512]{1,0:T(8,128)(2,1)S(1)}, bf16[144,512]{1,0:T(8,128)(2,1)S(1)}, u32[]{:S(2)}, u32[]{:S(2)}) collective-permute-start(bf16[144,512]{1,0:T(8,128)(2,1)S(1)} %concatenate.7.own.refs_0_), channel_id=1, source_target_pairs={{0,32},{8,40},{16,48},{24,56},{32,64},{40,72},{48,80},{56,88},{64,... | collective-permute-start | bytes 442376 | tf_op jit(solution)/shard_map/ppermute | solution.py:37
  7.7 12.0 %collective-permute-start.3 = (bf16[144,512]{1,0:T(8,128)(2,1)S(1)}, bf16[144,512]{1,0:T(8,128)(2,1)S(1)}, u32[]{:S(2)}, u32[]{:S(2)}) collective-permute-start(bf16[144,512]{1,0:T(8,128)(2,1)S(1)} %concatenate.7.own.refs_0_), channel_id=1, source_target_pairs={{0,96},{8,104},{16,112},{24,120},{32,0},{40,8},{48,16},{56,24},{64... | collective-permute-start | bytes 442376 | tf_op jit(solution)/shard_map/ppermute | solution.py:37
  11.5 10.3 %collective-permute-start.2 = (bf16[144,512]{1,0:T(8,128)(2,1)S(1)}, bf16[144,512]{1,0:T(8,128)(2,1)S(1)}, u32[]{:S(2)}, u32[]{:S(2)}) collective-permute-start(bf16[144,512]{1,0:T(8,128)(2,1)S(1)} %concatenate.7.own.refs_0_), channel_id=1, source_target_pairs={{0,16},{8,24},{16,32},{24,40},{32,48},{40,56},{48,64},{56,72},{64,... | collective-permute-start | bytes 442376 | tf_op jit(solution)/shard_map/ppermute | solution.py:37
  12.6 13.2 %collective-permute-start.1 = (bf16[144,512]{1,0:T(8,128)(2,1)S(1)}, bf16[144,512]{1,0:T(8,128)(2,1)S(1)}, u32[]{:S(2)}, u32[]{:S(2)}) collective-permute-start(bf16[144,512]{1,0:T(8,128)(2,1)S(1)} %concatenate.7.own.refs_0_), channel_id=1, source_target_pairs={{0,112},{8,120},{16,0},{24,8},{32,16},{40,24},{48,32},{56,40},{64,... | collective-permute-start | bytes 442376 | tf_op jit(solution)/shard_map/ppermute | solution.py:37
  19.8 10.5 %collective-permute-start.7 = (bf16[144,512]{1,0:T(8,128)(2,1)S(1)}, bf16[144,512]{1,0:T(8,128)(2,1)S(1)}, u32[]{:S(2)}, u32[]{:S(2)}) collective-permute-start(bf16[144,512]{1,0:T(8,128)(2,1)S(1)} %collective-permute-done.3.refs_3_), channel_id=1, source_target_pairs={{0,112},{8,120},{16,0},{24,8},{32,16},{40,24},{48,32},{56,40},{64,... | collective-permute-start | bytes 442376 | tf_op jit(solution)/shard_map/ppermute | solution.py:37
  21.5 8.7 %collective-permute-start.8 = (bf16[144,512]{1,0:T(8,128)(2,1)S(1)}, bf16[144,512]{1,0:T(8,128)(2,1)S(1)}, u32[]{:S(2)}, u32[]{:S(2)}) collective-permute-start(bf16[144,512]{1,0:T(8,128)(2,1)S(1)} %collective-permute-done.4.refs_4_), channel_id=1, source_target_pairs={{0,16},{8,24},{16,32},{24,40},{32,48},{40,56},{48,64},{56,72},{64,... | collective-permute-start | bytes 442376 | tf_op jit(solution)/shard_map/ppermute | solution.py:37
  21.8 8.4 %collective-permute-start.9 = (bf16[144,512]{1,0:T(8,128)(2,1)S(1)}, bf16[144,512]{1,0:T(8,128)(2,1)S(1)}, u32[]{:S(2)}, u32[]{:S(2)}) collective-permute-start(bf16[144,512]{1,0:T(8,128)(2,1)S(1)} %broadcast_select_fusion), channel_id=1, source_target_pairs={{0,32},{8,40},{16,112},{24,120},{32,64},{40,72},{48,16},{56,24},{6... | collective-permute-start | bytes 442376 | tf_op jit(solution)/shard_map/ppermute | solution.py:55
  28.1 5.0 %collective-permute-start.6 = (bf16[3088,128]{1,0:T(8,128)(2,1)S(1)}, bf16[3088,128]{1,0:T(8,128)(2,1)S(1)}, u32[]{:S(2)}, u32[]{:S(2)}) collective-permute-start(bf16[3088,128]{1,0:T(8,128)(2,1)S(1)} %collective-permute-done.5.refs_5_), channel_id=1, source_target_pairs={{0,8},{8,0},{16,24},{24,16},{32,40},{40,32},{48,56},{56,48},{64,72... | collective-permute-start | bytes 2371592 | tf_op jit(solution)/shard_map/ppermute | solution.py:37
  35.3 12.0 %collective-permute-start.14 = (bf16[144,512]{1,0:T(8,128)(2,1)S(1)}, bf16[144,512]{1,0:T(8,128)(2,1)S(1)}, u32[]{:S(2)}, u32[]{:S(2)}) collective-permute-start(bf16[144,512]{1,0:T(8,128)(2,1)S(1)} %get-tuple-element.71), channel_id=1, source_target_pairs={{0,32},{8,40},{16,112},{24,120},{32,64},{40,72},{48,16},{56,24},{6... | collective-permute-start | bytes 442376 | tf_op jit(solution)/shard_map/ppermute | solution.py:55
  36.6 10.8 %collective-permute-start.12 = (bf16[144,512]{1,0:T(8,128)(2,1)S(1)}, bf16[144,512]{1,0:T(8,128)(2,1)S(1)}, u32[]{:S(2)}, u32[]{:S(2)}) collective-permute-start(bf16[144,512]{1,0:T(8,128)(2,1)S(1)} %get-tuple-element.85), channel_id=1, source_target_pairs={{0,112},{8,120},{16,0},{24,8},{32,16},{40,24},{48,32},{56,40},{64,... | collective-permute-start | bytes 442376 | tf_op jit(solution)/shard_map/ppermute | solution.py:37
  38.9 8.5 %collective-permute-start.13 = (bf16[144,512]{1,0:T(8,128)(2,1)S(1)}, bf16[144,512]{1,0:T(8,128)(2,1)S(1)}, u32[]{:S(2)}, u32[]{:S(2)}) collective-permute-start(bf16[144,512]{1,0:T(8,128)(2,1)S(1)} %get-tuple-element.86), channel_id=1, source_target_pairs={{0,16},{8,24},{16,32},{24,40},{32,48},{40,56},{48,64},{56,72},{64,... | collective-permute-start | bytes 442376 | tf_op jit(solution)/shard_map/ppermute | solution.py:37
  42.1 10.0 %collective-permute-start.10 = (bf16[144,512]{1,0:T(8,128)(2,1)S(1)}, bf16[144,512]{1,0:T(8,128)(2,1)S(1)}, u32[]{:S(2)}, u32[]{:S(2)}) collective-permute-start(bf16[144,512]{1,0:T(8,128)(2,1)S(1)} %get-tuple-element.81), channel_id=1, source_target_pairs={{0,16},{8,24},{16,32},{24,40},{32,48},{40,56},{48,64},{56,72},{64,... | collective-permute-start | bytes 442376 | tf_op jit(solution)/shard_map/ppermute | solution.py:37
  45.5 6.7 %collective-permute-start.11 = (bf16[144,512]{1,0:T(8,128)(2,1)S(1)}, bf16[144,512]{1,0:T(8,128)(2,1)S(1)}, u32[]{:S(2)}, u32[]{:S(2)}) collective-permute-start(bf16[144,512]{1,0:T(8,128)(2,1)S(1)} %get-tuple-element.82), channel_id=1, source_target_pairs={{0,112},{8,120},{16,0},{24,8},{32,16},{40,24},{48,32},{56,40},{64,... | collective-permute-start | bytes 442376 | tf_op jit(solution)/shard_map/ppermute | solution.py:37
  47.6 9.7 %collective-permute-start.15 = (bf16[144,512]{1,0:T(8,128)(2,1)S(1)}, bf16[144,512]{1,0:T(8,128)(2,1)S(1)}, u32[]{:S(2)}, u32[]{:S(2)}) collective-permute-start(bf16[144,512]{1,0:T(8,128)(2,1)S(1)} %get-tuple-element.89), channel_id=1, source_target_pairs={{0,32},{8,40},{16,48},{24,56},{32,64},{40,72},{48,80},{56,88},{64,... | collective-permute-start | bytes 442376 | tf_op jit(solution)/shard_map/ppermute | solution.py:37
  51.2 9.1 %collective-permute-start.16 = (bf16[144,512]{1,0:T(8,128)(2,1)S(1)}, bf16[144,512]{1,0:T(8,128)(2,1)S(1)}, u32[]{:S(2)}, u32[]{:S(2)}) collective-permute-start(bf16[144,512]{1,0:T(8,128)(2,1)S(1)} %get-tuple-element.90), channel_id=1, source_target_pairs={{0,96},{8,104},{16,112},{24,120},{32,0},{40,8},{48,16},{56,24},{64... | collective-permute-start | bytes 442376 | tf_op jit(solution)/shard_map/ppermute | solution.py:37
  61.2 10.9 %collective-permute-start.20 = (bf16[128,1024]{1,0:T(8,128)(2,1)S(1)}, bf16[128,1024]{1,0:T(8,128)(2,1)S(1)}, u32[]{:S(2)}, u32[]{:S(2)}) collective-permute-start(bf16[128,1024]{1,0:T(8,128)(2,1)S(1)} %get-tuple-element.100), channel_id=1, source_target_pairs={{0,4},{1,5},{2,6},{3,7},{4,0},{5,1},{6,2},{7,3},{8,12},{9,13},{10,... | collective-permute-start | bytes 786440 | tf_op jit(solution)/shard_map/ppermute | solution.py:45
  62.7 12.6 %collective-permute-start.21 = (bf16[128,1024]{1,0:T(8,128)(2,1)S(1)}, bf16[128,1024]{1,0:T(8,128)(2,1)S(1)}, u32[]{:S(2)}, u32[]{:S(2)}) collective-permute-start(bf16[128,1024]{1,0:T(8,128)(2,1)S(1)} %get-tuple-element.101), channel_id=1, source_target_pairs={{0,2},{1,3},{2,4},{3,5},{4,6},{5,7},{6,0},{7,1},{8,10},{9,11},{10,... | collective-permute-start | bytes 786440 | tf_op jit(solution)/shard_map/ppermute | solution.py:45
  64.8 12.3 %collective-permute-start.22 = (bf16[128,1024]{1,0:T(8,128)(2,1)S(1)}, bf16[128,1024]{1,0:T(8,128)(2,1)S(1)}, u32[]{:S(2)}, u32[]{:S(2)}) collective-permute-start(bf16[128,1024]{1,0:T(8,128)(2,1)S(1)} %get-tuple-element.102), channel_id=1, source_target_pairs={{0,6},{1,7},{2,0},{3,1},{4,2},{5,3},{6,4},{7,5},{8,14},{9,15},{10,... | collective-permute-start | bytes 786440 | tf_op jit(solution)/shard_map/ppermute | solution.py:45
  65.5 14.7 %collective-permute-start.17 = (bf16[128,1024]{1,0:T(8,128)(2,1)S(1)}, bf16[128,1024]{1,0:T(8,128)(2,1)S(1)}, u32[]{:S(2)}, u32[]{:S(2)}) collective-permute-start(bf16[128,1024]{1,0:T(8,128)(2,1)S(1)} %get-tuple-element.96), channel_id=1, source_target_pairs={{0,4},{1,5},{2,6},{3,7},{4,0},{5,1},{6,2},{7,3},{8,12},{9,13},{10,... | collective-permute-start | bytes 786440 | tf_op jit(solution)/shard_map/ppermute | solution.py:45
  67.6 13.4 %collective-permute-start.18 = (bf16[128,1024]{1,0:T(8,128)(2,1)S(1)}, bf16[128,1024]{1,0:T(8,128)(2,1)S(1)}, u32[]{:S(2)}, u32[]{:S(2)}) collective-permute-start(bf16[128,1024]{1,0:T(8,128)(2,1)S(1)} %get-tuple-element.97), channel_id=1, source_target_pairs={{0,2},{1,3},{2,4},{3,5},{4,6},{5,7},{6,0},{7,1},{8,10},{9,11},{10,... | collective-permute-start | bytes 786440 | tf_op jit(solution)/shard_map/ppermute | solution.py:45
  72.1 10.6 %collective-permute-start.19 = (bf16[128,1024]{1,0:T(8,128)(2,1)S(1)}, bf16[128,1024]{1,0:T(8,128)(2,1)S(1)}, u32[]{:S(2)}, u32[]{:S(2)}) collective-permute-start(bf16[128,1024]{1,0:T(8,128)(2,1)S(1)} %get-tuple-element.98), channel_id=1, source_target_pairs={{0,6},{1,7},{2,0},{3,1},{4,2},{5,3},{6,4},{7,5},{8,14},{9,15},{10,... | collective-permute-start | bytes 786440 | tf_op jit(solution)/shard_map/ppermute | solution.py:45
  77.2 8.0 %collective-permute-start.23 = (bf16[128,1024]{1,0:T(8,128)(2,1)S(1)}, bf16[128,1024]{1,0:T(8,128)(2,1)S(1)}, u32[]{:S(2)}, u32[]{:S(2)}) collective-permute-start(bf16[128,1024]{1,0:T(8,128)(2,1)S(1)} %pass_on.1), channel_id=1, source_target_pairs={{0,1},{1,0},{2,3},{3,2},{4,5},{5,4},{6,7},{7,6},{8,9},{9,8},{10,11... | collective-permute-start | bytes 786440 | tf_op jit(solution)/shard_map/ppermute | solution.py:45
